TPU v7x, 32 devices: a whole 2x2x4 slice. The times are simulated.
32 devices in a mesh: seq: 4 (over y, x), head: 8 (over z, core).
Axes of the slice: x: 2, y: 2, z: 4, core: 2. Of those that a mesh axis runs over, the one named last changes fastest.
Arguments:
- queries: bfloat16 [2048, 1024], P('seq', 'head'), may hold values from -5 to 5
- keys: bfloat16 [2048, 1024], P('seq', 'head'), may hold values from -5 to 5
- values: bfloat16 [2048, 1024], P('seq', 'head'), may hold values from -5 to 5
- grad_out: bfloat16 [2048, 1024], P('seq', 'head'), may hold values from -6 to 6
Outputs:
- attended: bfloat16 [2048, 1024], P('seq', 'head')
- grad_query: bfloat16 [2048, 1024], P(('seq', 'head'))
- grad_key: bfloat16 [2048, 1024], P(('seq', 'head'))
- grad_value: bfloat16 [2048, 1024], P(('seq', 'head'))
All inputs are finite; a program needn't handle non-finite values.
Results may differ from a plain program's by a relative error of at most 0.024.
Values may be sent and summed in bfloat16 or wider, within the bound.
No kernel may reach another device: no remote copies, remote signals or barrier semaphores. Data moves between devices by JAX's collectives and lax.ppermute only.
A program may use at most 64 MiB of HBM per device.

v0:
```python
from functools import reduce

import jax
import jax.numpy as jnp
from jax import lax
from jax.sharding import PartitionSpec as P

BLOCK = 128


MASKED = -1e30


def padded_2(shard, sides, width):
    for axis, dim in sides:
        size, length = (lax.axis_size(axis), shard.shape[dim])
        up = [(i, (i + 1) % size) for i in range(size - 1)]
        down = [(j, i) for i, j in up]
        last = lax.slice_in_dim(shard, length - width, length, axis=dim)
        first = lax.slice_in_dim(shard, 0, width, axis=dim)
        before = lax.ppermute(last, axis, up)
        after = lax.ppermute(first, axis, down)
        shard = jnp.concatenate([before, shard, after], axis=dim)
    return shard


def from_behind(block, axis, distance):
    devices = range(lax.axis_size(axis))
    route = [(i - distance, i) for i in devices if i - distance in devices]
    return lax.ppermute(block, axis, route)


def coarsen(stacked):
    in_shape = stacked.shape
    paired = stacked.astype(jnp.float32).reshape(
        in_shape[:-2] + (in_shape[-2] // 2, 2, in_shape[-1])
    )
    halved = ((paired[..., 0, :] + paired[..., 1, :]) * 0.5).astype(jnp.bfloat16)
    return lax.optimization_barrier(halved)


def unit_stats(
    query_rows, query_index, key_rows, value_rows, key_index, block_count, coarse_level, block_rows
):
    scale = query_rows.shape[-1] ** (-0.5)
    scores = (
        jnp.einsum("urd,ukd->urk", query_rows, key_rows, preferred_element_type=jnp.float32) * scale
    )
    row_block = query_index // block_rows
    key_block = key_index // block_rows
    block_gap = jnp.abs(row_block[:, :, None] - key_block[:, None, :])
    if coarse_level == 0:
        allowed = block_gap <= 1
    else:
        parent_gap = jnp.abs(row_block[:, :, None] // 2 - key_block[:, None, :] // 2)
        allowed = (block_gap >= 2) & (parent_gap <= 1)
    allowed = allowed & (key_block[:, None, :] >= 0) & (key_block[:, None, :] < block_count)
    scores = jnp.where(allowed, scores, MASKED)
    row_peak = jnp.max(scores, axis=-1)
    exp_scores = jnp.exp(scores - row_peak[..., None])
    multiple = float(2**coarse_level)
    row_total = jnp.sum(exp_scores, axis=-1) * multiple
    rounded = exp_scores.astype(jnp.bfloat16)
    mixed_rows = (
        jnp.einsum("urk,ukd->urd", rounded, value_rows, preferred_element_type=jnp.float32)
        * multiple
    )
    return (row_peak, row_total, mixed_rows)


def windowed(coarse_query, padded, first_row, span_rows, block_count, coarse_level, block_rows):
    row_count, head_width = coarse_query.shape
    unit_count = row_count // span_rows
    unit_rows = padded.reshape(2, unit_count + 2, span_rows, head_width)
    window = jnp.concatenate([unit_rows[:, :-2], unit_rows[:, 1:-1], unit_rows[:, 2:]], axis=2)
    query_index = (first_row + jnp.arange(row_count, dtype=jnp.int32)).reshape(
        unit_count, span_rows
    )
    key_index = (
        first_row
        - span_rows
        + jnp.arange(unit_count, dtype=jnp.int32)[:, None] * span_rows
        + jnp.arange(3 * span_rows, dtype=jnp.int32)[None, :]
    )
    return unit_stats(
        coarse_query.reshape(unit_count, span_rows, head_width),
        query_index,
        window[0],
        window[1],
        key_index,
        block_count,
        coarse_level,
        block_rows,
    )


def expand(stats, coarse_level, head_width):
    repeats = 2**coarse_level
    return (
        jnp.repeat(stats[0].reshape(-1), repeats),
        jnp.repeat(stats[1].reshape(-1), repeats),
        jnp.repeat(stats[2].reshape(-1, head_width), repeats, axis=0),
    )


def combine(level_stats):
    overall_peak = reduce(jnp.maximum, [entry[0] for entry in level_stats])
    factors = [jnp.exp(entry[0] - overall_peak) for entry in level_stats]
    denominator = reduce(
        jnp.add, [factor * entry[1] for factor, entry in zip(factors, level_stats)]
    )
    numerator = reduce(
        jnp.add, [factor[:, None] * entry[2] for factor, entry in zip(factors, level_stats)]
    )
    return (numerator / denominator[:, None]).astype(jnp.bfloat16)


def level_counts(row_count, seq_count):
    fine_blocks = row_count * seq_count // BLOCK
    top_level = (fine_blocks // 4).bit_length() - 1
    gather_level = (row_count // BLOCK).bit_length() - 1
    return (fine_blocks, top_level, gather_level)


def local_pass(
    query_rows, key_rows, value_rows, fine_rims, coarse_rims, panels, seq_index, seq_count
):
    row_count, head_width = query_rows.shape
    fine_blocks, top_level, gather_level = level_counts(row_count, seq_count)
    key_value = jnp.stack([key_rows, value_rows])
    padded = jnp.concatenate([fine_rims[0], key_value, fine_rims[1]], axis=1)
    level_stats = [
        expand(
            windowed(query_rows, padded, seq_index * row_count, BLOCK, fine_blocks, 0, BLOCK),
            0,
            head_width,
        )
    ]
    coarse_query = query_rows
    coarse_level = 1
    coarse_query = coarsen(coarse_query)
    key_value = coarsen(key_value)
    rim_pair = coarse_rims[coarse_level - 1]
    padded = jnp.concatenate([rim_pair[0], key_value, rim_pair[1]], axis=1)
    stats = windowed(
        coarse_query,
        padded,
        seq_index * coarse_query.shape[0],
        2 * BLOCK,
        fine_blocks >> coarse_level,
        coarse_level,
        BLOCK,
    )
    level_stats.append(expand(stats, coarse_level, head_width))
    panel_keys = panels
    span_rows = 2 * BLOCK
    for coarse_level in range(gather_level, top_level + 1):
        coarse_query = coarsen(coarse_query)
        if coarse_level > gather_level:
            panel_keys = coarsen(panel_keys)
        query_count = coarse_query.shape[0]
        first_row = seq_index * query_count
        unit_index = first_row // span_rows
        padded = jnp.pad(panel_keys, ((0, 0), (span_rows, span_rows), (0, 0)))
        window = lax.dynamic_slice_in_dim(padded, unit_index * span_rows, 3 * span_rows, axis=1)
        query_index = (first_row + jnp.arange(query_count, dtype=jnp.int32)).reshape(1, query_count)
        key_index = (
            unit_index * span_rows - span_rows + jnp.arange(3 * span_rows, dtype=jnp.int32)
        ).reshape(1, 3 * span_rows)
        stats = unit_stats(
            coarse_query.reshape(1, query_count, head_width),
            query_index,
            window[0][None],
            window[1][None],
            key_index,
            fine_blocks >> coarse_level,
            coarse_level,
            BLOCK,
        )
        level_stats.append(expand(stats, coarse_level, head_width))
    return combine(level_stats)


def receive(key_rows, value_rows):
    key_value = jnp.stack([key_rows, value_rows])
    extended = padded_2(key_value, (("seq", 1),), BLOCK)
    fine_rims = (extended[:, :BLOCK], extended[:, -BLOCK:])
    key_value = coarsen(key_value)
    extended = padded_2(key_value, (("seq", 1),), 2 * BLOCK)
    coarse_rims = [(extended[:, : 2 * BLOCK], extended[:, -2 * BLOCK :])]
    key_value = coarsen(key_value)
    panels = lax.all_gather(key_value, "seq", axis=1, tiled=True)
    return (fine_rims, coarse_rims, panels)


def pyramid(key_value, gather_level):
    levels_out = []
    for coarse_level in range(1, gather_level + 1):
        key_value = coarsen(key_value)
        levels_out.append(key_value)
    return tuple(levels_out)


def place_rims(from_left, from_right, row_count):
    rim_width = from_left.shape[1]
    placed = jnp.zeros((2, row_count, from_left.shape[2]), jnp.float32)
    placed = placed.at[:, :rim_width].add(from_left.astype(jnp.float32))
    return placed.at[:, row_count - rim_width :].add(from_right.astype(jnp.float32))


def per_device(queries, keys, values, grad_out):
    seq_index = lax.axis_index("seq")
    seq_count = lax.axis_size("seq")
    row_count = queries.shape[0]
    fine_blocks, top_level, gather_level = level_counts(row_count, seq_count)

    def forward(query_rows, key_rows, value_rows, fine_rims, coarse_rims, panels):
        return local_pass(
            query_rows, key_rows, value_rows, fine_rims, coarse_rims, panels, seq_index, seq_count
        )

    fine_rims, coarse_rims, panels = receive(keys, values)
    attended = forward(queries, keys, values, fine_rims, coarse_rims, panels)
    attended, keys_again, values_again, queries_again = lax.optimization_barrier(
        (attended, keys, values, queries)
    )
    fine_rims, coarse_rims, panels = receive(keys_again, values_again)
    unused_output, pullback = jax.vjp(
        forward, queries_again, keys_again, values_again, fine_rims, coarse_rims, panels
    )
    query_grad, key_grad, value_grad, fine_back, coarse_back, panel_back = pullback(grad_out)
    panel_own = lax.psum_scatter(
        panel_back.astype(jnp.float32), "seq", scatter_dimension=1, tiled=True
    ).astype(jnp.bfloat16)
    rim_pairs = [fine_back] + list(coarse_back)
    arrivals = []
    for rim_pair in rim_pairs:
        from_right = from_behind(rim_pair[0], "seq", -1)
        from_left = from_behind(rim_pair[1], "seq", 1)
        arrivals.append((from_left, from_right))
    pyramid_grads = []
    level_rows = row_count >> 1
    pyramid_grads.append(
        place_rims(arrivals[1][0], arrivals[1][1], level_rows).astype(jnp.bfloat16)
    )
    pyramid_grads.append(panel_own)

    def build_pyramid(key_value):
        return pyramid(key_value, gather_level)

    unused_levels, pyramid_pull = jax.vjp(build_pyramid, jnp.stack([keys, values]))
    pyramid_back = pyramid_pull(tuple(pyramid_grads))[0]
    fine_terms = place_rims(arrivals[0][0], arrivals[0][1], row_count)
    local_terms = jnp.stack([key_grad, value_grad]).astype(jnp.float32)
    key_value_grad = (local_terms + fine_terms + pyramid_back.astype(jnp.float32)).astype(
        jnp.bfloat16
    )
    grad_query, grad_key, grad_value = (
        lax.all_to_all(query_grad, "head", split_axis=0, concat_axis=1, tiled=True),
        lax.all_to_all(key_value_grad[0], "head", split_axis=0, concat_axis=1, tiled=True),
        lax.all_to_all(key_value_grad[1], "head", split_axis=0, concat_axis=1, tiled=True),
    )
    return (attended, grad_query, grad_key, grad_value)


def solution(mesh):
    return jax.shard_map(
        per_device,
        mesh=mesh,
        in_specs=(P("seq", "head"), P("seq", "head"), P("seq", "head"), P("seq", "head")),
        out_specs=(
            P("seq", "head"),
            P(("seq", "head"), None),
            P(("seq", "head"), None),
            P(("seq", "head"), None),
        ),
        check_vma=False,
    )
```

profile of v0, /device:TPU:0, one launch (start us, length us, event | category | flops | bytes accessed | tf_op | source)
XLA Modules:
  0.0 204.1 jit_solution(6714716132882584944)
XLA Ops:
  10.2 5.5 %collective-permute-start.2 = (bf16[2,256,128]{2,1,0:T(8,128)(2,1)S(1)}, bf16[2,256,128]{2,1,0:T(8,128)(2,1)S(1)}, u32[]{:S(2)}, u32[]{:S(2)}) collective-permute-start(bf16[2,256,128]{2,1,0:T(8,128)(2,1)S(1)} %bitcast.326), channel_id=1, source_target_pairs={{0,8},{8,16},{16,24},{1,9},{9,17},{17,25},{2,10},{10,18},{18,26},{... | collective-permute-start | bytes 393224 | tf_op jit(solution)/shard_map/ppermute | solution.py:21
  17.0 5.4 %collective-permute-start = (bf16[2,128,128]{2,1,0:T(8,128)(2,1)S(1)}, bf16[2,128,128]{2,1,0:T(8,128)(2,1)S(1)}, u32[]{:S(2)}, u32[]{:S(2)}) collective-permute-start(bf16[2,128,128]{2,1,0:T(8,128)(2,1)S(1)} %get-tuple-element.129), channel_id=1, source_target_pairs={{0,8},{8,16},{16,24},{1,9},{9,17},{17,25},{2,10},{10,18},{18,26},{... | collective-permute-start | bytes 196616 | tf_op jit(solution)/shard_map/ppermute | solution.py:21
  23.7 10.4 %all_gather.6 = bf16[2,512,128]{2,1,0:T(8,128)(2,1)S(1)} all-gather(bf16[2,128,128]{2,1,0:T(8,128)(2,1)S(1)} %fusion.106), channel_id=1, replica_groups=mesh['seq'=4,'head'=8] {'seq'}, dimensions={1}, use_global_device_ids=true | all-gather | bytes 327680 | tf_op jit(solution)/shard_map/all_gather | solution.py:192
  42.8 5.2 %collective-permute-start.6 = (bf16[2,256,128]{2,1,0:T(8,128)(2,1)S(1)}, bf16[2,256,128]{2,1,0:T(8,128)(2,1)}, u32[]{:S(2)}, u32[]{:S(2)}) collective-permute-start(bf16[2,256,128]{2,1,0:T(8,128)(2,1)S(1)} %bitcast.330), channel_id=1, source_target_pairs={{0,8},{8,16},{16,24},{1,9},{9,17},{17,25},{2,10},{10,18},{18,26},{... | collective-permute-start | bytes 393224 | tf_op jit(solution)/shard_map/ppermute | solution.py:21
  48.6 7.7 %all_gather.7 = bf16[2,512,128]{2,1,0:T(8,128)(2,1)S(1)} all-gather(bf16[2,128,128]{2,1,0:T(8,128)(2,1)S(1)} %fusion.107), channel_id=1, replica_groups=mesh['seq'=4,'head'=8] {'seq'}, dimensions={1}, use_global_device_ids=true | all-gather | bytes 327680 | tf_op jit(solution)/shard_map/all_gather | solution.py:192
  60.8 4.5 %collective-permute-start.4 = (bf16[2,128,128]{2,1,0:T(8,128)(2,1)S(1)}, bf16[2,128,128]{2,1,0:T(8,128)(2,1)S(1)}, u32[]{:S(2)}, u32[]{:S(2)}) collective-permute-start(bf16[2,128,128]{2,1,0:T(8,128)(2,1)S(1)} %get-tuple-element.127), channel_id=1, source_target_pairs={{0,8},{8,16},{16,24},{1,9},{9,17},{17,25},{2,10},{10,18},{18,26},{... | collective-permute-start | bytes 196616 | tf_op jit(solution)/shard_map/ppermute | solution.py:21
  73.3 1.5 convert_reduce_fusion
  79.8 1.6 convert_reduce_fusion.1
  90.0 2.7 %fusion.70 = (f32[512]{0:T(512)S(1)}, f32[512]{0:T(512)}, f32[512]{0:T(512)}, f32[512]{0:T(512)}, f32[512,128]{1,0:T(8,128)}, /*index=5*/f32[512,128]{1,0:T(8,128)}) fusion(f32[4,128,128]{2,1,0:T(8,128)S(1)} %copy-done.3, f32[512]{0:T(512)S(1)} %get-tuple-element.91, bf16[512,128]{1,0:T(8,128)(2,1)} %param.19, f32[512,128]{1,0:T(8,128)S(1)} %bitcast.344, ...), kind=kLoop, calls=%fused_computation.150 | loop fusion | flops 1177600 | bytes 1460224 | tf_op jit(solution)/shard_map/transpose(jvp())/reduce_sum | solution.py:113
  104.0 1.5 copy.115
  112.3 1.9 add_reduce_fusion.1
  114.7 1.7 reduce_sum.224
  118.5 1.9 convolution_convert_fusion.11
  124.7 1.7 fusion.210
  127.5 2.5 %convolution_convert_fusion.9 = bf16[4,128,128]{2,1,0:T(8,128)(2,1)S(1)} fusion(f32[4,128,384]{1,2,0:T(8,128)} %get-tuple-element.156, pred[4,128,384]{1,2,0:T(32,128)(4,1)} %get-tuple-element.89, f32[4,128]{1,0:T(4,128)S(1)} %fusion.138, bf16[2,4,384,128]{3,2,1,0:T(8,128)(2,1)S(1)} %pad_maximum_fusion.1, s32[4,384]{1,0:T(4,128)} %copy-done.30, ...), kind=kOutput, calls=%fused_computation.37 | convolution fusion | flops 52166656 | bytes 1520640 | tf_op jit(solution)/shard_map/transpose(jvp(urd,ukd->urk))/dot_general | solution.py:47
  136.6 4.9 %all-to-all-start = ((bf16[8,64,128]{2,1,0:T(8,128)(2,1)}), bf16[8,64,128]{2,1,0:T(8,128)(2,1)S(1)}, u32[]{:S(2)}, u32[]{:S(2)}) async-start(bf16[8,64,128]{2,1,0:T(8,128)(2,1)} %bitcast_add_fusion), calls=%async_computation | async-start | bytes 262144 | tf_op jit(solution)/shard_map/all_to_all | solution.py:259
  144.7 5.2 %collective-permute-start.10 = (bf16[2,256,128]{2,1,0:T(8,128)(2,1)S(1)}, bf16[2,256,128]{2,1,0:T(8,128)(2,1)S(1)}, u32[]{:S(2)}, u32[]{:S(2)}) collective-permute-start(bf16[2,256,128]{2,1,0:T(8,128)(2,1)S(1)} %get-tuple-element.107), channel_id=1, source_target_pairs={{0,8},{8,16},{16,24},{1,9},{9,17},{17,25},{2,10},{10,18},{18,26},{... | collective-permute-start | bytes 393224 | tf_op jit(solution)/shard_map/ppermute | solution.py:30
  150.1 4.8 %collective-permute-start.8 = (bf16[2,128,128]{2,1,0:T(8,128)(2,1)S(1)}, bf16[2,128,128]{2,1,0:T(8,128)(2,1)S(1)}, u32[]{:S(2)}, u32[]{:S(2)}) collective-permute-start(bf16[2,128,128]{2,1,0:T(8,128)(2,1)S(1)} %get-tuple-element.109), channel_id=1, source_target_pairs={{0,8},{8,16},{16,24},{1,9},{9,17},{17,25},{2,10},{10,18},{18,26},{... | collective-permute-start | bytes 196616 | tf_op jit(solution)/shard_map/ppermute | solution.py:30
  156.8 5.0 %collective-permute-done.9 = bf16[2,128,128]{2,1,0:T(8,128)(2,1)S(1)} collective-permute-done((bf16[2,128,128]{2,1,0:T(8,128)(2,1)S(1)}, bf16[2,128,128]{2,1,0:T(8,128)(2,1)S(1)}, u32[]{:S(2)}, u32[]{:S(2)}) %collective-permute-start.9) | collective-permute-done | bytes 65568 | tf_op jit(solution)/shard_map/ppermute | solution.py:30
  161.8 10.8 %reduce-scatter.2.cloned.1.call-done = f32[2,128,128]{2,1,0:T(8,128)} async-done(((f32[2,512,128]{2,1,0:T(8,128)}), f32[2,128,128]{2,1,0:T(8,128)}) %reduce-scatter.2.cloned.1.call-update) | async-done | bytes 131088 | tf_op jit(solution)/shard_map/reduce_scatter | solution.py:232
  175.2 4.6 %all-to-all-start.1 = ((bf16[8,64,128]{2,1,0:T(8,128)(2,1)}), bf16[8,64,128]{2,1,0:T(8,128)(2,1)S(1)}, u32[]{:S(2)}, u32[]{:S(2)}) async-start(bf16[8,64,128]{2,1,0:T(8,128)(2,1)} %bitcast.87), calls=%async_computation.2 | async-start | bytes 262144 | tf_op jit(solution)/shard_map/all_to_all | solution.py:260
  180.4 6.1 %all-to-all-done.1 = bf16[8,64,128]{2,1,0:T(8,128)(2,1)S(1)} async-done(((bf16[8,64,128]{2,1,0:T(8,128)(2,1)}), bf16[8,64,128]{2,1,0:T(8,128)(2,1)S(1)}, u32[]{:S(2)}, u32[]{:S(2)}) %all-to-all-start.1) | async-done | bytes 131104 | tf_op jit(solution)/shard_map/all_to_all | solution.py:260
  186.5 3.4 %all-to-all-start.2 = ((bf16[8,64,128]{2,1,0:T(8,128)(2,1)}), bf16[8,64,128]{2,1,0:T(8,128)(2,1)S(1)}, u32[]{:S(2)}, u32[]{:S(2)}) async-start(bf16[8,64,128]{2,1,0:T(8,128)(2,1)} %bitcast.89), calls=%async_computation.3 | async-start | bytes 262144 | tf_op jit(solution)/shard_map/all_to_all | solution.py:261
  190.6 6.0 %all-to-all-done.2 = bf16[8,64,128]{2,1,0:T(8,128)(2,1)S(1)} async-done(((bf16[8,64,128]{2,1,0:T(8,128)(2,1)}), bf16[8,64,128]{2,1,0:T(8,128)(2,1)S(1)}, u32[]{:S(2)}, u32[]{:S(2)}) %all-to-all-start.2) | async-done | bytes 131104 | tf_op jit(solution)/shard_map/all_to_all | solution.py:261
  (331 shorter events, 81.7 us)
Async XLA Ops:
  8.9 28.7 %collective-permute-start.3 = (bf16[2,256,128]{2,1,0:T(8,128)(2,1)S(1)}, bf16[2,256,128]{2,1,0:T(8,128)(2,1)S(1)}, u32[]{:S(2)}, u32[]{:S(2)}) collective-permute-start(bf16[2,256,128]{2,1,0:T(8,128)(2,1)S(1)} %bitcast.325), channel_id=1, source_target_pairs={{8,0},{16,8},{24,16},{9,1},{17,9},{25,17},{10,2},{18,10},{26,18},{... | collective-permute-start | bytes 393224 | tf_op jit(solution)/shard_map/ppermute | solution.py:22
  10.2 27.4 %collective-permute-start.2 = (bf16[2,256,128]{2,1,0:T(8,128)(2,1)S(1)}, bf16[2,256,128]{2,1,0:T(8,128)(2,1)S(1)}, u32[]{:S(2)}, u32[]{:S(2)}) collective-permute-start(bf16[2,256,128]{2,1,0:T(8,128)(2,1)S(1)} %bitcast.326), channel_id=1, source_target_pairs={{0,8},{8,16},{16,24},{1,9},{9,17},{17,25},{2,10},{10,18},{18,26},{... | collective-permute-start | bytes 393224 | tf_op jit(solution)/shard_map/ppermute | solution.py:21
  15.7 20.1 %collective-permute-start.1 = (bf16[2,128,128]{2,1,0:T(8,128)(2,1)S(1)}, bf16[2,128,128]{2,1,0:T(8,128)(2,1)S(1)}, u32[]{:S(2)}, u32[]{:S(2)}) collective-permute-start(bf16[2,128,128]{2,1,0:T(8,128)(2,1)S(1)} %get-tuple-element.130), channel_id=1, source_target_pairs={{8,0},{16,8},{24,16},{9,1},{17,9},{25,17},{10,2},{18,10},{26,18},{... | collective-permute-start | bytes 196616 | tf_op jit(solution)/shard_map/ppermute | solution.py:22
  17.0 18.8 %collective-permute-start = (bf16[2,128,128]{2,1,0:T(8,128)(2,1)S(1)}, bf16[2,128,128]{2,1,0:T(8,128)(2,1)S(1)}, u32[]{:S(2)}, u32[]{:S(2)}) collective-permute-start(bf16[2,128,128]{2,1,0:T(8,128)(2,1)S(1)} %get-tuple-element.129), channel_id=1, source_target_pairs={{0,8},{8,16},{16,24},{1,9},{9,17},{17,25},{2,10},{10,18},{18,26},{... | collective-permute-start | bytes 196616 | tf_op jit(solution)/shard_map/ppermute | solution.py:21
  22.7 55.8 %copy-start.50 = (pred[768]{0:T(1024)(128)(4,1)}, pred[768]{0:T(1024)(128)(4,1)S(1)}, u32[]{:S(2)}) copy-start(pred[768]{0:T(1024)(128)(4,1)S(1)} %get-tuple-element.171) | copy-start | bytes 2308
  22.7 55.8 %copy-start.52 = (pred[768]{0:T(1024)(128)(4,1)}, pred[768]{0:T(1024)(128)(4,1)S(1)}, u32[]{:S(2)}) copy-start(pred[768]{0:T(1024)(128)(4,1)S(1)} %get-tuple-element.172) | copy-start | bytes 2308
  22.7 55.7 %copy-start.35 = (s32[768]{0:T(1024)}, s32[768]{0:T(1024)S(1)}, u32[]{:S(2)}) copy-start(s32[768]{0:T(1024)S(1)} %get-tuple-element.169) | copy-start | bytes 9220
  22.7 55.7 %copy-start.37 = (s32[768]{0:T(1024)}, s32[768]{0:T(1024)S(1)}, u32[]{:S(2)}) copy-start(s32[768]{0:T(1024)S(1)} %get-tuple-element.170) | copy-start | bytes 9220
  22.7 55.7 %copy-start.54 = (s32[256]{0:T(256)}, s32[256]{0:T(256)S(1)}, u32[]{:S(2)}) copy-start(s32[256]{0:T(256)S(1)} %get-tuple-element.163) | copy-start | bytes 3076
  22.8 55.7 %copy-start.56 = (s32[256]{0:T(256)}, s32[256]{0:T(256)S(1)}, u32[]{:S(2)}) copy-start(s32[256]{0:T(256)S(1)} %get-tuple-element.164) | copy-start | bytes 3076
  22.9 47.7 %copy-start.46 = (pred[4,384]{1,0:T(4,128)(4,1)}, pred[4,384]{1,0:T(4,128)(4,1)S(1)}, u32[]{:S(2)}) copy-start(pred[4,384]{1,0:T(4,128)(4,1)S(1)} %get-tuple-element.141) | copy-start | bytes 4612
  22.9 47.7 %copy-start.48 = (pred[4,384]{1,0:T(4,128)(4,1)}, pred[4,384]{1,0:T(4,128)(4,1)S(1)}, u32[]{:S(2)}) copy-start(pred[4,384]{1,0:T(4,128)(4,1)S(1)} %get-tuple-element.142) | copy-start | bytes 4612
  41.5 35.9 %collective-permute-start.7 = (bf16[2,256,128]{2,1,0:T(8,128)(2,1)S(1)}, bf16[2,256,128]{2,1,0:T(8,128)(2,1)S(1)}, u32[]{:S(2)}, u32[]{:S(2)}) collective-permute-start(bf16[2,256,128]{2,1,0:T(8,128)(2,1)S(1)} %bitcast.329), channel_id=1, source_target_pairs={{8,0},{16,8},{24,16},{9,1},{17,9},{25,17},{10,2},{18,10},{26,18},{... | collective-permute-start | bytes 393224 | tf_op jit(solution)/shard_map/ppermute | solution.py:22
  42.8 34.6 %collective-permute-start.6 = (bf16[2,256,128]{2,1,0:T(8,128)(2,1)S(1)}, bf16[2,256,128]{2,1,0:T(8,128)(2,1)}, u32[]{:S(2)}, u32[]{:S(2)}) collective-permute-start(bf16[2,256,128]{2,1,0:T(8,128)(2,1)S(1)} %bitcast.330), channel_id=1, source_target_pairs={{0,8},{8,16},{16,24},{1,9},{9,17},{17,25},{2,10},{10,18},{18,26},{... | collective-permute-start | bytes 393224 | tf_op jit(solution)/shard_map/ppermute | solution.py:21
  59.5 10.8 %collective-permute-start.5 = (bf16[2,128,128]{2,1,0:T(8,128)(2,1)S(1)}, bf16[2,128,128]{2,1,0:T(8,128)(2,1)S(1)}, u32[]{:S(2)}, u32[]{:S(2)}) collective-permute-start(bf16[2,128,128]{2,1,0:T(8,128)(2,1)S(1)} %get-tuple-element.128), channel_id=1, source_target_pairs={{8,0},{16,8},{24,16},{9,1},{17,9},{25,17},{10,2},{18,10},{26,18},{... | collective-permute-start | bytes 196616 | tf_op jit(solution)/shard_map/ppermute | solution.py:22
  60.8 9.5 %collective-permute-start.4 = (bf16[2,128,128]{2,1,0:T(8,128)(2,1)S(1)}, bf16[2,128,128]{2,1,0:T(8,128)(2,1)S(1)}, u32[]{:S(2)}, u32[]{:S(2)}) collective-permute-start(bf16[2,128,128]{2,1,0:T(8,128)(2,1)S(1)} %get-tuple-element.127), channel_id=1, source_target_pairs={{0,8},{8,16},{16,24},{1,9},{9,17},{17,25},{2,10},{10,18},{18,26},{... | collective-permute-start | bytes 196616 | tf_op jit(solution)/shard_map/ppermute | solution.py:21
  136.6 38.5 %all-to-all-start = ((bf16[8,64,128]{2,1,0:T(8,128)(2,1)}), bf16[8,64,128]{2,1,0:T(8,128)(2,1)S(1)}, u32[]{:S(2)}, u32[]{:S(2)}) async-start(bf16[8,64,128]{2,1,0:T(8,128)(2,1)} %bitcast_add_fusion), calls=%async_computation | async-start | bytes 262144 | tf_op jit(solution)/shard_map/all_to_all | solution.py:259
  141.5 31.1 %reduce-scatter.2.cloned.1.call-start = ((), (), s32[]{:S(2)}) async-start(), calls=%async_computation.4 | async-start | bytes 655360 | tf_op jit(solution)/shard_map/reduce_scatter | solution.py:232
  143.4 30.4 %collective-permute-start.11 = (bf16[2,256,128]{2,1,0:T(8,128)(2,1)S(1)}, bf16[2,256,128]{2,1,0:T(8,128)(2,1)S(1)}, u32[]{:S(2)}, u32[]{:S(2)}) collective-permute-start(bf16[2,256,128]{2,1,0:T(8,128)(2,1)S(1)} %get-tuple-element.106), channel_id=1, source_target_pairs={{8,0},{16,8},{24,16},{9,1},{17,9},{25,17},{10,2},{18,10},{26,18},{... | collective-permute-start | bytes 393224 | tf_op jit(solution)/shard_map/ppermute | solution.py:30
  144.7 29.1 %collective-permute-start.10 = (bf16[2,256,128]{2,1,0:T(8,128)(2,1)S(1)}, bf16[2,256,128]{2,1,0:T(8,128)(2,1)S(1)}, u32[]{:S(2)}, u32[]{:S(2)}) collective-permute-start(bf16[2,256,128]{2,1,0:T(8,128)(2,1)S(1)} %get-tuple-element.107), channel_id=1, source_target_pairs={{0,8},{8,16},{16,24},{1,9},{9,17},{17,25},{2,10},{10,18},{18,26},{... | collective-permute-start | bytes 393224 | tf_op jit(solution)/shard_map/ppermute | solution.py:30
  150.1 6.7 %collective-permute-start.8 = (bf16[2,128,128]{2,1,0:T(8,128)(2,1)S(1)}, bf16[2,128,128]{2,1,0:T(8,128)(2,1)S(1)}, u32[]{:S(2)}, u32[]{:S(2)}) collective-permute-start(bf16[2,128,128]{2,1,0:T(8,128)(2,1)S(1)} %get-tuple-element.109), channel_id=1, source_target_pairs={{0,8},{8,16},{16,24},{1,9},{9,17},{17,25},{2,10},{10,18},{18,26},{... | collective-permute-start | bytes 196616 | tf_op jit(solution)/shard_map/ppermute | solution.py:30
  154.9 6.9 %collective-permute-start.9 = (bf16[2,128,128]{2,1,0:T(8,128)(2,1)S(1)}, bf16[2,128,128]{2,1,0:T(8,128)(2,1)S(1)}, u32[]{:S(2)}, u32[]{:S(2)}) collective-permute-start(bf16[2,128,128]{2,1,0:T(8,128)(2,1)S(1)} %get-tuple-element.108), channel_id=1, source_target_pairs={{8,0},{16,8},{24,16},{9,1},{17,9},{25,17},{10,2},{18,10},{26,18},{... | collective-permute-start | bytes 196616 | tf_op jit(solution)/shard_map/ppermute | solution.py:30
  175.2 11.4 %all-to-all-start.1 = ((bf16[8,64,128]{2,1,0:T(8,128)(2,1)}), bf16[8,64,128]{2,1,0:T(8,128)(2,1)S(1)}, u32[]{:S(2)}, u32[]{:S(2)}) async-start(bf16[8,64,128]{2,1,0:T(8,128)(2,1)} %bitcast.87), calls=%async_computation.2 | async-start | bytes 262144 | tf_op jit(solution)/shard_map/all_to_all | solution.py:260
  186.5 10.1 %all-to-all-start.2 = ((bf16[8,64,128]{2,1,0:T(8,128)(2,1)}), bf16[8,64,128]{2,1,0:T(8,128)(2,1)S(1)}, u32[]{:S(2)}, u32[]{:S(2)}) async-start(bf16[8,64,128]{2,1,0:T(8,128)(2,1)} %bitcast.89), calls=%async_computation.3 | async-start | bytes 262144 | tf_op jit(solution)/shard_map/all_to_all | solution.py:261
  (58 other events, 452.1 us)
Sparse Core Ops, SparseCore 0:
  145.2 27.3 reduce-scatter.1
where the time goes:
time: 206 us; the launch traced here: 204 us
  starting transfers between devices  51.6 us (25%)
  local copies, waits for them, and re-layouts  41.9 us (20%)
  waiting for transfers between devices  28.2 us (14%)
  other arithmetic  26.4 us (13%)
  matrix products  22.1 us (11%)
  blocking collectives  18.1 us (9%)
  between operations  15.8 us (8%)
    ppermute x4, starting transfers between devices, padded_2(): before = lax.ppermute(last, axis, up)  20.7 us
    all_gather x2, blocking collectives, receive(): panels = lax.all_gather(key_value, 'seq', axis=1, tiled=True)  18.1 us
    dot_general x12, matrix products, unit_stats(): jnp.einsum('urd,ukd->urk', query_rows, key_rows, preferred_element_type=j...  13.3 us
    ppermute x4, starting transfers between devices, from_behind(): return lax.ppermute(block, axis, route)  12.6 us
    reduce_scatter x1, waiting for transfers between devices, per_device(): lax.psum_scatter(panel_back.astype(jnp.float32), 'seq', scatter_dimension...  10.8 us
    broadcast_in_dim x17, local copies, waits for them, and re-layouts, expand(): jnp.repeat(stats[0].reshape(-1), repeats)  9.01 us
    dot_general x12, matrix products, unit_stats(): jnp.einsum('urk,ukd->urd', rounded, value_rows, preferred_element_type=jn...  8.73 us
    reduce_sum x6, local copies, waits for them, and re-layouts, combine(): factor[:, None] * entry[2]  7.15 us
  transfers between devices with their start and end apart: 16, of which 5 were waited for; matrix products, arithmetic and copies ran while one was open for 13% of the time, Pallas kernels for 0%

commit v1 on v0

v1 whole, which is shorter than its diff:
```python
import functools

import jax
import jax.numpy as jnp
from jax import lax
from jax.experimental import pallas as pl
from jax.experimental.pallas import tpu as pltpu
from jax.sharding import PartitionSpec as P

BLOCK = 128
EDGE = BLOCK // 2
REST = 2 * BLOCK - EDGE
MASKED = -1e30
LOG2E = 1.4426950408889634
F32 = jnp.float32
BF16 = jnp.bfloat16
VMEM = pl.BlockSpec(memory_space=pltpu.VMEM)


def nt(a, b):
    return lax.dot_general(a, b, (((1,), (1,)), ((), ())), preferred_element_type=F32)


def nn(a, b):
    return lax.dot_general(a, b, (((1,), (0,)), ((), ())), preferred_element_type=F32)


def tn(a, b):
    return lax.dot_general(a, b, (((0,), (0,)), ((), ())), preferred_element_type=F32)


def pair_sum(x, scratch):
    rows = x.shape[0]
    scratch[:rows] = x
    return scratch[pl.ds(0, rows // 2, stride=2), :] + scratch[pl.ds(1, rows // 2, stride=2), :]


def coarse(x, scratch):
    return (pair_sum(x.astype(F32), scratch) * 0.5).astype(BF16)


def spread(x, scratch):
    rows = x.shape[0]
    scratch[pl.ds(0, rows, stride=2), :] = x
    scratch[pl.ds(1, rows, stride=2), :] = x
    return scratch[: 2 * rows]


def wide_distances(seq_count):
    return sorted({i ^ (i + 1) for i in range(seq_count - 1)})


def prep_kernel(seq_count, key_ref, value_ref, *refs):
    sends, scratches = refs[: seq_count - 1], refs[seq_count - 1 :]
    seq_index = lax.axis_index("seq")
    wides = wide_distances(seq_count)
    rows = key_ref.shape[0]
    for i, ref in enumerate((key_ref, value_ref)):
        level_1 = coarse(ref[...], scratches[2 * i])
        level_2 = coarse(level_1, scratches[2 * i + 1])
        for d in range(1, seq_count):
            out = sends[d - 1]
            partner = seq_index ^ d
            if d not in wides:
                out[i] = level_2
                continue

            @pl.when(partner == seq_index + 1)
            def _():
                out[i, :BLOCK] = ref[rows - BLOCK :]
                out[i, BLOCK:] = level_1[:REST]

            @pl.when(partner == seq_index - 1)
            def _():
                out[i, :BLOCK] = ref[:BLOCK]
                out[i, BLOCK:] = level_1[EDGE:]

            @pl.when((partner != seq_index + 1) & (partner != seq_index - 1))
            def _():
                out[i, :BLOCK] = level_2
                out[i, BLOCK:] = level_1[:REST]


def slots_of(block, block_count):
    parent, odd = block // 2, block % 2
    if block_count == 4:
        first = parent == 0
        return [
            (jnp.where(first, 3, 0), None),
            (jnp.where(first, 2, 1), jnp.where(first, odd == 0, odd == 1)),
        ]
    near = jnp.where(odd == 0, 2 * parent + 2, 2 * parent - 1)
    raw = [2 * parent - 2, near, 2 * parent + 3]
    return [(jnp.clip(j, 0, block_count - 1), (j >= 0) & (j < block_count)) for j in raw]


def softmax_parts(parts):
    peak = functools.reduce(jnp.maximum, [jnp.max(p, axis=-1, keepdims=True) for p in parts])
    exps = [jnp.exp2(p - peak) for p in parts]
    total = functools.reduce(jnp.add, [jnp.sum(e, axis=-1, keepdims=True) for e in exps])
    return peak, exps, total


def wide_lanes(column, width):
    return jnp.broadcast_to(column, (column.shape[0], width))


def main_kernel(seq_count, top_level, *refs):
    refs = list(refs)

    def take(count):
        taken = refs[:count]
        del refs[:count]
        return taken

    query_ref, key_ref, value_ref, cot_ref = take(4)
    received = take(seq_count - 1)
    (attended_ref,) = take(1)
    sends = take(seq_count - 1)
    grad_query_ref, local_ref = take(2)
    ext, near = take(2)
    panels = take(top_level - 1)
    panel_grads = take(top_level - 1)
    pools = refs

    def pool():
        return pools.pop(0)

    seq_index = lax.axis_index("seq")
    wides = wide_distances(seq_count)
    rows, width = query_ref.shape
    blocks = rows // BLOCK
    scale = width ** (-0.5)
    factor = scale * LOG2E
    has_prev, has_next = seq_index > 0, seq_index < seq_count - 1

    for panel in panels:
        panel[...] = jnp.zeros(panel.shape, BF16)
    for i, ref in enumerate((key_ref, value_ref)):
        ext[i, BLOCK : BLOCK + rows] = ref[...]

    @pl.when(seq_index == 0)
    def _():
        ext[:, :BLOCK] = jnp.zeros((2, BLOCK, width), BF16)
        near[:, : 2 * BLOCK] = jnp.zeros((2, 2 * BLOCK, width), BF16)

    @pl.when(seq_index == seq_count - 1)
    def _():
        ext[:, BLOCK + rows :] = jnp.zeros((2, BLOCK, width), BF16)
        near[:, 2 * BLOCK :] = jnp.zeros((2, 2 * BLOCK, width), BF16)

    halo_scratch = pool()
    for d in range(1, seq_count):
        got = received[d - 1]
        partner = seq_index ^ d
        at = pl.ds(pl.multiple_of(partner * BLOCK, BLOCK), BLOCK)
        if d not in wides:
            for i in range(2):
                panels[0][i, at] = got[i]
            continue

        @pl.when(partner == seq_index - 1)
        def _():
            for i in range(2):
                ext[i, :BLOCK] = got[i, :BLOCK]
                near[i, :REST] = got[i, BLOCK:]
                near[i, REST : 2 * BLOCK] = coarse(got[i, :BLOCK], halo_scratch)

        @pl.when(partner == seq_index + 1)
        def _():
            for i in range(2):
                ext[i, BLOCK + rows :] = got[i, :BLOCK]
                near[i, 2 * BLOCK : 2 * BLOCK + EDGE] = coarse(got[i, :BLOCK], halo_scratch)
                near[i, 2 * BLOCK + EDGE :] = got[i, BLOCK:]

        @pl.when((partner != seq_index + 1) & (partner != seq_index - 1))
        def _():
            for i in range(2):
                panels[0][i, at] = got[i, :BLOCK]

    panel_scratch = pool()
    for level in range(3, top_level + 1):
        for i in range(2):
            panels[level - 2][i] = coarse(panels[level - 3][i], panel_scratch)

    level_queries = [query_ref[...]]
    for level in range(1, top_level + 1):
        level_queries.append(coarse(level_queries[-1], pool()))

    def masked(scores, valid):
        return scores if valid is None else jnp.where(valid, scores, MASKED)

    def unit(query, pieces):
        scores = []
        for key, _, valid in pieces:
            scores.append(masked(nt(query, key) * factor, valid))
        peak, exps, total = softmax_parts(scores)
        rounded = [e.astype(BF16) for e in exps]
        sums = functools.reduce(jnp.add, [nn(r, p[1]) for r, p in zip(rounded, pieces)])
        return wide_lanes(peak, width), wide_lanes(total, width), sums, exps, rounded

    def window(ref, lo, hi):
        return ref[0, lo * BLOCK : hi * BLOCK], ref[1, lo * BLOCK : hi * BLOCK]

    level_pieces = []
    fine = []
    for a in range(blocks):
        if a == 0:
            cuts = [(0, 1, has_prev), (1, 3, None)]
        elif a == blocks - 1:
            cuts = [(a, a + 2, None), (a + 2, a + 3, has_next)]
        else:
            cuts = [(a, a + 3, None)]
        fine.append([window(ext, lo, hi) + (valid, (lo, hi)) for lo, hi, valid in cuts])
    level_pieces.append(fine)
    level_pieces.append(
        [
            [
                window(near, 0, 1) + (has_prev, (0, 1)),
                window(near, 2, 4) + (has_next, (2, 4)),
            ],
            [
                window(near, 0, 2) + (has_prev, (0, 2)),
                window(near, 3, 4) + (has_next, (3, 4)),
            ],
        ]
    )
    for level in range(2, top_level + 1):
        block_count = seq_count >> (level - 2)
        pieces = []
        for index, valid in slots_of(seq_index >> (level - 2), block_count):
            at = pl.ds(pl.multiple_of(index * BLOCK, BLOCK), BLOCK)
            panel = panels[level - 2]
            pieces.append((panel[0, at], panel[1, at], valid, at))
        level_pieces.append([pieces])

    level_units = []
    for level, pieces_of in enumerate(level_pieces):
        query = level_queries[level]
        step = query.shape[0] // len(pieces_of)
        level_units.append(
            [
                unit(query[a * step : (a + 1) * step], [p[:3] for p in pieces])
                for a, pieces in enumerate(pieces_of)
            ]
        )

    def stacked(units, which):
        return jnp.concatenate([u[which] for u in units], axis=0)

    run = [stacked(level_units[top_level], w) for w in range(3)]
    own_factors, run_factors = [None] * top_level, [None] * top_level
    for level in range(top_level - 1, -1, -1):
        up_peak, up_total, up_sums = [spread(x, pool()) for x in run]
        peak, total, sums = [stacked(level_units[level], w) for w in range(3)]
        both = jnp.maximum(peak, up_peak)
        own = jnp.exp2(peak - both)
        up = 2.0 * jnp.exp2(up_peak - both)
        own_factors[level], run_factors[level] = own, up
        run = [both, own * total + up * up_total, own * sums + up * up_sums]

    inverse = 1.0 / run[1]
    attended = run[2] * inverse
    attended_ref[...] = attended.astype(BF16)

    cot = cot_ref[...].astype(F32)
    inner = wide_lanes(jnp.sum(cot * attended, axis=-1, keepdims=True), width)
    grad, shift = cot * inverse, inner * inverse
    level_grads = []
    for level in range(top_level):
        level_grads.append((own_factors[level] * grad, own_factors[level] * shift))
        grad = pair_sum(run_factors[level] * grad, pool())
        shift = pair_sum(run_factors[level] * shift, pool())
    level_grads.append((grad, shift))

    def unit_back(query, grad, shift, pieces, exps, rounded):
        grad_rounded = grad.astype(BF16)
        grad_scaled = (grad * scale).astype(BF16)
        shift_scaled = shift[:, :1] * scale
        grad_query = None
        outs = []
        for piece, e, r in zip(pieces, exps, rounded):
            key, value = piece[0], piece[1]
            score_grad = (e * (nt(grad_scaled, value) - shift_scaled)).astype(BF16)
            part = nn(score_grad, key)
            grad_query = part if grad_query is None else grad_query + part
            outs.append((tn(score_grad, query), tn(r, grad_rounded)))
        return grad_query, outs

    for panel_grad in panel_grads:
        panel_grad[...] = jnp.zeros(panel_grad.shape, F32)

    grad_queries = []
    fine_parts = [[[] for _ in range(blocks + 2)] for _ in range(2)]
    near_parts = [[[] for _ in range(4)] for _ in range(2)]
    for level, pieces_of in reversed(list(enumerate(level_pieces))):
        query = level_queries[level]
        step = query.shape[0] // len(pieces_of)
        grad, shift = level_grads[level]
        parts = []
        for a, pieces in enumerate(pieces_of):
            cut = slice(a * step, (a + 1) * step)
            exps, rounded = level_units[level][a][3:]
            grad_query, outs = unit_back(query[cut], grad[cut], shift[cut], pieces, exps, rounded)
            parts.append(grad_query)
            for piece, out in zip(pieces, outs):
                for i in range(2):
                    if level >= 2:
                        panel_grads[level - 2][i, piece[3]] += out[i]
                        continue
                    into = fine_parts if level == 0 else near_parts
                    lo, hi = piece[3]
                    for b in range(lo, hi):
                        into[i][b].append(out[i][(b - lo) * BLOCK : (b - lo + 1) * BLOCK])
        grad_queries.append(jnp.concatenate(parts, axis=0))

    run_grad = grad_queries[0]
    for grad_query in grad_queries[1:]:
        run_grad = grad_query + 0.5 * spread(run_grad, pool())
    grad_query_ref[...] = run_grad.astype(BF16)

    for level in range(top_level, 2, -1):
        for i in range(2):
            panel_grads[level - 3][i] += 0.5 * spread(panel_grads[level - 2][i], panel_scratch)

    def total_of(parts):
        return functools.reduce(jnp.add, parts)

    for i in range(2):
        for b in range(blocks):
            local_ref[i, b * BLOCK : (b + 1) * BLOCK] = total_of(fine_parts[i][b + 1])
    near_grads = [[total_of(p) for p in near_parts[i]] for i in range(2)]
    to_prev = [
        total_of(fine_parts[i][0]) + 0.5 * spread(near_grads[i][1][EDGE:], pool()) for i in range(2)
    ]
    to_next = [
        total_of(fine_parts[i][blocks + 1]) + 0.5 * spread(near_grads[i][2][:EDGE], pool())
        for i in range(2)
    ]
    for d in range(1, seq_count):
        out = sends[d - 1]
        partner = seq_index ^ d
        at = pl.ds(pl.multiple_of(partner * BLOCK, BLOCK), BLOCK)
        if d not in wides:
            for i in range(2):
                out[i] = panel_grads[0][i, at].astype(BF16)
            continue

        @pl.when(partner == seq_index - 1)
        def _():
            for i in range(2):
                out[i, :BLOCK] = to_prev[i].astype(BF16)
                out[i, BLOCK : 2 * BLOCK] = near_grads[i][0].astype(BF16)
                out[i, 2 * BLOCK :] = near_grads[i][1][:EDGE].astype(BF16)

        @pl.when(partner == seq_index + 1)
        def _():
            for i in range(2):
                out[i, :BLOCK] = to_next[i].astype(BF16)
                out[i, BLOCK : BLOCK + EDGE] = near_grads[i][2][EDGE:].astype(BF16)
                out[i, BLOCK + EDGE :] = near_grads[i][3].astype(BF16)

        @pl.when((partner != seq_index + 1) & (partner != seq_index - 1))
        def _():
            for i in range(2):
                out[i, :BLOCK] = panel_grads[0][i, at].astype(BF16)
                out[i, BLOCK:] = jnp.zeros((REST, width), BF16)


def combine_kernel(seq_count, head_count, grad_query_ref, local_ref, *refs):
    received, refs = refs[: seq_count - 1], refs[seq_count - 1 :]
    outs, refs = refs[:head_count], refs[head_count:]
    total, level_1, level_2 = refs
    seq_index, head_index = lax.axis_index("seq"), lax.axis_index("head")
    wides = wide_distances(seq_count)
    rows, width = local_ref.shape[1:]
    share = rows // head_count

    level_1[...] = jnp.zeros(level_1.shape, F32)
    level_2[...] = jnp.zeros(level_2.shape, F32)
    for i in range(2):
        total[i] = local_ref[i]
    for d in range(1, seq_count):
        got = received[d - 1]
        partner = seq_index ^ d
        if d not in wides:
            for i in range(2):
                level_2[i] += got[i].astype(F32)
            continue

        @pl.when(partner == seq_index - 1)
        def _():
            for i in range(2):
                total[i, :BLOCK] += got[i, :BLOCK].astype(F32)
                level_1[i, EDGE:] += got[i, BLOCK:].astype(F32)

        @pl.when(partner == seq_index + 1)
        def _():
            for i in range(2):
                total[i, rows - BLOCK :] += got[i, :BLOCK].astype(F32)
                level_1[i, :REST] += got[i, BLOCK:].astype(F32)

        @pl.when((partner != seq_index + 1) & (partner != seq_index - 1))
        def _():
            for i in range(2):
                level_2[i] += got[i, :BLOCK].astype(F32)

    for i in range(2):
        half = level_2[i] * 0.5
        for phase in range(2):
            level_1[i, pl.ds(phase, half.shape[0], stride=2), :] += half
        half = level_1[i] * 0.5
        for phase in range(2):
            total[i, pl.ds(phase, half.shape[0], stride=2), :] += half
    for d in range(head_count):
        at = pl.ds(pl.multiple_of((head_index ^ d) * share, share), share)
        outs[d][0] = grad_query_ref[at, :]
        outs[d][1] = total[0, at].astype(BF16)
        outs[d][2] = total[1, at].astype(BF16)


def place_kernel(head_count, *refs):
    parts, outs = refs[:head_count], refs[head_count:]
    head_index = lax.axis_index("head")
    width = parts[0].shape[-1]
    for d in range(head_count):
        at = pl.ds(pl.multiple_of((head_index ^ d) * width, width), width)
        for i in range(3):
            outs[i][:, at] = parts[d][i]


def call(kernel, outs, scratch, args):
    return pl.pallas_call(
        kernel,
        out_shape=outs,
        in_specs=[VMEM] * len(args),
        out_specs=[VMEM] * len(outs),
        scratch_shapes=scratch,
        compiler_params=pltpu.CompilerParams(vmem_limit_bytes=48 * 2**20),
    )(*args)


def swap(x, axis, distance):
    return lax.ppermute(x, axis, [(i, i ^ distance) for i in range(lax.axis_size(axis))])


def per_device(queries, keys, values, grad_out):
    seq_count, head_count = lax.axis_size("seq"), lax.axis_size("head")
    rows, width = queries.shape
    assert rows == 4 * BLOCK
    fine_blocks = rows * seq_count // BLOCK
    top_level = (fine_blocks // 4).bit_length() - 1
    wides = wide_distances(seq_count)
    distances = range(1, seq_count)

    def shape(dims, dtype=BF16):
        return jax.ShapeDtypeStruct(dims, dtype)

    def f32(*dims):
        return pltpu.VMEM(dims, F32)

    payloads = [shape((2, BLOCK + REST if d in wides else BLOCK, width)) for d in distances]
    sends = call(
        functools.partial(prep_kernel, seq_count),
        payloads,
        [f32(rows, width), f32(rows // 2, width)] * 2,
        (keys, values),
    )
    received = [swap(x, "seq", d) for d, x in zip(distances, sends)]

    panel_rows = [(seq_count >> (level - 2)) * BLOCK for level in range(2, top_level + 1)]
    pools = [f32(BLOCK, width), f32(max(seq_count * BLOCK, rows), width)]
    pools += [f32(rows >> level, width) for level in range(top_level)]
    for level in range(top_level - 1, -1, -1):
        pools += [f32(rows >> level, width)] * 3
    for level in range(top_level):
        pools += [f32(rows >> level, width)] * 2
    for level in range(top_level - 1, -1, -1):
        pools += [f32(rows >> level, width)]
    pools += [f32(BLOCK, width)] * 4
    main = call(
        functools.partial(main_kernel, seq_count, top_level),
        [shape((rows, width))] + payloads + [shape((rows, width)), shape((2, rows, width), F32)],
        [pltpu.VMEM((2, rows + 2 * BLOCK, width), BF16), pltpu.VMEM((2, 4 * BLOCK, width), BF16)]
        + [pltpu.VMEM((2, r, width), BF16) for r in panel_rows]
        + [f32(2, r, width) for r in panel_rows]
        + pools,
        (queries, keys, values, grad_out, *received),
    )
    attended, sends, grad_query, local = main[0], main[1:seq_count], main[-2], main[-1]
    returned = [swap(x, "seq", d) for d, x in zip(distances, sends)]

    share = rows // head_count
    parts = call(
        functools.partial(combine_kernel, seq_count, head_count),
        [shape((3, share, width))] * head_count,
        [f32(2, rows, width), f32(2, rows // 2, width), f32(2, rows // 4, width)],
        (grad_query, local, *returned),
    )
    parts = [parts[0]] + [swap(parts[d], "head", d) for d in range(1, head_count)]
    grads = call(
        functools.partial(place_kernel, head_count),
        [shape((share, head_count * width))] * 3,
        [],
        parts,
    )
    return (attended, *grads)


def solution(mesh):
    return jax.shard_map(
        per_device,
        mesh=mesh,
        in_specs=(P("seq", "head"),) * 4,
        out_specs=(P("seq", "head"),) + (P(("seq", "head"), None),) * 3,
        check_vma=False,
    )
```

time: 206 us -> 43.8 us (0.21)
  local copies, waits for them, and re-layouts: 41.9 us -> 1.81 us
  starting transfers between devices: 51.6 us -> 16.4 us
  other arithmetic: 26.4 us -> 0 us
  matrix products: 22.1 us -> 0 us
  blocking collectives: 18.1 us -> 0 us
  between operations: 15.8 us -> 0.68 us
  waiting for transfers between devices: 28.2 us -> 18 us
  Pallas kernels: 0 us -> 6.67 us
    dot_general x24 -> x0, matrix products: 22.1 us -> none  [the longest x12 13.3 us: unit_stats(): jnp.einsum('urd,ukd->urk', query_rows, key_rows, preferred_element_type=j...]
    ppermute x12 -> x13, starting transfers between devices: 38.5 us -> 16.4 us  [swap(): lax.ppermute(x, axis, [(i, i ^ distance) for i in range(lax.axis_size(axi...]
    all_gather x2 -> x0, blocking collectives: 18.1 us -> none  [receive(): panels = lax.all_gather(key_value, 'seq', axis=1, tiled=True)]
    broadcast_in_dim x34 -> x0, local copies, waits for them, and re-layouts: 15.8 us -> none  [the longest x17 9.01 us: expand(): jnp.repeat(stats[0].reshape(-1), repeats)]
    all_to_all x3 -> x0, starting transfers between devices: 12.8 us -> none  [the longest x1 4.88 us: per_device(): lax.all_to_all(query_grad, 'head', split_axis=0, concat_axis=1, tiled=True)]
    ppermute x12 -> x13, waiting for transfers between devices: 5.22 us -> 18 us  [swap(): lax.ppermute(x, axis, [(i, i ^ distance) for i in range(lax.axis_size(axi...]
    all_to_all x3 -> x0, waiting for transfers between devices: 12.1 us -> none  [the longest x1 6.11 us: per_device(): lax.all_to_all(key_value_grad[0], 'head', split_axis=0, concat_axis=1, ti...]
    reduce_sum x11 -> x0, other arithmetic: 12 us -> none  [the longest x3 4.39 us: unit_stats(): row_peak = jnp.max(scores, axis=-1)]
  transfers between devices with their start and end apart: 16 -> 13, of which waited for: 5 -> 7; matrix products, arithmetic and copies ran while one was open for 13% -> 0% of each run, Pallas kernels for 0% -> 0%
where the time goes in v1:
time: 43.8 us; the launch traced here: 43.6 us
  waiting for transfers between devices  18 us (41%)
  starting transfers between devices  16.4 us (37%)
  Pallas kernels  6.67 us (15%)
  local copies, waits for them, and re-layouts  1.81 us (4%)
  between operations  0.68 us (2%)
    ppermute x13, waiting for transfers between devices, swap(): lax.ppermute(x, axis, [(i, i ^ distance) for i in range(lax.axis_size(axi...  18 us
    ppermute x13, starting transfers between devices, swap(): lax.ppermute(x, axis, [(i, i ^ distance) for i in range(lax.axis_size(axi...  16.4 us
    pallas_call x4, Pallas kernels, call(): pl.pallas_call(kernel, out_shape=outs, in_specs=[VMEM] * len(args), out_s...  6.67 us
    unnamed x8, local copies, waits for them, and re-layouts  1.81 us
  transfers between devices with their start and end apart: 13, of which 7 were waited for; matrix products, arithmetic and copies ran while one was open for 0% of the time, Pallas kernels for 0%

profile of v1, /device:TPU:0, one launch (start us, length us, event | category | flops | bytes accessed | tf_op | source)
XLA Modules:
  0.0 43.6 jit_solution(18077721721997774556)
XLA Ops:
  0.6 0.9 %copy-done = bf16[512,128]{1,0:T(8,128)(2,1)S(1)} copy-done((bf16[512,128]{1,0:T(8,128)(2,1)S(1)}, bf16[512,128]{1,0:T(8,128)(2,1)}, u32[]{:S(2)}) %copy-start) | copy-done | bytes 131096
  1.5 0.9 %copy-done.1 = bf16[512,128]{1,0:T(8,128)(2,1)S(1)} copy-done((bf16[512,128]{1,0:T(8,128)(2,1)S(1)}, bf16[512,128]{1,0:T(8,128)(2,1)}, u32[]{:S(2)}) %copy-start.1) | copy-done | bytes 131096
  2.4 0.1 shard_map.75
  2.6 3.0 %collective-permute-start = (bf16[2,320,128]{2,1,0:T(8,128)(2,1)S(1)}, bf16[2,320,128]{2,1,0:T(8,128)(2,1)S(1)}, u32[]{:S(2)}, u32[]{:S(2)}) collective-permute-start(bf16[2,320,128]{2,1,0:T(8,128)(2,1)S(1)} %get-tuple-element.24), channel_id=1, source_target_pairs={{0,8},{8,0},{16,24},{24,16},{1,9},{9,1},{17,25},{25,17},{2,10},{10... | collective-permute-start | bytes 491528 | tf_op jit(solution)/shard_map/ppermute | solution.py:444
  5.6 1.5 %collective-permute-start.2 = (bf16[2,320,128]{2,1,0:T(8,128)(2,1)S(1)}, bf16[2,320,128]{2,1,0:T(8,128)(2,1)S(1)}, u32[]{:S(2)}, u32[]{:S(2)}) collective-permute-start(bf16[2,320,128]{2,1,0:T(8,128)(2,1)S(1)} %get-tuple-element.26), channel_id=1, source_target_pairs={{0,24},{8,16},{16,8},{24,0},{1,25},{9,17},{17,9},{25,1},{2,26},{10... | collective-permute-start | bytes 491528 | tf_op jit(solution)/shard_map/ppermute | solution.py:444
  7.2 4.9 %collective-permute-done.1.refs_5_ = bf16[2,128,128]{2,1,0:T(8,128)(2,1)S(1)} collective-permute-done((bf16[2,128,128]{2,1,0:T(8,128)(2,1)S(1)}, bf16[2,128,128]{2,1,0:T(8,128)(2,1)S(1)}, u32[]{:S(2)}, u32[]{:S(2)}) %collective-permute-start.1) | collective-permute-done | bytes 65568 | tf_op jit(solution)/shard_map/ppermute | solution.py:444
  12.1 2.5 %collective-permute-done.2.refs_6_ = bf16[2,320,128]{2,1,0:T(8,128)(2,1)S(1)} collective-permute-done((bf16[2,320,128]{2,1,0:T(8,128)(2,1)S(1)}, bf16[2,320,128]{2,1,0:T(8,128)(2,1)S(1)}, u32[]{:S(2)}, u32[]{:S(2)}) %collective-permute-start.2) | collective-permute-done | bytes 163872 | tf_op jit(solution)/shard_map/ppermute | solution.py:444
  14.5 5.4 %shard_map.76 = (bf16[512,128]{1,0:T(8,128)(2,1)}, bf16[2,320,128]{2,1,0:T(8,128)(2,1)S(1)}, bf16[2,128,128]{2,1,0:T(8,128)(2,1)S(1)}, bf16[2,320,128]{2,1,0:T(8...) custom-call(bf16[512,128]{1,0:T(8,128)(2,1)S(1)} %copy-done.2, bf16[512,128]{1,0:T(8,128)(2,1)S(1)} %copy-done, ...), custom_call_target="tpu_custom_call" | custom-call | tf_op jit(solution)/shard_map/pallas_call | solution.py:433
  20.0 1.5 %collective-permute-start.3 = (bf16[2,320,128]{2,1,0:T(8,128)(2,1)S(1)}, bf16[2,320,128]{2,1,0:T(8,128)(2,1)S(1)}, u32[]{:S(2)}, u32[]{:S(2)}) collective-permute-start(bf16[2,320,128]{2,1,0:T(8,128)(2,1)S(1)} %get-tuple-element.30), channel_id=1, source_target_pairs={{0,8},{8,0},{16,24},{24,16},{1,9},{9,1},{17,25},{25,17},{2,10},{10... | collective-permute-start | bytes 491528 | tf_op jit(solution)/shard_map/ppermute | solution.py:444
  21.5 0.2 collective-permute-start.5
  21.7 1.8 %collective-permute-start.4 = (bf16[2,128,128]{2,1,0:T(8,128)(2,1)S(1)}, bf16[2,128,128]{2,1,0:T(8,128)(2,1)S(1)}, u32[]{:S(2)}, u32[]{:S(2)}) collective-permute-start(bf16[2,128,128]{2,1,0:T(8,128)(2,1)S(1)} %get-tuple-element.31), channel_id=1, source_target_pairs={{0,16},{8,24},{16,0},{24,8},{1,17},{9,25},{17,1},{25,9},{2,18},{10... | collective-permute-start | bytes 196616 | tf_op jit(solution)/shard_map/ppermute | solution.py:444
  23.4 3.1 %collective-permute-done.4.refs_1_ = bf16[2,128,128]{2,1,0:T(8,128)(2,1)S(1)} collective-permute-done((bf16[2,128,128]{2,1,0:T(8,128)(2,1)S(1)}, bf16[2,128,128]{2,1,0:T(8,128)(2,1)S(1)}, u32[]{:S(2)}, u32[]{:S(2)}) %collective-permute-start.4) | collective-permute-done | bytes 65568 | tf_op jit(solution)/shard_map/ppermute | solution.py:444
  26.6 0.2 collective-permute-done.3.refs_0_
  26.8 1.9 %collective-permute-done.5.refs_2_ = bf16[2,320,128]{2,1,0:T(8,128)(2,1)S(1)} collective-permute-done((bf16[2,320,128]{2,1,0:T(8,128)(2,1)S(1)}, bf16[2,320,128]{2,1,0:T(8,128)(2,1)S(1)}, u32[]{:S(2)}, u32[]{:S(2)}) %collective-permute-start.5) | collective-permute-done | bytes 163872 | tf_op jit(solution)/shard_map/ppermute | solution.py:444
  28.7 0.2 shard_map.77
  28.9 0.1 collective-permute-start.6
  29.0 1.8 %collective-permute-start.7 = (bf16[3,64,128]{2,1,0:T(8,128)(2,1)S(1)}, bf16[3,64,128]{2,1,0:T(8,128)(2,1)S(1)}, u32[]{:S(2)}, u32[]{:S(2)}) collective-permute-start(bf16[3,64,128]{2,1,0:T(8,128)(2,1)S(1)} %get-tuple-element.35), channel_id=1, source_target_pairs={{0,2},{1,3},{2,0},{3,1},{4,6},{5,7},{6,4},{7,5},{8,10},{9,11},{10,... | collective-permute-start | bytes 147464 | tf_op jit(solution)/shard_map/ppermute | solution.py:444
  30.7 0.1 collective-permute-start.8
  30.8 2.7 %collective-permute-start.9 = (bf16[3,64,128]{2,1,0:T(8,128)(2,1)S(1)}, bf16[3,64,128]{2,1,0:T(8,128)(2,1)S(1)}, u32[]{:S(2)}, u32[]{:S(2)}) collective-permute-start(bf16[3,64,128]{2,1,0:T(8,128)(2,1)S(1)} %get-tuple-element.37), channel_id=1, source_target_pairs={{0,4},{1,5},{2,6},{3,7},{4,0},{5,1},{6,2},{7,3},{8,12},{9,13},{10,... | collective-permute-start | bytes 147464 | tf_op jit(solution)/shard_map/ppermute | solution.py:444
  33.6 3.6 %collective-permute-start.11 = (bf16[3,64,128]{2,1,0:T(8,128)(2,1)S(1)}, bf16[3,64,128]{2,1,0:T(8,128)(2,1)S(1)}, u32[]{:S(2)}, u32[]{:S(2)}) collective-permute-start(bf16[3,64,128]{2,1,0:T(8,128)(2,1)S(1)} %get-tuple-element.39), channel_id=1, source_target_pairs={{0,6},{1,7},{2,4},{3,5},{4,2},{5,3},{6,0},{7,1},{8,14},{9,15},{10,... | collective-permute-start | bytes 147464 | tf_op jit(solution)/shard_map/ppermute | solution.py:444
  37.2 0.1 collective-permute-start.12
  37.3 3.7 %collective-permute-done.10.refs_5_ = bf16[3,64,128]{2,1,0:T(8,128)(2,1)S(1)} collective-permute-done((bf16[3,64,128]{2,1,0:T(8,128)(2,1)S(1)}, bf16[3,64,128]{2,1,0:T(8,128)(2,1)S(1)}, u32[]{:S(2)}, u32[]{:S(2)}) %collective-permute-start.10) | collective-permute-done | bytes 49184 | tf_op jit(solution)/shard_map/ppermute | solution.py:444
  41.0 1.8 %collective-permute-done.12.refs_7_ = bf16[3,64,128]{2,1,0:T(8,128)(2,1)S(1)} collective-permute-done((bf16[3,64,128]{2,1,0:T(8,128)(2,1)S(1)}, bf16[3,64,128]{2,1,0:T(8,128)(2,1)S(1)}, u32[]{:S(2)}, u32[]{:S(2)}) %collective-permute-start.12) | collective-permute-done | bytes 49184 | tf_op jit(solution)/shard_map/ppermute | solution.py:444
  42.8 0.8 %shard_map.78 = (bf16[64,1024]{1,0:T(8,128)(2,1)}, bf16[64,1024]{1,0:T(8,128)(2,1)}, bf16[64,1024]{1,0:T(8,128)(2,1)}) custom-call(bf16[3,64,128]{2,1,0:T(8,128)(2,1)S(1)} %get-tuple-element.33.refs_0_, bf16[3,64,128]{2,1,0:T(8,128)(2,1)S(1)} %collective-permute-done.6.refs_1_, bf16[3,64,128]{2,1,0:T(8,128)(2,1)S(1)} %collective-permute-done.7.refs_2_, ...), custom_call_target="tpu_custom_call" | custom-call | tf_op jit(solution)/shard_map/pallas_call | solution.py:433
  (14 shorter events, 0.1 us)
Async XLA Ops:
  0.6 0.9 %copy-start = (bf16[512,128]{1,0:T(8,128)(2,1)S(1)}, bf16[512,128]{1,0:T(8,128)(2,1)}, u32[]{:S(2)}) copy-start(bf16[512,128]{1,0:T(8,128)(2,1)} %refs_1_.1) | copy-start | bytes 393220
  1.5 0.9 %copy-start.1 = (bf16[512,128]{1,0:T(8,128)(2,1)S(1)}, bf16[512,128]{1,0:T(8,128)(2,1)}, u32[]{:S(2)}) copy-start(bf16[512,128]{1,0:T(8,128)(2,1)} %refs_2_.1) | copy-start | bytes 393220
  2.4 12.1 %copy-start.2 = (bf16[512,128]{1,0:T(8,128)(2,1)S(1)}, bf16[512,128]{1,0:T(8,128)(2,1)}, u32[]{:S(2)}) copy-start(bf16[512,128]{1,0:T(8,128)(2,1)} %refs_0_.1) | copy-start | bytes 393220
  2.4 12.1 %copy-start.3 = (bf16[512,128]{1,0:T(8,128)(2,1)S(1)}, bf16[512,128]{1,0:T(8,128)(2,1)}, u32[]{:S(2)}) copy-start(bf16[512,128]{1,0:T(8,128)(2,1)} %refs_3_.1) | copy-start | bytes 393220
  2.6 9.5 %collective-permute-start = (bf16[2,320,128]{2,1,0:T(8,128)(2,1)S(1)}, bf16[2,320,128]{2,1,0:T(8,128)(2,1)S(1)}, u32[]{:S(2)}, u32[]{:S(2)}) collective-permute-start(bf16[2,320,128]{2,1,0:T(8,128)(2,1)S(1)} %get-tuple-element.24), channel_id=1, source_target_pairs={{0,8},{8,0},{16,24},{24,16},{1,9},{9,1},{17,25},{25,17},{2,10},{10... | collective-permute-start | bytes 491528 | tf_op jit(solution)/shard_map/ppermute | solution.py:444
  5.6 8.9 %collective-permute-start.2 = (bf16[2,320,128]{2,1,0:T(8,128)(2,1)S(1)}, bf16[2,320,128]{2,1,0:T(8,128)(2,1)S(1)}, u32[]{:S(2)}, u32[]{:S(2)}) collective-permute-start(bf16[2,320,128]{2,1,0:T(8,128)(2,1)S(1)} %get-tuple-element.26), channel_id=1, source_target_pairs={{0,24},{8,16},{16,8},{24,0},{1,25},{9,17},{17,9},{25,1},{2,26},{10... | collective-permute-start | bytes 491528 | tf_op jit(solution)/shard_map/ppermute | solution.py:444
  7.1 5.0 %collective-permute-start.1 = (bf16[2,128,128]{2,1,0:T(8,128)(2,1)S(1)}, bf16[2,128,128]{2,1,0:T(8,128)(2,1)S(1)}, u32[]{:S(2)}, u32[]{:S(2)}) collective-permute-start(bf16[2,128,128]{2,1,0:T(8,128)(2,1)S(1)} %get-tuple-element.25), channel_id=1, source_target_pairs={{0,16},{8,24},{16,0},{24,8},{1,17},{9,25},{17,1},{25,9},{2,18},{10... | collective-permute-start | bytes 196616 | tf_op jit(solution)/shard_map/ppermute | solution.py:444
  20.0 6.8 %collective-permute-start.3 = (bf16[2,320,128]{2,1,0:T(8,128)(2,1)S(1)}, bf16[2,320,128]{2,1,0:T(8,128)(2,1)S(1)}, u32[]{:S(2)}, u32[]{:S(2)}) collective-permute-start(bf16[2,320,128]{2,1,0:T(8,128)(2,1)S(1)} %get-tuple-element.30), channel_id=1, source_target_pairs={{0,8},{8,0},{16,24},{24,16},{1,9},{9,1},{17,25},{25,17},{2,10},{10... | collective-permute-start | bytes 491528 | tf_op jit(solution)/shard_map/ppermute | solution.py:444
  21.5 7.2 %collective-permute-start.5 = (bf16[2,320,128]{2,1,0:T(8,128)(2,1)S(1)}, bf16[2,320,128]{2,1,0:T(8,128)(2,1)S(1)}, u32[]{:S(2)}, u32[]{:S(2)}) collective-permute-start(bf16[2,320,128]{2,1,0:T(8,128)(2,1)S(1)} %get-tuple-element.32), channel_id=1, source_target_pairs={{0,24},{8,16},{16,8},{24,0},{1,25},{9,17},{17,9},{25,1},{2,26},{10... | collective-permute-start | bytes 491528 | tf_op jit(solution)/shard_map/ppermute | solution.py:444
  21.7 4.9 %collective-permute-start.4 = (bf16[2,128,128]{2,1,0:T(8,128)(2,1)S(1)}, bf16[2,128,128]{2,1,0:T(8,128)(2,1)S(1)}, u32[]{:S(2)}, u32[]{:S(2)}) collective-permute-start(bf16[2,128,128]{2,1,0:T(8,128)(2,1)S(1)} %get-tuple-element.31), channel_id=1, source_target_pairs={{0,16},{8,24},{16,0},{24,8},{1,17},{9,25},{17,1},{25,9},{2,18},{10... | collective-permute-start | bytes 196616 | tf_op jit(solution)/shard_map/ppermute | solution.py:444
  28.9 4.7 %collective-permute-start.6 = (bf16[3,64,128]{2,1,0:T(8,128)(2,1)S(1)}, bf16[3,64,128]{2,1,0:T(8,128)(2,1)S(1)}, u32[]{:S(2)}, u32[]{:S(2)}) collective-permute-start(bf16[3,64,128]{2,1,0:T(8,128)(2,1)S(1)} %get-tuple-element.34), channel_id=1, source_target_pairs={{0,1},{1,0},{2,3},{3,2},{4,5},{5,4},{6,7},{7,6},{8,9},{9,8},{10,11... | collective-permute-start | bytes 147464 | tf_op jit(solution)/shard_map/ppermute | solution.py:444
  29.0 8.2 %collective-permute-start.7 = (bf16[3,64,128]{2,1,0:T(8,128)(2,1)S(1)}, bf16[3,64,128]{2,1,0:T(8,128)(2,1)S(1)}, u32[]{:S(2)}, u32[]{:S(2)}) collective-permute-start(bf16[3,64,128]{2,1,0:T(8,128)(2,1)S(1)} %get-tuple-element.35), channel_id=1, source_target_pairs={{0,2},{1,3},{2,0},{3,1},{4,6},{5,7},{6,4},{7,5},{8,10},{9,11},{10,... | collective-permute-start | bytes 147464 | tf_op jit(solution)/shard_map/ppermute | solution.py:444
  30.7 6.6 %collective-permute-start.8 = (bf16[3,64,128]{2,1,0:T(8,128)(2,1)S(1)}, bf16[3,64,128]{2,1,0:T(8,128)(2,1)S(1)}, u32[]{:S(2)}, u32[]{:S(2)}) collective-permute-start(bf16[3,64,128]{2,1,0:T(8,128)(2,1)S(1)} %get-tuple-element.36), channel_id=1, source_target_pairs={{0,3},{1,2},{2,1},{3,0},{4,7},{5,6},{6,5},{7,4},{8,11},{9,10},{10,... | collective-permute-start | bytes 147464 | tf_op jit(solution)/shard_map/ppermute | solution.py:444
  30.8 6.5 %collective-permute-start.9 = (bf16[3,64,128]{2,1,0:T(8,128)(2,1)S(1)}, bf16[3,64,128]{2,1,0:T(8,128)(2,1)S(1)}, u32[]{:S(2)}, u32[]{:S(2)}) collective-permute-start(bf16[3,64,128]{2,1,0:T(8,128)(2,1)S(1)} %get-tuple-element.37), channel_id=1, source_target_pairs={{0,4},{1,5},{2,6},{3,7},{4,0},{5,1},{6,2},{7,3},{8,12},{9,13},{10,... | collective-permute-start | bytes 147464 | tf_op jit(solution)/shard_map/ppermute | solution.py:444
  33.6 7.4 %collective-permute-start.10 = (bf16[3,64,128]{2,1,0:T(8,128)(2,1)S(1)}, bf16[3,64,128]{2,1,0:T(8,128)(2,1)S(1)}, u32[]{:S(2)}, u32[]{:S(2)}) collective-permute-start(bf16[3,64,128]{2,1,0:T(8,128)(2,1)S(1)} %get-tuple-element.38), channel_id=1, source_target_pairs={{0,5},{1,4},{2,7},{3,6},{4,1},{5,0},{6,3},{7,2},{8,13},{9,12},{10,... | collective-permute-start | bytes 147464 | tf_op jit(solution)/shard_map/ppermute | solution.py:444
  33.6 7.4 %collective-permute-start.11 = (bf16[3,64,128]{2,1,0:T(8,128)(2,1)S(1)}, bf16[3,64,128]{2,1,0:T(8,128)(2,1)S(1)}, u32[]{:S(2)}, u32[]{:S(2)}) collective-permute-start(bf16[3,64,128]{2,1,0:T(8,128)(2,1)S(1)} %get-tuple-element.39), channel_id=1, source_target_pairs={{0,6},{1,7},{2,4},{3,5},{4,2},{5,3},{6,0},{7,1},{8,14},{9,15},{10,... | collective-permute-start | bytes 147464 | tf_op jit(solution)/shard_map/ppermute | solution.py:444
  37.2 5.6 %collective-permute-start.12 = (bf16[3,64,128]{2,1,0:T(8,128)(2,1)S(1)}, bf16[3,64,128]{2,1,0:T(8,128)(2,1)S(1)}, u32[]{:S(2)}, u32[]{:S(2)}) collective-permute-start(bf16[3,64,128]{2,1,0:T(8,128)(2,1)S(1)} %get-tuple-element.40), channel_id=1, source_target_pairs={{0,7},{1,6},{2,5},{3,4},{4,3},{5,2},{6,1},{7,0},{8,15},{9,14},{10,... | collective-permute-start | bytes 147464 | tf_op jit(solution)/shard_map/ppermute | solution.py:444

commit v2 on v1

v2 whole, which is shorter than its diff:
```python
import functools

import jax
import jax.numpy as jnp
from jax import lax
from jax.experimental import pallas as pl
from jax.experimental.pallas import tpu as pltpu
from jax.sharding import PartitionSpec as P

BLOCK = 128
EDGE = BLOCK // 2
REST = 2 * BLOCK - EDGE
MASKED = -1e30
LOG2E = 1.4426950408889634
F32 = jnp.float32
BF16 = jnp.bfloat16
VMEM = pl.BlockSpec(memory_space=pltpu.VMEM)


def nt(a, b):
    return lax.dot_general(a, b, (((1,), (1,)), ((), ())), preferred_element_type=F32)


def nn(a, b):
    return lax.dot_general(a, b, (((1,), (0,)), ((), ())), preferred_element_type=F32)


def tn(a, b):
    return lax.dot_general(a, b, (((0,), (0,)), ((), ())), preferred_element_type=F32)


def pair_sum(x, scratch):
    rows = x.shape[0]
    scratch[:rows] = x
    return scratch[pl.ds(0, rows // 2, stride=2), :] + scratch[pl.ds(1, rows // 2, stride=2), :]


def coarse(x, scratch):
    return (pair_sum(x.astype(F32), scratch) * 0.5).astype(BF16)


def spread(x, scratch):
    rows = x.shape[0]
    scratch[pl.ds(0, rows, stride=2), :] = x
    scratch[pl.ds(1, rows, stride=2), :] = x
    return scratch[: 2 * rows]


def wide_distances(seq_count):
    return sorted({i ^ (i + 1) for i in range(seq_count - 1)})


def seq_order(seq_count):
    wides = wide_distances(seq_count)
    return wides[::-1] + [d for d in range(1, seq_count) if d not in wides]


def head_order(head_count):
    return [d for d in range(4, head_count)] + [d for d in (2, 3, 1) if d < head_count]


def prep_kernel(seq_count, *refs):
    sources, refs = refs[:4], refs[4:]
    held, refs = refs[0], refs[1:]
    sends, scratches, sems = refs[: seq_count - 1], refs[seq_count - 1 : -1], refs[-1]
    sends = dict(zip(seq_order(seq_count), sends))
    seq_index = lax.axis_index("seq")
    wides = wide_distances(seq_count)
    rows = held.shape[1]
    copies = [
        pltpu.make_async_copy(source, held.at[i], sems.at[i]) for i, source in enumerate(sources)
    ]
    for i in (1, 2, 0, 3):
        copies[i].start()
    for i in range(2):
        copies[1 + i].wait()
        ref = held.at[1 + i]
        level_1 = coarse(ref[...], scratches[2 * i])
        level_2 = coarse(level_1, scratches[2 * i + 1])
        for d in range(1, seq_count):
            out = sends[d]
            partner = seq_index ^ d
            if d not in wides:
                out[i] = level_2
                continue

            @pl.when(partner == seq_index + 1)
            def _():
                out[i, :BLOCK] = ref[rows - BLOCK :]
                out[i, BLOCK:] = level_1[:REST]

            @pl.when(partner == seq_index - 1)
            def _():
                out[i, :BLOCK] = ref[:BLOCK]
                out[i, BLOCK:] = level_1[EDGE:]

            @pl.when((partner != seq_index + 1) & (partner != seq_index - 1))
            def _():
                out[i, :BLOCK] = level_2
                out[i, BLOCK:] = level_1[:REST]

    copies[0].wait()
    copies[3].wait()


def slots_of(block, block_count):
    parent, odd = block // 2, block % 2
    if block_count == 4:
        first = parent == 0
        return [
            (jnp.where(first, 3, 0), None),
            (jnp.where(first, 2, 1), jnp.where(first, odd == 0, odd == 1)),
        ]
    near = jnp.where(odd == 0, 2 * parent + 2, 2 * parent - 1)
    raw = [2 * parent - 2, near, 2 * parent + 3]
    return [(jnp.clip(j, 0, block_count - 1), (j >= 0) & (j < block_count)) for j in raw]


def across(x, width):
    return jnp.concatenate([x] * (width // x.shape[1]), axis=1)


def lanes(column):
    return jnp.broadcast_to(column, (column.shape[0], BLOCK))


def row_max(x):
    return lanes(jnp.max(x, axis=-1, keepdims=True))


def row_sum(x):
    return lanes(jnp.sum(x, axis=-1, keepdims=True))


def total_of(parts):
    return functools.reduce(jnp.add, parts)


def rows_of(block, count=1):
    return slice(block * BLOCK, (block + count) * BLOCK)


def own_window(a, blocks):
    return max(a - 1, 0), min(a + 2, blocks)


def fine_kernel(held, stats, *refs):
    levels = len(refs) // 2
    blocks, width = held.shape[1] // BLOCK, held.shape[2]
    factor = width ** (-0.5) * LOG2E
    for a in range(blocks):
        lo, hi = own_window(a, blocks)
        window = rows_of(lo, hi - lo)
        scores = nt(held[0, rows_of(a)], held[1, window]) * factor
        peak = row_max(scores)
        exps = jnp.exp2(scores - across(peak, scores.shape[1]))
        stats[0, rows_of(a)] = peak
        stats[1, rows_of(a)] = row_sum(exps)
        stats[2, rows_of(a)] = nn(exps.astype(BF16), held[2, window])
    query = held[0]
    for level in range(levels):
        query = coarse(query, refs[levels + level])
        refs[level][...] = query


def main_kernel(seq_count, top_level, *refs):
    refs = list(refs)

    def take(count):
        taken = refs[:count]
        del refs[:count]
        return taken

    held, stats = take(2)
    query_refs = take(top_level)
    received = dict(zip(seq_order(seq_count), take(seq_count - 1)))
    (attended_ref,) = take(1)
    sends = dict(zip(seq_order(seq_count), take(seq_count - 1)))
    back, partial_ref = take(2)
    halo, near = take(2)
    panels = take(top_level - 1)
    panel_grads = take(top_level - 1)
    pools = refs

    def pool():
        return pools.pop(0)

    seq_index = lax.axis_index("seq")
    wides = wide_distances(seq_count)
    rows, width = held.shape[1:]
    blocks = rows // BLOCK
    scale = width ** (-0.5)
    factor = scale * LOG2E
    has_prev, has_next = seq_index > 0, seq_index < seq_count - 1

    for panel in panels:
        panel[...] = jnp.zeros(panel.shape, BF16)

    @pl.when(seq_index == 0)
    def _():
        halo[:, :BLOCK] = jnp.zeros((2, BLOCK, width), BF16)
        near[:, : 2 * BLOCK] = jnp.zeros((2, 2 * BLOCK, width), BF16)

    @pl.when(seq_index == seq_count - 1)
    def _():
        halo[:, BLOCK:] = jnp.zeros((2, BLOCK, width), BF16)
        near[:, 2 * BLOCK :] = jnp.zeros((2, 2 * BLOCK, width), BF16)

    halo_scratch = pool()
    for d in range(1, seq_count):
        got = received[d]
        partner = seq_index ^ d
        at = pl.ds(pl.multiple_of(partner * BLOCK, BLOCK), BLOCK)
        if d not in wides:
            for i in range(2):
                panels[0][i, at] = got[i]
            continue

        @pl.when(partner == seq_index - 1)
        def _():
            for i in range(2):
                halo[i, :BLOCK] = got[i, :BLOCK]
                near[i, :REST] = got[i, BLOCK:]
                near[i, REST : 2 * BLOCK] = coarse(got[i, :BLOCK], halo_scratch)

        @pl.when(partner == seq_index + 1)
        def _():
            for i in range(2):
                halo[i, BLOCK:] = got[i, :BLOCK]
                near[i, 2 * BLOCK : 2 * BLOCK + EDGE] = coarse(got[i, :BLOCK], halo_scratch)
                near[i, 2 * BLOCK + EDGE :] = got[i, BLOCK:]

        @pl.when((partner != seq_index + 1) & (partner != seq_index - 1))
        def _():
            for i in range(2):
                panels[0][i, at] = got[i, :BLOCK]

    panel_scratch = pool()
    for level in range(3, top_level + 1):
        for i in range(2):
            panels[level - 2][i] = coarse(panels[level - 3][i], panel_scratch)

    def window(ref, lo, hi, valid):
        return ref[0, rows_of(lo, hi - lo)], ref[1, rows_of(lo, hi - lo)], valid, (lo, hi)

    level_pieces = [
        [[window(halo, 0, 1, has_prev)], [window(halo, 1, 2, has_next)]],
        [
            [window(near, 0, 1, has_prev), window(near, 2, 4, has_next)],
            [window(near, 0, 2, has_prev), window(near, 3, 4, has_next)],
        ],
    ]
    for level in range(2, top_level + 1):
        pieces = []
        for index, valid in slots_of(seq_index >> (level - 2), seq_count >> (level - 2)):
            at = pl.ds(pl.multiple_of(index * BLOCK, BLOCK), BLOCK)
            panel = panels[level - 2]
            pieces.append((panel[0, at], panel[1, at], valid, at))
        level_pieces.append([pieces])
    level_queries = [[held[0, rows_of(0)], held[0, rows_of(blocks - 1)]]]
    for level in range(1, top_level + 1):
        query = query_refs[level - 1][...]
        step = query.shape[0] // len(level_pieces[level])
        level_queries.append(
            [query[a * step : (a + 1) * step] for a in range(len(level_pieces[level]))]
        )

    def unit(query, pieces, before=None):
        scores = []
        for key, _, valid, _ in pieces:
            score = nt(query, key) * factor
            scores.append(score if valid is None else jnp.where(valid, score, MASKED))
        peak = functools.reduce(jnp.maximum, [row_max(score) for score in scores])
        if before is not None:
            peak = jnp.maximum(peak, before[0])
        exps = [jnp.exp2(score - across(peak, score.shape[1])) for score in scores]
        rounded = [e.astype(BF16) for e in exps]
        total = total_of([row_sum(e) for e in exps])
        sums = total_of([nn(r, piece[1]) for r, piece in zip(rounded, pieces)])
        if before is not None:
            keep = jnp.exp2(before[0] - peak)
            total, sums = total + keep * before[1], sums + keep * before[2]
        return peak, total, sums, exps, rounded

    def before_of(block):
        return [stats[w, rows_of(block)] for w in range(3)]

    level_units = [
        [
            unit(query, pieces, before_of(block))
            for query, pieces, block in zip(level_queries[0], level_pieces[0], (0, blocks - 1))
        ]
    ]
    for level in range(1, top_level + 1):
        level_units.append(
            [unit(q, pieces) for q, pieces in zip(level_queries[level], level_pieces[level])]
        )

    def stacked(level, which):
        units = [u[which] for u in level_units[level]]
        if level == 0:
            units = [units[0], stats[which, rows_of(1, blocks - 2)], units[1]]
        return jnp.concatenate(units, axis=0)

    run = [stacked(top_level, w) for w in range(3)]
    own_factors, run_factors = [None] * top_level, [None] * top_level
    for level in range(top_level - 1, -1, -1):
        up_peak, up_total, up_sums = [spread(x, pool()) for x in run]
        peak, total, sums = [stacked(level, w) for w in range(3)]
        both = jnp.maximum(peak, up_peak)
        own = jnp.exp2(peak - both)
        up = 2.0 * jnp.exp2(up_peak - both)
        own_factors[level], run_factors[level] = own, up
        run = [both, own * total + up * up_total, own * sums + up * up_sums]

    inverse = 1.0 / run[1]
    attended = run[2] * inverse
    attended_ref[...] = attended.astype(BF16)

    cot = held[3].astype(F32)
    grad, shift = cot * inverse, row_sum(cot * attended) * inverse
    level_grads = []
    for level in range(top_level):
        level_grads.append((own_factors[level] * grad, own_factors[level] * shift))
        grad = pair_sum(run_factors[level] * grad, pool())
        shift = pair_sum(run_factors[level] * shift, pool())
    level_grads.append((grad, shift))
    back[0] = stacked(0, 0)
    back[1], back[2] = level_grads[0]

    for panel_grad in panel_grads:
        panel_grad[...] = jnp.zeros(panel_grad.shape, F32)

    grad_queries = []
    parts_of = [[[[] for _ in range(4)] for _ in range(2)] for _ in range(2)]
    for level in range(top_level, -1, -1):
        grad, shift = level_grads[level]
        step = level_queries[level][0].shape[0]
        level_parts = []
        for a, (query, pieces) in enumerate(zip(level_queries[level], level_pieces[level])):
            at = a if level > 0 else a * (blocks - 1)
            cut = slice(at * step, (at + 1) * step)
            grad_rounded = grad[cut].astype(BF16)
            grad_scaled = (grad[cut] * scale).astype(BF16)
            shift_scaled = shift[cut] * scale
            exps, rounded = level_units[level][a][3:]
            query_parts = []
            for piece, e, r in zip(pieces, exps, rounded):
                key, value, _, where = piece
                score_grad = nt(grad_scaled, value) - across(shift_scaled, e.shape[1])
                score_grad = (e * score_grad).astype(BF16)
                query_parts.append(nn(score_grad, key))
                outs = tn(score_grad, query), tn(r, grad_rounded)
                for i in range(2):
                    if level >= 2:
                        panel_grads[level - 2][i, where] += outs[i]
                        continue
                    lo, hi = where
                    for b in range(lo, hi):
                        parts_of[level][i][b].append(outs[i][rows_of(b - lo)])
            level_parts.append(total_of(query_parts))
        grad_queries.append(level_parts)

    run_grad = grad_queries[0][0]
    for level_parts in grad_queries[1:-1]:
        run_grad = jnp.concatenate(level_parts, axis=0) + 0.5 * spread(run_grad, pool())
    partial_ref[...] = 0.5 * spread(run_grad, pool())
    for a, block in enumerate((0, blocks - 1)):
        partial_ref[rows_of(block)] += grad_queries[-1][a]

    for level in range(top_level, 2, -1):
        for i in range(2):
            panel_grads[level - 3][i] += 0.5 * spread(panel_grads[level - 2][i], panel_scratch)

    near_grads = [[total_of(p) for p in parts_of[1][i]] for i in range(2)]
    halo_grads = [[total_of(p) for p in parts_of[0][i][:2]] for i in range(2)]
    to_prev = [halo_grads[i][0] + 0.5 * spread(near_grads[i][1][EDGE:], pool()) for i in range(2)]
    to_next = [halo_grads[i][1] + 0.5 * spread(near_grads[i][2][:EDGE], pool()) for i in range(2)]
    for d in range(1, seq_count):
        out = sends[d]
        partner = seq_index ^ d
        at = pl.ds(pl.multiple_of(partner * BLOCK, BLOCK), BLOCK)
        if d not in wides:
            for i in range(2):
                out[i] = panel_grads[0][i, at].astype(BF16)
            continue

        @pl.when(partner == seq_index - 1)
        def _():
            for i in range(2):
                out[i, :BLOCK] = to_prev[i].astype(BF16)
                out[i, BLOCK : 2 * BLOCK] = near_grads[i][0].astype(BF16)
                out[i, 2 * BLOCK :] = near_grads[i][1][:EDGE].astype(BF16)

        @pl.when(partner == seq_index + 1)
        def _():
            for i in range(2):
                out[i, :BLOCK] = to_next[i].astype(BF16)
                out[i, BLOCK : BLOCK + EDGE] = near_grads[i][2][EDGE:].astype(BF16)
                out[i, BLOCK + EDGE :] = near_grads[i][3].astype(BF16)

        @pl.when((partner != seq_index + 1) & (partner != seq_index - 1))
        def _():
            for i in range(2):
                out[i, :BLOCK] = panel_grads[0][i, at].astype(BF16)
                out[i, BLOCK:] = jnp.zeros((REST, width), BF16)


def local_kernel(held, back, partial_ref, grad_query_ref, local_ref):
    blocks, width = held.shape[1] // BLOCK, held.shape[2]
    scale = width ** (-0.5)
    factor = scale * LOG2E
    parts = [[[] for _ in range(blocks)] for _ in range(2)]
    for a in range(blocks):
        lo, hi = own_window(a, blocks)
        window = rows_of(lo, hi - lo)
        query, key, value = held[0, rows_of(a)], held[1, window], held[2, window]
        peak, grad, shift = [back[w, rows_of(a)] for w in range(3)]
        wide = key.shape[0]
        exps = jnp.exp2(nt(query, key) * factor - across(peak, wide))
        score_grad = nt((grad * scale).astype(BF16), value) - across(shift * scale, wide)
        score_grad = (exps * score_grad).astype(BF16)
        grad_query_ref[rows_of(a)] = (nn(score_grad, key) + partial_ref[rows_of(a)]).astype(BF16)
        outs = tn(score_grad, query), tn(exps.astype(BF16), grad.astype(BF16))
        for i in range(2):
            for b in range(lo, hi):
                parts[i][b].append(outs[i][rows_of(b - lo)])
    for i in range(2):
        for b in range(blocks):
            local_ref[i, rows_of(b)] = total_of(parts[i][b])


def combine_kernel(seq_count, head_count, grad_query_ref, local_ref, *refs):
    received, refs = refs[: seq_count - 1], refs[seq_count - 1 :]
    received = dict(zip(seq_order(seq_count), received))
    outs, refs = refs[:head_count], refs[head_count:]
    outs = dict(zip([0] + head_order(head_count), outs))
    total, level_1, level_2 = refs
    seq_index, head_index = lax.axis_index("seq"), lax.axis_index("head")
    wides = wide_distances(seq_count)
    rows, width = local_ref.shape[1:]
    share = rows // head_count

    level_1[...] = jnp.zeros(level_1.shape, F32)
    level_2[...] = jnp.zeros(level_2.shape, F32)
    for i in range(2):
        total[i] = local_ref[i]
    for d in range(1, seq_count):
        got = received[d]
        partner = seq_index ^ d
        if d not in wides:
            for i in range(2):
                level_2[i] += got[i].astype(F32)
            continue

        @pl.when(partner == seq_index - 1)
        def _():
            for i in range(2):
                total[i, :BLOCK] += got[i, :BLOCK].astype(F32)
                level_1[i, EDGE:] += got[i, BLOCK:].astype(F32)

        @pl.when(partner == seq_index + 1)
        def _():
            for i in range(2):
                total[i, rows - BLOCK :] += got[i, :BLOCK].astype(F32)
                level_1[i, :REST] += got[i, BLOCK:].astype(F32)

        @pl.when((partner != seq_index + 1) & (partner != seq_index - 1))
        def _():
            for i in range(2):
                level_2[i] += got[i, :BLOCK].astype(F32)

    for i in range(2):
        half = level_2[i] * 0.5
        for phase in range(2):
            level_1[i, pl.ds(phase, half.shape[0], stride=2), :] += half
        half = level_1[i] * 0.5
        for phase in range(2):
            total[i, pl.ds(phase, half.shape[0], stride=2), :] += half
    for d in range(head_count):
        at = pl.ds(pl.multiple_of((head_index ^ d) * share, share), share)
        outs[d][0] = grad_query_ref[at, :]
        outs[d][1] = total[0, at].astype(BF16)
        outs[d][2] = total[1, at].astype(BF16)


def place_kernel(head_count, *refs):
    parts, outs = refs[:head_count], refs[head_count:]
    parts = dict(zip([0] + head_order(head_count), parts))
    head_index = lax.axis_index("head")
    width = parts[0].shape[-1]
    for d in range(head_count):
        at = pl.ds(pl.multiple_of((head_index ^ d) * width, width), width)
        for i in range(3):
            outs[i][:, at] = parts[d][i]


def call(kernel, outs, scratch, args, space=pltpu.VMEM, flops=0):
    return pl.pallas_call(
        kernel,
        out_shape=outs,
        in_specs=[pl.BlockSpec(memory_space=space)] * len(args),
        out_specs=[VMEM] * len(outs),
        scratch_shapes=scratch,
        compiler_params=pltpu.CompilerParams(vmem_limit_bytes=48 * 2**20),
        cost_estimate=pl.CostEstimate(flops=flops, bytes_accessed=2**20, transcendentals=0),
    )(*args)


def swap_all(arrays, axis, distances):
    size = lax.axis_size(axis)
    return [
        lax.ppermute(x, axis, [(i, i ^ d) for i in range(size)]) for x, d in zip(arrays, distances)
    ]


def per_device(queries, keys, values, grad_out):
    seq_count, head_count = lax.axis_size("seq"), lax.axis_size("head")
    rows, width = queries.shape
    assert rows == 4 * BLOCK and width == BLOCK
    fine_blocks = rows * seq_count // BLOCK
    top_level = (fine_blocks // 4).bit_length() - 1
    wides = wide_distances(seq_count)
    distances = seq_order(seq_count)

    def shape(*dims, dtype=BF16):
        return jax.ShapeDtypeStruct(dims, dtype)

    def f32(*dims):
        return pltpu.VMEM(dims, F32)

    payloads = [shape(2, BLOCK + REST if d in wides else BLOCK, width) for d in distances]
    arguments = [
        pltpu.with_memory_space_constraint(x, pltpu.HBM) for x in (queries, keys, values, grad_out)
    ]
    held, *sends = call(
        functools.partial(prep_kernel, seq_count),
        [shape(4, rows, width)] + payloads,
        [f32(rows, width), f32(rows // 2, width)] * 2 + [pltpu.SemaphoreType.DMA((4,))],
        arguments,
        pltpu.HBM,
    )
    received = swap_all(sends, "seq", distances)

    unit_flops = 2 * BLOCK * BLOCK * width
    stats, *level_queries = call(
        fine_kernel,
        [shape(3, rows, width, dtype=F32)]
        + [shape(rows >> level, width) for level in range(1, top_level + 1)],
        [f32(rows >> level, width) for level in range(top_level)],
        (held,),
        flops=20 * unit_flops,
    )

    panel_rows = [(seq_count >> (level - 2)) * BLOCK for level in range(2, top_level + 1)]
    pools = [f32(BLOCK, width), f32(max(seq_count * BLOCK, rows), width)]
    for level in range(top_level - 1, -1, -1):
        pools += [f32(rows >> level, width)] * 3
    for level in range(top_level):
        pools += [f32(rows >> level, width)] * 2
    for level in range(top_level - 1, -1, -1):
        pools += [f32(rows >> level, width)]
    pools += [f32(BLOCK, width)] * 4
    main = call(
        functools.partial(main_kernel, seq_count, top_level),
        [shape(rows, width)]
        + payloads
        + [shape(3, rows, width, dtype=F32), shape(rows, width, dtype=F32)],
        [pltpu.VMEM((2, 2 * BLOCK, width), BF16), pltpu.VMEM((2, 4 * BLOCK, width), BF16)]
        + [pltpu.VMEM((2, r, width), BF16) for r in panel_rows]
        + [f32(2, r, width) for r in panel_rows]
        + pools,
        (held, stats, *level_queries, *received),
        flops=70 * unit_flops,
    )
    attended, sends, back, partial = main[0], main[1:seq_count], main[-2], main[-1]
    returned = swap_all(sends, "seq", distances)

    grad_query, local = call(
        local_kernel,
        [shape(rows, width), shape(2, rows, width, dtype=F32)],
        [],
        (held, back, partial),
        flops=50 * unit_flops,
    )

    share = rows // head_count
    parts = call(
        functools.partial(combine_kernel, seq_count, head_count),
        [shape(3, share, width)] * head_count,
        [f32(2, rows, width), f32(2, rows // 2, width), f32(2, rows // 4, width)],
        (grad_query, local, *returned),
    )
    parts = [parts[0]] + swap_all(parts[1:], "head", head_order(head_count))
    grads = call(
        functools.partial(place_kernel, head_count),
        [shape(share, head_count * width)] * 3,
        [],
        parts,
    )
    return (attended, *grads)


def solution(mesh):
    return jax.shard_map(
        per_device,
        mesh=mesh,
        in_specs=(P("seq", "head"),) * 4,
        out_specs=(P("seq", "head"),) + (P(("seq", "head"), None),) * 3,
        check_vma=False,
    )
```

time: 43.8 us -> 39.7 us (0.906)
  waiting for transfers between devices: 18 us -> 13.9 us
  Pallas kernels: 6.67 us -> 8.53 us
  local copies, waits for them, and re-layouts: 1.81 us -> 0 us
    ppermute x13, waiting for transfers between devices: 18 us -> 13.9 us  [swap_all(): lax.ppermute(x, axis, [(i, i ^ d) for i in range(size)])]
    pallas_call x4 -> x6, Pallas kernels: 6.67 us -> 8.53 us  [call(): pl.pallas_call(kernel, out_shape=outs, in_specs=[pl.BlockSpec(memory_spac...]
    unnamed x8 -> x0, local copies, waits for them, and re-layouts: 1.81 us -> none
  transfers between devices with their start and end apart: 13 -> 13, of which waited for: 7 -> 9; matrix products, arithmetic and copies ran while one was open for 0% -> 0% of each run, Pallas kernels for 0% -> 6%
where the time goes in v2:
time: 39.7 us; the launch traced here: 39.5 us
  starting transfers between devices  16.5 us (42%)
  waiting for transfers between devices  13.9 us (35%)
  Pallas kernels  8.53 us (21%)
  between operations  0.66 us (2%)
    ppermute x13, starting transfers between devices, swap_all(): lax.ppermute(x, axis, [(i, i ^ d) for i in range(size)])  16.5 us
    ppermute x13, waiting for transfers between devices, swap_all(): lax.ppermute(x, axis, [(i, i ^ d) for i in range(size)])  13.9 us
    pallas_call x6, Pallas kernels, call(): pl.pallas_call(kernel, out_shape=outs, in_specs=[pl.BlockSpec(memory_spac...  8.53 us
  transfers between devices with their start and end apart: 13, of which 9 were waited for; matrix products, arithmetic and copies ran while one was open for 0% of the time, Pallas kernels for 6%

profile of v2, /device:TPU:0, one launch (start us, length us, event | category | flops | bytes accessed | tf_op | source)
XLA Modules:
  0.0 39.5 jit_solution(10307365102620470138)
XLA Ops:
  0.6 1.1 %shard_map.75 = (bf16[4,512,128]{2,1,0:T(8,128)(2,1)S(1)}, bf16[2,320,128]{2,1,0:T(8,128)(2,1)S(1)}, bf16[2,320,128]{2,1,0:T(8,128)(2,1)S(1)}, bf16[2,128,128]{2,1,0:T(8,128)(2,1)S(1)}) custom-call(bf16[512,128]{1,0:T(8,128)(2,1)} %refs_0_.1, bf16[512,128]{1,0:T(8,128)(2,1)} %refs_1_.1, bf16[512,128]{1,0:T(8,128)(2,1)} %refs_2_.1, bf16[512,128]{1,0:T(8,128)(2,1)} %refs_3_.1), custom_call_target="tpu_custom_call" | custom-call | bytes 1048576 | tf_op jit(solution)/shard_map/pallas_call | solution.py:499
  1.8 4.0 %collective-permute-start = (bf16[2,320,128]{2,1,0:T(8,128)(2,1)S(1)}, bf16[2,320,128]{2,1,0:T(8,128)(2,1)S(1)}, u32[]{:S(2)}, u32[]{:S(2)}) collective-permute-start(bf16[2,320,128]{2,1,0:T(8,128)(2,1)S(1)} %get-tuple-element.34), channel_id=1, source_target_pairs={{0,24},{8,16},{16,8},{24,0},{1,25},{9,17},{17,9},{25,1},{2,26},{10... | collective-permute-start | bytes 491528 | tf_op jit(solution)/shard_map/ppermute | solution.py:513
  5.7 0.5 %collective-permute-start.1 = (bf16[2,320,128]{2,1,0:T(8,128)(2,1)S(1)}, bf16[2,320,128]{2,1,0:T(8,128)(2,1)S(1)}, u32[]{:S(2)}, u32[]{:S(2)}) collective-permute-start(bf16[2,320,128]{2,1,0:T(8,128)(2,1)S(1)} %get-tuple-element.35), channel_id=1, source_target_pairs={{0,8},{8,0},{16,24},{24,16},{1,9},{9,1},{17,25},{25,17},{2,10},{10... | collective-permute-start | bytes 491528 | tf_op jit(solution)/shard_map/ppermute | solution.py:513
  6.4 1.1 %shard_map.76 = (f32[3,512,128]{2,1,0:T(8,128)S(1)}, bf16[256,128]{1,0:T(8,128)(2,1)S(1)}, bf16[128,128]{1,0:T(8,128)(2,1)S(1)}) custom-call(bf16[4,512,128]{2,1,0:T(8,128)(2,1)S(1)} %get-tuple-element.30.held.refs_0_), custom_call_target="tpu_custom_call" | custom-call | flops 83886080 | bytes 1048576 | tf_op jit(solution)/shard_map/pallas_call | solution.py:499
  7.5 3.8 %collective-permute-done.2.refs_6_ = bf16[2,128,128]{2,1,0:T(8,128)(2,1)S(1)} collective-permute-done((bf16[2,128,128]{2,1,0:T(8,128)(2,1)S(1)}, bf16[2,128,128]{2,1,0:T(8,128)(2,1)S(1)}, u32[]{:S(2)}, u32[]{:S(2)}) %collective-permute-start.2) | collective-permute-done | bytes 65568 | tf_op jit(solution)/shard_map/ppermute | solution.py:513
  11.3 2.4 %collective-permute-done.1.refs_5_ = bf16[2,320,128]{2,1,0:T(8,128)(2,1)S(1)} collective-permute-done((bf16[2,320,128]{2,1,0:T(8,128)(2,1)S(1)}, bf16[2,320,128]{2,1,0:T(8,128)(2,1)S(1)}, u32[]{:S(2)}, u32[]{:S(2)}) %collective-permute-start.1) | collective-permute-done | bytes 163872 | tf_op jit(solution)/shard_map/ppermute | solution.py:513
  13.7 4.0 %shard_map.77 = (bf16[512,128]{1,0:T(8,128)(2,1)}, bf16[2,320,128]{2,1,0:T(8,128)(2,1)S(1)}, bf16[2,320,128]{2,1,0:T(8,128)(2,1)S(1)}, bf16[2,128,128]{2,1,0:T(8...) custom-call(bf16[4,512,128]{2,1,0:T(8,128)(2,1)S(1)} %get-tuple-element.30.held.refs_0_, ...), custom_call_target="tpu_custom_call" | custom-call | flops 293601280 | bytes 1048576 | tf_op jit(solution)/shard_map/pallas_call | solution.py:499
  17.7 1.4 %collective-permute-start.3 = (bf16[2,320,128]{2,1,0:T(8,128)(2,1)S(1)}, bf16[2,320,128]{2,1,0:T(8,128)(2,1)S(1)}, u32[]{:S(2)}, u32[]{:S(2)}) collective-permute-start(bf16[2,320,128]{2,1,0:T(8,128)(2,1)S(1)} %get-tuple-element.42), channel_id=1, source_target_pairs={{0,24},{8,16},{16,8},{24,0},{1,25},{9,17},{17,9},{25,1},{2,26},{10... | collective-permute-start | bytes 491528 | tf_op jit(solution)/shard_map/ppermute | solution.py:513
  19.1 0.3 collective-permute-start.4
  19.5 1.8 %collective-permute-start.5 = (bf16[2,128,128]{2,1,0:T(8,128)(2,1)S(1)}, bf16[2,128,128]{2,1,0:T(8,128)(2,1)S(1)}, u32[]{:S(2)}, u32[]{:S(2)}) collective-permute-start(bf16[2,128,128]{2,1,0:T(8,128)(2,1)S(1)} %get-tuple-element.44), channel_id=1, source_target_pairs={{0,16},{8,24},{16,0},{24,8},{1,17},{9,25},{17,1},{25,9},{2,18},{10... | collective-permute-start | bytes 196616 | tf_op jit(solution)/shard_map/ppermute | solution.py:513
  21.2 1.2 %shard_map.78 = (bf16[512,128]{1,0:T(8,128)(2,1)S(1)}, f32[2,512,128]{2,1,0:T(8,128)S(1)}) custom-call(bf16[4,512,128]{2,1,0:T(8,128)(2,1)S(1)} %get-tuple-element.30.held.refs_0_, f32[3,512,128]{2,1,0:T(8,128)S(1)} %get-tuple-element.38.back, f32[512,128]{1,0:T(8,128)S(1)} %get-tuple-element.39.partial_ref), custom_call_target="tpu_custom_call" | custom-call | flops 209715200 | bytes 1048576 | tf_op jit(solution)/shard_map/pallas_call | solution.py:499
  22.4 2.0 %collective-permute-done.5.refs_2_ = bf16[2,128,128]{2,1,0:T(8,128)(2,1)S(1)} collective-permute-done((bf16[2,128,128]{2,1,0:T(8,128)(2,1)S(1)}, bf16[2,128,128]{2,1,0:T(8,128)(2,1)S(1)}, u32[]{:S(2)}, u32[]{:S(2)}) %collective-permute-start.5) | collective-permute-done | bytes 65568 | tf_op jit(solution)/shard_map/ppermute | solution.py:513
  24.4 1.0 %collective-permute-done.3.refs_0_ = bf16[2,320,128]{2,1,0:T(8,128)(2,1)S(1)} collective-permute-done((bf16[2,320,128]{2,1,0:T(8,128)(2,1)S(1)}, bf16[2,320,128]{2,1,0:T(8,128)(2,1)S(1)}, u32[]{:S(2)}, u32[]{:S(2)}) %collective-permute-start.3) | collective-permute-done | bytes 163872 | tf_op jit(solution)/shard_map/ppermute | solution.py:513
  25.5 0.9 %collective-permute-done.4.refs_1_ = bf16[2,320,128]{2,1,0:T(8,128)(2,1)S(1)} collective-permute-done((bf16[2,320,128]{2,1,0:T(8,128)(2,1)S(1)}, bf16[2,320,128]{2,1,0:T(8,128)(2,1)S(1)}, u32[]{:S(2)}, u32[]{:S(2)}) %collective-permute-start.4) | collective-permute-done | bytes 163872 | tf_op jit(solution)/shard_map/ppermute | solution.py:513
  26.6 2.5 %collective-permute-start.6 = (bf16[3,64,128]{2,1,0:T(8,128)(2,1)S(1)}, bf16[3,64,128]{2,1,0:T(8,128)(2,1)S(1)}, u32[]{:S(2)}, u32[]{:S(2)}) collective-permute-start(bf16[3,64,128]{2,1,0:T(8,128)(2,1)S(1)} %get-tuple-element.46), channel_id=1, source_target_pairs={{0,4},{1,5},{2,6},{3,7},{4,0},{5,1},{6,2},{7,3},{8,12},{9,13},{10,... | collective-permute-start | bytes 147464 | tf_op jit(solution)/shard_map/ppermute | solution.py:513
  29.1 1.3 %collective-permute-start.8 = (bf16[3,64,128]{2,1,0:T(8,128)(2,1)S(1)}, bf16[3,64,128]{2,1,0:T(8,128)(2,1)S(1)}, u32[]{:S(2)}, u32[]{:S(2)}) collective-permute-start(bf16[3,64,128]{2,1,0:T(8,128)(2,1)S(1)} %get-tuple-element.48), channel_id=1, source_target_pairs={{0,6},{1,7},{2,4},{3,5},{4,2},{5,3},{6,0},{7,1},{8,14},{9,15},{10,... | collective-permute-start | bytes 147464 | tf_op jit(solution)/shard_map/ppermute | solution.py:513
  30.5 2.4 %collective-permute-start.9 = (bf16[3,64,128]{2,1,0:T(8,128)(2,1)S(1)}, bf16[3,64,128]{2,1,0:T(8,128)(2,1)S(1)}, u32[]{:S(2)}, u32[]{:S(2)}) collective-permute-start(bf16[3,64,128]{2,1,0:T(8,128)(2,1)S(1)} %get-tuple-element.49), channel_id=1, source_target_pairs={{0,7},{1,6},{2,5},{3,4},{4,3},{5,2},{6,1},{7,0},{8,15},{9,14},{10,... | collective-permute-start | bytes 147464 | tf_op jit(solution)/shard_map/ppermute | solution.py:513
  32.9 1.6 %collective-permute-start.11 = (bf16[3,64,128]{2,1,0:T(8,128)(2,1)S(1)}, bf16[3,64,128]{2,1,0:T(8,128)(2,1)S(1)}, u32[]{:S(2)}, u32[]{:S(2)}) collective-permute-start(bf16[3,64,128]{2,1,0:T(8,128)(2,1)S(1)} %get-tuple-element.51), channel_id=1, source_target_pairs={{0,3},{1,2},{2,1},{3,0},{4,7},{5,6},{6,5},{7,4},{8,11},{9,10},{10,... | collective-permute-start | bytes 147464 | tf_op jit(solution)/shard_map/ppermute | solution.py:513
  34.4 0.6 %collective-permute-start.12 = (bf16[3,64,128]{2,1,0:T(8,128)(2,1)S(1)}, bf16[3,64,128]{2,1,0:T(8,128)(2,1)S(1)}, u32[]{:S(2)}, u32[]{:S(2)}) collective-permute-start(bf16[3,64,128]{2,1,0:T(8,128)(2,1)S(1)} %get-tuple-element.52), channel_id=1, source_target_pairs={{0,1},{1,0},{2,3},{3,2},{4,5},{5,4},{6,7},{7,6},{8,9},{9,8},{10,11... | collective-permute-start | bytes 147464 | tf_op jit(solution)/shard_map/ppermute | solution.py:513
  35.0 0.6 %collective-permute-done.8.refs_3_ = bf16[3,64,128]{2,1,0:T(8,128)(2,1)S(1)} collective-permute-done((bf16[3,64,128]{2,1,0:T(8,128)(2,1)S(1)}, bf16[3,64,128]{2,1,0:T(8,128)(2,1)S(1)}, u32[]{:S(2)}, u32[]{:S(2)}) %collective-permute-start.8) | collective-permute-done | bytes 49184 | tf_op jit(solution)/shard_map/ppermute | solution.py:513
  35.6 0.7 %collective-permute-done.9.refs_4_ = bf16[3,64,128]{2,1,0:T(8,128)(2,1)S(1)} collective-permute-done((bf16[3,64,128]{2,1,0:T(8,128)(2,1)S(1)}, bf16[3,64,128]{2,1,0:T(8,128)(2,1)S(1)}, u32[]{:S(2)}, u32[]{:S(2)}) %collective-permute-start.9) | collective-permute-done | bytes 49184 | tf_op jit(solution)/shard_map/ppermute | solution.py:513
  36.3 1.2 %collective-permute-done.10.refs_5_ = bf16[3,64,128]{2,1,0:T(8,128)(2,1)S(1)} collective-permute-done((bf16[3,64,128]{2,1,0:T(8,128)(2,1)S(1)}, bf16[3,64,128]{2,1,0:T(8,128)(2,1)S(1)}, u32[]{:S(2)}, u32[]{:S(2)}) %collective-permute-start.10) | collective-permute-done | bytes 49184 | tf_op jit(solution)/shard_map/ppermute | solution.py:513
  37.5 1.2 %collective-permute-done.11.refs_6_ = bf16[3,64,128]{2,1,0:T(8,128)(2,1)S(1)} collective-permute-done((bf16[3,64,128]{2,1,0:T(8,128)(2,1)S(1)}, bf16[3,64,128]{2,1,0:T(8,128)(2,1)S(1)}, u32[]{:S(2)}, u32[]{:S(2)}) %collective-permute-start.11) | collective-permute-done | bytes 49184 | tf_op jit(solution)/shard_map/ppermute | solution.py:513
  38.7 0.8 %shard_map.80 = (bf16[64,1024]{1,0:T(8,128)(2,1)}, bf16[64,1024]{1,0:T(8,128)(2,1)}, bf16[64,1024]{1,0:T(8,128)(2,1)}) custom-call(bf16[3,64,128]{2,1,0:T(8,128)(2,1)S(1)} %get-tuple-element.45.refs_0_, bf16[3,64,128]{2,1,0:T(8,128)(2,1)S(1)} %collective-permute-done.6.refs_1_, bf16[3,64,128]{2,1,0:T(8,128)(2,1)S(1)} %collective-permute-done.7.refs_2_, ...), custom_call_target="tpu_custom_call" | custom-call | bytes 1048576 | tf_op jit(solution)/shard_map/pallas_call | solution.py:499
  (8 shorter events, 0.4 us)
Async XLA Ops:
  1.8 9.6 %collective-permute-start = (bf16[2,320,128]{2,1,0:T(8,128)(2,1)S(1)}, bf16[2,320,128]{2,1,0:T(8,128)(2,1)S(1)}, u32[]{:S(2)}, u32[]{:S(2)}) collective-permute-start(bf16[2,320,128]{2,1,0:T(8,128)(2,1)S(1)} %get-tuple-element.34), channel_id=1, source_target_pairs={{0,24},{8,16},{16,8},{24,0},{1,25},{9,17},{17,9},{25,1},{2,26},{10... | collective-permute-start | bytes 491528 | tf_op jit(solution)/shard_map/ppermute | solution.py:513
  5.7 8.0 %collective-permute-start.1 = (bf16[2,320,128]{2,1,0:T(8,128)(2,1)S(1)}, bf16[2,320,128]{2,1,0:T(8,128)(2,1)S(1)}, u32[]{:S(2)}, u32[]{:S(2)}) collective-permute-start(bf16[2,320,128]{2,1,0:T(8,128)(2,1)S(1)} %get-tuple-element.35), channel_id=1, source_target_pairs={{0,8},{8,0},{16,24},{24,16},{1,9},{9,1},{17,25},{25,17},{2,10},{10... | collective-permute-start | bytes 491528 | tf_op jit(solution)/shard_map/ppermute | solution.py:513
  6.3 5.1 %collective-permute-start.2 = (bf16[2,128,128]{2,1,0:T(8,128)(2,1)S(1)}, bf16[2,128,128]{2,1,0:T(8,128)(2,1)S(1)}, u32[]{:S(2)}, u32[]{:S(2)}) collective-permute-start(bf16[2,128,128]{2,1,0:T(8,128)(2,1)S(1)} %get-tuple-element.36), channel_id=1, source_target_pairs={{0,16},{8,24},{16,0},{24,8},{1,17},{9,25},{17,1},{25,9},{2,18},{10... | collective-permute-start | bytes 196616 | tf_op jit(solution)/shard_map/ppermute | solution.py:513
  17.7 7.7 %collective-permute-start.3 = (bf16[2,320,128]{2,1,0:T(8,128)(2,1)S(1)}, bf16[2,320,128]{2,1,0:T(8,128)(2,1)S(1)}, u32[]{:S(2)}, u32[]{:S(2)}) collective-permute-start(bf16[2,320,128]{2,1,0:T(8,128)(2,1)S(1)} %get-tuple-element.42), channel_id=1, source_target_pairs={{0,24},{8,16},{16,8},{24,0},{1,25},{9,17},{17,9},{25,1},{2,26},{10... | collective-permute-start | bytes 491528 | tf_op jit(solution)/shard_map/ppermute | solution.py:513
  19.1 7.2 %collective-permute-start.4 = (bf16[2,320,128]{2,1,0:T(8,128)(2,1)S(1)}, bf16[2,320,128]{2,1,0:T(8,128)(2,1)S(1)}, u32[]{:S(2)}, u32[]{:S(2)}) collective-permute-start(bf16[2,320,128]{2,1,0:T(8,128)(2,1)S(1)} %get-tuple-element.43), channel_id=1, source_target_pairs={{0,8},{8,0},{16,24},{24,16},{1,9},{9,1},{17,25},{25,17},{2,10},{10... | collective-permute-start | bytes 491528 | tf_op jit(solution)/shard_map/ppermute | solution.py:513
  19.5 5.0 %collective-permute-start.5 = (bf16[2,128,128]{2,1,0:T(8,128)(2,1)S(1)}, bf16[2,128,128]{2,1,0:T(8,128)(2,1)S(1)}, u32[]{:S(2)}, u32[]{:S(2)}) collective-permute-start(bf16[2,128,128]{2,1,0:T(8,128)(2,1)S(1)} %get-tuple-element.44), channel_id=1, source_target_pairs={{0,16},{8,24},{16,0},{24,8},{1,17},{9,25},{17,1},{25,9},{2,18},{10... | collective-permute-start | bytes 196616 | tf_op jit(solution)/shard_map/ppermute | solution.py:513
  26.6 6.3 %collective-permute-start.6 = (bf16[3,64,128]{2,1,0:T(8,128)(2,1)S(1)}, bf16[3,64,128]{2,1,0:T(8,128)(2,1)S(1)}, u32[]{:S(2)}, u32[]{:S(2)}) collective-permute-start(bf16[3,64,128]{2,1,0:T(8,128)(2,1)S(1)} %get-tuple-element.46), channel_id=1, source_target_pairs={{0,4},{1,5},{2,6},{3,7},{4,0},{5,1},{6,2},{7,3},{8,12},{9,13},{10,... | collective-permute-start | bytes 147464 | tf_op jit(solution)/shard_map/ppermute | solution.py:513
  29.1 5.3 %collective-permute-start.7 = (bf16[3,64,128]{2,1,0:T(8,128)(2,1)S(1)}, bf16[3,64,128]{2,1,0:T(8,128)(2,1)S(1)}, u32[]{:S(2)}, u32[]{:S(2)}) collective-permute-start(bf16[3,64,128]{2,1,0:T(8,128)(2,1)S(1)} %get-tuple-element.47), channel_id=1, source_target_pairs={{0,5},{1,4},{2,7},{3,6},{4,1},{5,0},{6,3},{7,2},{8,13},{9,12},{10,... | collective-permute-start | bytes 147464 | tf_op jit(solution)/shard_map/ppermute | solution.py:513
  29.1 6.4 %collective-permute-start.8 = (bf16[3,64,128]{2,1,0:T(8,128)(2,1)S(1)}, bf16[3,64,128]{2,1,0:T(8,128)(2,1)S(1)}, u32[]{:S(2)}, u32[]{:S(2)}) collective-permute-start(bf16[3,64,128]{2,1,0:T(8,128)(2,1)S(1)} %get-tuple-element.48), channel_id=1, source_target_pairs={{0,6},{1,7},{2,4},{3,5},{4,2},{5,3},{6,0},{7,1},{8,14},{9,15},{10,... | collective-permute-start | bytes 147464 | tf_op jit(solution)/shard_map/ppermute | solution.py:513
  30.5 5.8 %collective-permute-start.9 = (bf16[3,64,128]{2,1,0:T(8,128)(2,1)S(1)}, bf16[3,64,128]{2,1,0:T(8,128)(2,1)S(1)}, u32[]{:S(2)}, u32[]{:S(2)}) collective-permute-start(bf16[3,64,128]{2,1,0:T(8,128)(2,1)S(1)} %get-tuple-element.49), channel_id=1, source_target_pairs={{0,7},{1,6},{2,5},{3,4},{4,3},{5,2},{6,1},{7,0},{8,15},{9,14},{10,... | collective-permute-start | bytes 147464 | tf_op jit(solution)/shard_map/ppermute | solution.py:513
  32.9 4.6 %collective-permute-start.10 = (bf16[3,64,128]{2,1,0:T(8,128)(2,1)S(1)}, bf16[3,64,128]{2,1,0:T(8,128)(2,1)S(1)}, u32[]{:S(2)}, u32[]{:S(2)}) collective-permute-start(bf16[3,64,128]{2,1,0:T(8,128)(2,1)S(1)} %get-tuple-element.50), channel_id=1, source_target_pairs={{0,2},{1,3},{2,0},{3,1},{4,6},{5,7},{6,4},{7,5},{8,10},{9,11},{10,... | collective-permute-start | bytes 147464 | tf_op jit(solution)/shard_map/ppermute | solution.py:513
  32.9 5.8 %collective-permute-start.11 = (bf16[3,64,128]{2,1,0:T(8,128)(2,1)S(1)}, bf16[3,64,128]{2,1,0:T(8,128)(2,1)S(1)}, u32[]{:S(2)}, u32[]{:S(2)}) collective-permute-start(bf16[3,64,128]{2,1,0:T(8,128)(2,1)S(1)} %get-tuple-element.51), channel_id=1, source_target_pairs={{0,3},{1,2},{2,1},{3,0},{4,7},{5,6},{6,5},{7,4},{8,11},{9,10},{10,... | collective-permute-start | bytes 147464 | tf_op jit(solution)/shard_map/ppermute | solution.py:513
  34.4 4.3 %collective-permute-start.12 = (bf16[3,64,128]{2,1,0:T(8,128)(2,1)S(1)}, bf16[3,64,128]{2,1,0:T(8,128)(2,1)S(1)}, u32[]{:S(2)}, u32[]{:S(2)}) collective-permute-start(bf16[3,64,128]{2,1,0:T(8,128)(2,1)S(1)} %get-tuple-element.52), channel_id=1, source_target_pairs={{0,1},{1,0},{2,3},{3,2},{4,5},{5,4},{6,7},{7,6},{8,9},{9,8},{10,11... | collective-permute-start | bytes 147464 | tf_op jit(solution)/shard_map/ppermute | solution.py:513

commit v3 on v2

--- a/solution.py
+++ b/solution.py
@@ -275,8 +275,13 @@
             peak = jnp.maximum(peak, before[0])
         exps = [jnp.exp2(score - across(peak, score.shape[1])) for score in scores]
         rounded = [e.astype(BF16) for e in exps]
-        total = total_of([row_sum(e) for e in exps])
-        sums = total_of([nn(r, piece[1]) for r, piece in zip(rounded, pieces)])
+        ones = jnp.ones((BLOCK, width), BF16)
+        both = []
+        for r, piece in zip(rounded, pieces):
+            count = piece[1].shape[0] // BLOCK
+            both.append(nn(r, jnp.concatenate([piece[1], jnp.concatenate([ones] * count, axis=0)], axis=1)))
+        both = total_of(both)
+        sums, total = both[:, :width], both[:, width:]
         if before is not None:
             keep = jnp.exp2(before[0] - peak)
             total, sums = total + keep * before[1], sums + keep * before[2]
@@ -406,7 +411,8 @@
                 out[i, BLOCK:] = jnp.zeros((REST, width), BF16)
 
 
-def local_kernel(held, back, partial_ref, grad_query_ref, local_ref):
+def local_kernel(held, back, partial_ref, merged, attended_ref, grad_query_ref, local_ref):
+    attended_ref[...] = merged[...]
     blocks, width = held.shape[1] // BLOCK, held.shape[2]
     scale = width ** (-0.5)
     factor = scale * LOG2E
@@ -573,14 +579,14 @@
         (held, stats, *level_queries, *received),
         flops=70 * unit_flops,
     )
-    attended, sends, back, partial = main[0], main[1:seq_count], main[-2], main[-1]
+    merged, sends, back, partial = main[0], main[1:seq_count], main[-2], main[-1]
     returned = swap_all(sends, "seq", distances)
 
-    grad_query, local = call(
+    attended, grad_query, local = call(
         local_kernel,
-        [shape(rows, width), shape(2, rows, width, dtype=F32)],
+        [shape(rows, width), shape(rows, width), shape(2, rows, width, dtype=F32)],
         [],
-        (held, back, partial),
+        (held, back, partial, merged),
         flops=50 * unit_flops,
     )
 

time: 39.7 us -> 38.7 us (0.975)
  waiting for transfers between devices: 13.9 us -> 13.3 us
  Pallas kernels: 8.53 us -> 8.06 us
    ppermute x13, waiting for transfers between devices: 13.9 us -> 13.3 us  [swap_all(): lax.ppermute(x, axis, [(i, i ^ d) for i in range(size)])]
    pallas_call x6, Pallas kernels: 8.53 us -> 8.06 us  [call(): pl.pallas_call(kernel, out_shape=outs, in_specs=[pl.BlockSpec(memory_spac...]
  transfers between devices with their start and end apart: 13 -> 13, of which waited for: 9 -> 9; matrix products, arithmetic and copies ran while one was open for 0% -> 0% of each run, Pallas kernels for 6% -> 7%
where the time goes in v3:
time: 38.7 us; the launch traced here: 38.6 us
  starting transfers between devices  16.6 us (43%)
  waiting for transfers between devices  13.3 us (34%)
  Pallas kernels  8.06 us (21%)
  between operations  0.67 us (2%)
    ppermute x13, starting transfers between devices, swap_all(): lax.ppermute(x, axis, [(i, i ^ d) for i in range(size)])  16.6 us
    ppermute x13, waiting for transfers between devices, swap_all(): lax.ppermute(x, axis, [(i, i ^ d) for i in range(size)])  13.3 us
    pallas_call x6, Pallas kernels, call(): pl.pallas_call(kernel, out_shape=outs, in_specs=[pl.BlockSpec(memory_spac...  8.06 us
  transfers between devices with their start and end apart: 13, of which 9 were waited for; matrix products, arithmetic and copies ran while one was open for 0% of the time, Pallas kernels for 7%

profile of v3, /device:TPU:0, one launch (start us, length us, event | category | flops | bytes accessed | tf_op | source)
XLA Modules:
  0.0 38.6 jit_solution(2594860841091636605)
XLA Ops:
  0.6 1.1 %shard_map.75 = (bf16[4,512,128]{2,1,0:T(8,128)(2,1)S(1)}, bf16[2,320,128]{2,1,0:T(8,128)(2,1)S(1)}, bf16[2,320,128]{2,1,0:T(8,128)(2,1)S(1)}, bf16[2,128,128]{2,1,0:T(8,128)(2,1)S(1)}) custom-call(bf16[512,128]{1,0:T(8,128)(2,1)} %refs_0_.1, bf16[512,128]{1,0:T(8,128)(2,1)} %refs_1_.1, bf16[512,128]{1,0:T(8,128)(2,1)} %refs_2_.1, bf16[512,128]{1,0:T(8,128)(2,1)} %refs_3_.1), custom_call_target="tpu_custom_call" | custom-call | bytes 1048576 | tf_op jit(solution)/shard_map/pallas_call | solution.py:505
  1.8 4.0 %collective-permute-start = (bf16[2,320,128]{2,1,0:T(8,128)(2,1)S(1)}, bf16[2,320,128]{2,1,0:T(8,128)(2,1)S(1)}, u32[]{:S(2)}, u32[]{:S(2)}) collective-permute-start(bf16[2,320,128]{2,1,0:T(8,128)(2,1)S(1)} %get-tuple-element.35), channel_id=1, source_target_pairs={{0,24},{8,16},{16,8},{24,0},{1,25},{9,17},{17,9},{25,1},{2,26},{10... | collective-permute-start | bytes 491528 | tf_op jit(solution)/shard_map/ppermute | solution.py:519
  5.7 0.5 %collective-permute-start.1 = (bf16[2,320,128]{2,1,0:T(8,128)(2,1)S(1)}, bf16[2,320,128]{2,1,0:T(8,128)(2,1)S(1)}, u32[]{:S(2)}, u32[]{:S(2)}) collective-permute-start(bf16[2,320,128]{2,1,0:T(8,128)(2,1)S(1)} %get-tuple-element.36), channel_id=1, source_target_pairs={{0,8},{8,0},{16,24},{24,16},{1,9},{9,1},{17,25},{25,17},{2,10},{10... | collective-permute-start | bytes 491528 | tf_op jit(solution)/shard_map/ppermute | solution.py:519
  6.4 1.1 %shard_map.76 = (f32[3,512,128]{2,1,0:T(8,128)S(1)}, bf16[256,128]{1,0:T(8,128)(2,1)S(1)}, bf16[128,128]{1,0:T(8,128)(2,1)S(1)}) custom-call(bf16[4,512,128]{2,1,0:T(8,128)(2,1)S(1)} %get-tuple-element.31.held.refs_0_), custom_call_target="tpu_custom_call" | custom-call | flops 83886080 | bytes 1048576 | tf_op jit(solution)/shard_map/pallas_call | solution.py:505
  7.5 3.8 %collective-permute-done.2.refs_6_ = bf16[2,128,128]{2,1,0:T(8,128)(2,1)S(1)} collective-permute-done((bf16[2,128,128]{2,1,0:T(8,128)(2,1)S(1)}, bf16[2,128,128]{2,1,0:T(8,128)(2,1)S(1)}, u32[]{:S(2)}, u32[]{:S(2)}) %collective-permute-start.2) | collective-permute-done | bytes 65568 | tf_op jit(solution)/shard_map/ppermute | solution.py:519
  11.3 2.4 %collective-permute-done.1.refs_5_ = bf16[2,320,128]{2,1,0:T(8,128)(2,1)S(1)} collective-permute-done((bf16[2,320,128]{2,1,0:T(8,128)(2,1)S(1)}, bf16[2,320,128]{2,1,0:T(8,128)(2,1)S(1)}, u32[]{:S(2)}, u32[]{:S(2)}) %collective-permute-start.1) | collective-permute-done | bytes 163872 | tf_op jit(solution)/shard_map/ppermute | solution.py:519
  13.7 3.0 %shard_map.77 = (bf16[512,128]{1,0:T(8,128)(2,1)S(1)}, bf16[2,320,128]{2,1,0:T(8,128)(2,1)S(1)}, bf16[2,320,128]{2,1,0:T(8,128)(2,1)S(1)}, bf16[2,128,128]{2,1,0...) custom-call(bf16[4,512,128]{2,1,0:T(8,128)(2,1)S(1)} %get-tuple-element.31.held.refs_0_, ...), custom_call_target="tpu_custom_call" | custom-call | flops 293601280 | bytes 1048576 | tf_op jit(solution)/shard_map/pallas_call | solution.py:505
  16.7 1.5 %collective-permute-start.3 = (bf16[2,320,128]{2,1,0:T(8,128)(2,1)S(1)}, bf16[2,320,128]{2,1,0:T(8,128)(2,1)S(1)}, u32[]{:S(2)}, u32[]{:S(2)}) collective-permute-start(bf16[2,320,128]{2,1,0:T(8,128)(2,1)S(1)} %get-tuple-element.44), channel_id=1, source_target_pairs={{0,24},{8,16},{16,8},{24,0},{1,25},{9,17},{17,9},{25,1},{2,26},{10... | collective-permute-start | bytes 491528 | tf_op jit(solution)/shard_map/ppermute | solution.py:519
  18.2 0.3 collective-permute-start.4
  18.5 1.8 %collective-permute-start.5 = (bf16[2,128,128]{2,1,0:T(8,128)(2,1)S(1)}, bf16[2,128,128]{2,1,0:T(8,128)(2,1)S(1)}, u32[]{:S(2)}, u32[]{:S(2)}) collective-permute-start(bf16[2,128,128]{2,1,0:T(8,128)(2,1)S(1)} %get-tuple-element.46), channel_id=1, source_target_pairs={{0,16},{8,24},{16,0},{24,8},{1,17},{9,25},{17,1},{25,9},{2,18},{10... | collective-permute-start | bytes 196616 | tf_op jit(solution)/shard_map/ppermute | solution.py:519
  20.3 1.7 %shard_map.78 = (bf16[512,128]{1,0:T(8,128)(2,1)}, bf16[512,128]{1,0:T(8,128)(2,1)S(1)}, f32[2,512,128]{2,1,0:T(8,128)S(1)}) custom-call(bf16[4,512,128]{2,1,0:T(8,128)(2,1)S(1)} %get-tuple-element.31.held.refs_0_, f32[3,512,128]{2,1,0:T(8,128)S(1)} %get-tuple-element.38.back, f32[512,128]{1,0:T(8,128)S(1)} %get-tuple-element.39.partial_ref, ...), custom_call_target="tpu_custom_call" | custom-call | flops 209715200 | bytes 1048576 | tf_op jit(solution)/shard_map/pallas_call | solution.py:505
  22.0 1.5 %collective-permute-done.5.refs_2_ = bf16[2,128,128]{2,1,0:T(8,128)(2,1)S(1)} collective-permute-done((bf16[2,128,128]{2,1,0:T(8,128)(2,1)S(1)}, bf16[2,128,128]{2,1,0:T(8,128)(2,1)S(1)}, u32[]{:S(2)}, u32[]{:S(2)}) %collective-permute-start.5) | collective-permute-done | bytes 65568 | tf_op jit(solution)/shard_map/ppermute | solution.py:519
  23.5 1.0 %collective-permute-done.3.refs_0_ = bf16[2,320,128]{2,1,0:T(8,128)(2,1)S(1)} collective-permute-done((bf16[2,320,128]{2,1,0:T(8,128)(2,1)S(1)}, bf16[2,320,128]{2,1,0:T(8,128)(2,1)S(1)}, u32[]{:S(2)}, u32[]{:S(2)}) %collective-permute-start.3) | collective-permute-done | bytes 163872 | tf_op jit(solution)/shard_map/ppermute | solution.py:519
  24.5 0.9 %collective-permute-done.4.refs_1_ = bf16[2,320,128]{2,1,0:T(8,128)(2,1)S(1)} collective-permute-done((bf16[2,320,128]{2,1,0:T(8,128)(2,1)S(1)}, bf16[2,320,128]{2,1,0:T(8,128)(2,1)S(1)}, u32[]{:S(2)}, u32[]{:S(2)}) %collective-permute-start.4) | collective-permute-done | bytes 163872 | tf_op jit(solution)/shard_map/ppermute | solution.py:519
  25.6 2.5 %collective-permute-start.6 = (bf16[3,64,128]{2,1,0:T(8,128)(2,1)S(1)}, bf16[3,64,128]{2,1,0:T(8,128)(2,1)S(1)}, u32[]{:S(2)}, u32[]{:S(2)}) collective-permute-start(bf16[3,64,128]{2,1,0:T(8,128)(2,1)S(1)} %get-tuple-element.48), channel_id=1, source_target_pairs={{0,4},{1,5},{2,6},{3,7},{4,0},{5,1},{6,2},{7,3},{8,12},{9,13},{10,... | collective-permute-start | bytes 147464 | tf_op jit(solution)/shard_map/ppermute | solution.py:519
  28.2 1.4 %collective-permute-start.8 = (bf16[3,64,128]{2,1,0:T(8,128)(2,1)S(1)}, bf16[3,64,128]{2,1,0:T(8,128)(2,1)S(1)}, u32[]{:S(2)}, u32[]{:S(2)}) collective-permute-start(bf16[3,64,128]{2,1,0:T(8,128)(2,1)S(1)} %get-tuple-element.50), channel_id=1, source_target_pairs={{0,6},{1,7},{2,4},{3,5},{4,2},{5,3},{6,0},{7,1},{8,14},{9,15},{10,... | collective-permute-start | bytes 147464 | tf_op jit(solution)/shard_map/ppermute | solution.py:519
  29.5 2.4 %collective-permute-start.9 = (bf16[3,64,128]{2,1,0:T(8,128)(2,1)S(1)}, bf16[3,64,128]{2,1,0:T(8,128)(2,1)S(1)}, u32[]{:S(2)}, u32[]{:S(2)}) collective-permute-start(bf16[3,64,128]{2,1,0:T(8,128)(2,1)S(1)} %get-tuple-element.51), channel_id=1, source_target_pairs={{0,7},{1,6},{2,5},{3,4},{4,3},{5,2},{6,1},{7,0},{8,15},{9,14},{10,... | collective-permute-start | bytes 147464 | tf_op jit(solution)/shard_map/ppermute | solution.py:519
  31.9 1.6 %collective-permute-start.11 = (bf16[3,64,128]{2,1,0:T(8,128)(2,1)S(1)}, bf16[3,64,128]{2,1,0:T(8,128)(2,1)S(1)}, u32[]{:S(2)}, u32[]{:S(2)}) collective-permute-start(bf16[3,64,128]{2,1,0:T(8,128)(2,1)S(1)} %get-tuple-element.53), channel_id=1, source_target_pairs={{0,3},{1,2},{2,1},{3,0},{4,7},{5,6},{6,5},{7,4},{8,11},{9,10},{10,... | collective-permute-start | bytes 147464 | tf_op jit(solution)/shard_map/ppermute | solution.py:519
  33.5 0.6 %collective-permute-start.12 = (bf16[3,64,128]{2,1,0:T(8,128)(2,1)S(1)}, bf16[3,64,128]{2,1,0:T(8,128)(2,1)S(1)}, u32[]{:S(2)}, u32[]{:S(2)}) collective-permute-start(bf16[3,64,128]{2,1,0:T(8,128)(2,1)S(1)} %get-tuple-element.54), channel_id=1, source_target_pairs={{0,1},{1,0},{2,3},{3,2},{4,5},{5,4},{6,7},{7,6},{8,9},{9,8},{10,11... | collective-permute-start | bytes 147464 | tf_op jit(solution)/shard_map/ppermute | solution.py:519
  34.0 0.6 %collective-permute-done.8.refs_3_ = bf16[3,64,128]{2,1,0:T(8,128)(2,1)S(1)} collective-permute-done((bf16[3,64,128]{2,1,0:T(8,128)(2,1)S(1)}, bf16[3,64,128]{2,1,0:T(8,128)(2,1)S(1)}, u32[]{:S(2)}, u32[]{:S(2)}) %collective-permute-start.8) | collective-permute-done | bytes 49184 | tf_op jit(solution)/shard_map/ppermute | solution.py:519
  34.6 0.7 %collective-permute-done.9.refs_4_ = bf16[3,64,128]{2,1,0:T(8,128)(2,1)S(1)} collective-permute-done((bf16[3,64,128]{2,1,0:T(8,128)(2,1)S(1)}, bf16[3,64,128]{2,1,0:T(8,128)(2,1)S(1)}, u32[]{:S(2)}, u32[]{:S(2)}) %collective-permute-start.9) | collective-permute-done | bytes 49184 | tf_op jit(solution)/shard_map/ppermute | solution.py:519
  35.3 1.2 %collective-permute-done.10.refs_5_ = bf16[3,64,128]{2,1,0:T(8,128)(2,1)S(1)} collective-permute-done((bf16[3,64,128]{2,1,0:T(8,128)(2,1)S(1)}, bf16[3,64,128]{2,1,0:T(8,128)(2,1)S(1)}, u32[]{:S(2)}, u32[]{:S(2)}) %collective-permute-start.10) | collective-permute-done | bytes 49184 | tf_op jit(solution)/shard_map/ppermute | solution.py:519
  36.5 1.2 %collective-permute-done.11.refs_6_ = bf16[3,64,128]{2,1,0:T(8,128)(2,1)S(1)} collective-permute-done((bf16[3,64,128]{2,1,0:T(8,128)(2,1)S(1)}, bf16[3,64,128]{2,1,0:T(8,128)(2,1)S(1)}, u32[]{:S(2)}, u32[]{:S(2)}) %collective-permute-start.11) | collective-permute-done | bytes 49184 | tf_op jit(solution)/shard_map/ppermute | solution.py:519
  37.7 0.8 %shard_map.80 = (bf16[64,1024]{1,0:T(8,128)(2,1)}, bf16[64,1024]{1,0:T(8,128)(2,1)}, bf16[64,1024]{1,0:T(8,128)(2,1)}) custom-call(bf16[3,64,128]{2,1,0:T(8,128)(2,1)S(1)} %get-tuple-element.47.refs_0_, bf16[3,64,128]{2,1,0:T(8,128)(2,1)S(1)} %collective-permute-done.6.refs_1_, bf16[3,64,128]{2,1,0:T(8,128)(2,1)S(1)} %collective-permute-done.7.refs_2_, ...), custom_call_target="tpu_custom_call" | custom-call | bytes 1048576 | tf_op jit(solution)/shard_map/pallas_call | solution.py:505
  (8 shorter events, 0.4 us)
Async XLA Ops:
  1.8 9.6 %collective-permute-start = (bf16[2,320,128]{2,1,0:T(8,128)(2,1)S(1)}, bf16[2,320,128]{2,1,0:T(8,128)(2,1)S(1)}, u32[]{:S(2)}, u32[]{:S(2)}) collective-permute-start(bf16[2,320,128]{2,1,0:T(8,128)(2,1)S(1)} %get-tuple-element.35), channel_id=1, source_target_pairs={{0,24},{8,16},{16,8},{24,0},{1,25},{9,17},{17,9},{25,1},{2,26},{10... | collective-permute-start | bytes 491528 | tf_op jit(solution)/shard_map/ppermute | solution.py:519
  5.7 8.0 %collective-permute-start.1 = (bf16[2,320,128]{2,1,0:T(8,128)(2,1)S(1)}, bf16[2,320,128]{2,1,0:T(8,128)(2,1)S(1)}, u32[]{:S(2)}, u32[]{:S(2)}) collective-permute-start(bf16[2,320,128]{2,1,0:T(8,128)(2,1)S(1)} %get-tuple-element.36), channel_id=1, source_target_pairs={{0,8},{8,0},{16,24},{24,16},{1,9},{9,1},{17,25},{25,17},{2,10},{10... | collective-permute-start | bytes 491528 | tf_op jit(solution)/shard_map/ppermute | solution.py:519
  6.3 5.1 %collective-permute-start.2 = (bf16[2,128,128]{2,1,0:T(8,128)(2,1)S(1)}, bf16[2,128,128]{2,1,0:T(8,128)(2,1)S(1)}, u32[]{:S(2)}, u32[]{:S(2)}) collective-permute-start(bf16[2,128,128]{2,1,0:T(8,128)(2,1)S(1)} %get-tuple-element.37), channel_id=1, source_target_pairs={{0,16},{8,24},{16,0},{24,8},{1,17},{9,25},{17,1},{25,9},{2,18},{10... | collective-permute-start | bytes 196616 | tf_op jit(solution)/shard_map/ppermute | solution.py:519
  16.7 7.8 %collective-permute-start.3 = (bf16[2,320,128]{2,1,0:T(8,128)(2,1)S(1)}, bf16[2,320,128]{2,1,0:T(8,128)(2,1)S(1)}, u32[]{:S(2)}, u32[]{:S(2)}) collective-permute-start(bf16[2,320,128]{2,1,0:T(8,128)(2,1)S(1)} %get-tuple-element.44), channel_id=1, source_target_pairs={{0,24},{8,16},{16,8},{24,0},{1,25},{9,17},{17,9},{25,1},{2,26},{10... | collective-permute-start | bytes 491528 | tf_op jit(solution)/shard_map/ppermute | solution.py:519
  18.2 7.2 %collective-permute-start.4 = (bf16[2,320,128]{2,1,0:T(8,128)(2,1)S(1)}, bf16[2,320,128]{2,1,0:T(8,128)(2,1)S(1)}, u32[]{:S(2)}, u32[]{:S(2)}) collective-permute-start(bf16[2,320,128]{2,1,0:T(8,128)(2,1)S(1)} %get-tuple-element.45), channel_id=1, source_target_pairs={{0,8},{8,0},{16,24},{24,16},{1,9},{9,1},{17,25},{25,17},{2,10},{10... | collective-permute-start | bytes 491528 | tf_op jit(solution)/shard_map/ppermute | solution.py:519
  18.5 5.0 %collective-permute-start.5 = (bf16[2,128,128]{2,1,0:T(8,128)(2,1)S(1)}, bf16[2,128,128]{2,1,0:T(8,128)(2,1)S(1)}, u32[]{:S(2)}, u32[]{:S(2)}) collective-permute-start(bf16[2,128,128]{2,1,0:T(8,128)(2,1)S(1)} %get-tuple-element.46), channel_id=1, source_target_pairs={{0,16},{8,24},{16,0},{24,8},{1,17},{9,25},{17,1},{25,9},{2,18},{10... | collective-permute-start | bytes 196616 | tf_op jit(solution)/shard_map/ppermute | solution.py:519
  25.6 6.3 %collective-permute-start.6 = (bf16[3,64,128]{2,1,0:T(8,128)(2,1)S(1)}, bf16[3,64,128]{2,1,0:T(8,128)(2,1)S(1)}, u32[]{:S(2)}, u32[]{:S(2)}) collective-permute-start(bf16[3,64,128]{2,1,0:T(8,128)(2,1)S(1)} %get-tuple-element.48), channel_id=1, source_target_pairs={{0,4},{1,5},{2,6},{3,7},{4,0},{5,1},{6,2},{7,3},{8,12},{9,13},{10,... | collective-permute-start | bytes 147464 | tf_op jit(solution)/shard_map/ppermute | solution.py:519
  28.2 5.3 %collective-permute-start.7 = (bf16[3,64,128]{2,1,0:T(8,128)(2,1)S(1)}, bf16[3,64,128]{2,1,0:T(8,128)(2,1)S(1)}, u32[]{:S(2)}, u32[]{:S(2)}) collective-permute-start(bf16[3,64,128]{2,1,0:T(8,128)(2,1)S(1)} %get-tuple-element.49), channel_id=1, source_target_pairs={{0,5},{1,4},{2,7},{3,6},{4,1},{5,0},{6,3},{7,2},{8,13},{9,12},{10,... | collective-permute-start | bytes 147464 | tf_op jit(solution)/shard_map/ppermute | solution.py:519
  28.2 6.4 %collective-permute-start.8 = (bf16[3,64,128]{2,1,0:T(8,128)(2,1)S(1)}, bf16[3,64,128]{2,1,0:T(8,128)(2,1)S(1)}, u32[]{:S(2)}, u32[]{:S(2)}) collective-permute-start(bf16[3,64,128]{2,1,0:T(8,128)(2,1)S(1)} %get-tuple-element.50), channel_id=1, source_target_pairs={{0,6},{1,7},{2,4},{3,5},{4,2},{5,3},{6,0},{7,1},{8,14},{9,15},{10,... | collective-permute-start | bytes 147464 | tf_op jit(solution)/shard_map/ppermute | solution.py:519
  29.5 5.8 %collective-permute-start.9 = (bf16[3,64,128]{2,1,0:T(8,128)(2,1)S(1)}, bf16[3,64,128]{2,1,0:T(8,128)(2,1)S(1)}, u32[]{:S(2)}, u32[]{:S(2)}) collective-permute-start(bf16[3,64,128]{2,1,0:T(8,128)(2,1)S(1)} %get-tuple-element.51), channel_id=1, source_target_pairs={{0,7},{1,6},{2,5},{3,4},{4,3},{5,2},{6,1},{7,0},{8,15},{9,14},{10,... | collective-permute-start | bytes 147464 | tf_op jit(solution)/shard_map/ppermute | solution.py:519
  31.9 4.6 %collective-permute-start.10 = (bf16[3,64,128]{2,1,0:T(8,128)(2,1)S(1)}, bf16[3,64,128]{2,1,0:T(8,128)(2,1)S(1)}, u32[]{:S(2)}, u32[]{:S(2)}) collective-permute-start(bf16[3,64,128]{2,1,0:T(8,128)(2,1)S(1)} %get-tuple-element.52), channel_id=1, source_target_pairs={{0,2},{1,3},{2,0},{3,1},{4,6},{5,7},{6,4},{7,5},{8,10},{9,11},{10,... | collective-permute-start | bytes 147464 | tf_op jit(solution)/shard_map/ppermute | solution.py:519
  31.9 5.8 %collective-permute-start.11 = (bf16[3,64,128]{2,1,0:T(8,128)(2,1)S(1)}, bf16[3,64,128]{2,1,0:T(8,128)(2,1)S(1)}, u32[]{:S(2)}, u32[]{:S(2)}) collective-permute-start(bf16[3,64,128]{2,1,0:T(8,128)(2,1)S(1)} %get-tuple-element.53), channel_id=1, source_target_pairs={{0,3},{1,2},{2,1},{3,0},{4,7},{5,6},{6,5},{7,4},{8,11},{9,10},{10,... | collective-permute-start | bytes 147464 | tf_op jit(solution)/shard_map/ppermute | solution.py:519
  33.5 4.3 %collective-permute-start.12 = (bf16[3,64,128]{2,1,0:T(8,128)(2,1)S(1)}, bf16[3,64,128]{2,1,0:T(8,128)(2,1)S(1)}, u32[]{:S(2)}, u32[]{:S(2)}) collective-permute-start(bf16[3,64,128]{2,1,0:T(8,128)(2,1)S(1)} %get-tuple-element.54), channel_id=1, source_target_pairs={{0,1},{1,0},{2,3},{3,2},{4,5},{5,4},{6,7},{7,6},{8,9},{9,8},{10,11... | collective-permute-start | bytes 147464 | tf_op jit(solution)/shard_map/ppermute | solution.py:519

commit v4 on v3

--- a/solution.py
+++ b/solution.py
@@ -55,8 +55,12 @@
     return wides[::-1] + [d for d in range(1, seq_count) if d not in wides]
 
 
+def paired(head_count):
+    return list(range(4, head_count, 2))
+
+
 def head_order(head_count):
-    return [d for d in range(4, head_count)] + [d for d in (2, 3, 1) if d < head_count]
+    return [d for d in [2, 3] + paired(head_count) + [1] if d < head_count]
 
 
 def prep_kernel(seq_count, *refs):
@@ -411,8 +415,9 @@
                 out[i, BLOCK:] = jnp.zeros((REST, width), BF16)
 
 
-def local_kernel(held, back, partial_ref, merged, attended_ref, grad_query_ref, local_ref):
-    attended_ref[...] = merged[...]
+def local_kernel(held, back, partial_ref, merged, attended_hbm, local_ref, grad_query_ref, sem):
+    copy = pltpu.make_async_copy(merged, attended_hbm, sem)
+    copy.start()
     blocks, width = held.shape[1] // BLOCK, held.shape[2]
     scale = width ** (-0.5)
     factor = scale * LOG2E
@@ -434,12 +439,13 @@
     for i in range(2):
         for b in range(blocks):
             local_ref[i, rows_of(b)] = total_of(parts[i][b])
+    copy.wait()
 
 
 def combine_kernel(seq_count, head_count, grad_query_ref, local_ref, *refs):
     received, refs = refs[: seq_count - 1], refs[seq_count - 1 :]
     received = dict(zip(seq_order(seq_count), received))
-    outs, refs = refs[:head_count], refs[head_count:]
+    outs, refs = refs[:-3], refs[-3:]
     outs = dict(zip([0] + head_order(head_count), outs))
     total, level_1, level_2 = refs
     seq_index, head_index = lax.axis_index("seq"), lax.axis_index("head")
@@ -485,29 +491,47 @@
             total[i, pl.ds(phase, half.shape[0], stride=2), :] += half
     for d in range(head_count):
         at = pl.ds(pl.multiple_of((head_index ^ d) * share, share), share)
-        outs[d][0] = grad_query_ref[at, :]
-        outs[d][1] = total[0, at].astype(BF16)
-        outs[d][2] = total[1, at].astype(BF16)
+        out = outs[d & ~1].at[d & 1] if d & ~1 in paired(head_count) else outs[d]
+        out[0] = grad_query_ref[at, :]
+        out[1] = total[0, at].astype(BF16)
+        out[2] = total[1, at].astype(BF16)
 
 
 def place_kernel(head_count, *refs):
-    parts, outs = refs[:head_count], refs[head_count:]
-    parts = dict(zip([0] + head_order(head_count), parts))
+    parts, outs = refs[:-3], refs[-3:]
     head_index = lax.axis_index("head")
     width = parts[0].shape[-1]
-    for d in range(head_count):
+    for d, part in zip([0] + head_order(head_count), parts):
         at = pl.ds(pl.multiple_of((head_index ^ d) * width, width), width)
         for i in range(3):
-            outs[i][:, at] = parts[d][i]
-
-
-def call(kernel, outs, scratch, args, space=pltpu.VMEM, flops=0):
+            outs[i][:, at] = part[0, i] if d in paired(head_count) else part[i]
+
+
+def place_late_kernel(head_count, *refs):
+    late, outs, sems = refs[3], refs[4:7], refs[7]
+    head_index = lax.axis_index("head")
+    width = late.shape[-1]
+    far = [d for d in head_order(head_count) if d in paired(head_count)]
+    copies = []
+    for row, d in enumerate(far):
+        at = pl.ds(pl.multiple_of((head_index ^ d ^ 1) * width, width), width)
+        for i in range(3):
+            k = 3 * row + i
+            copies.append(pltpu.make_async_copy(late.at[k], outs[i].at[:, at], sems.at[k]))
+            copies[-1].start()
+    for copy in copies:
+        copy.wait()
+
+
+def call(kernel, outs, scratch, args, in_hbm=0, hbm_outs=0, aliases={}, flops=0):
     return pl.pallas_call(
         kernel,
         out_shape=outs,
-        in_specs=[pl.BlockSpec(memory_space=space)] * len(args),
-        out_specs=[VMEM] * len(outs),
+        in_specs=[pl.BlockSpec(memory_space=pltpu.HBM)] * in_hbm + [VMEM] * (len(args) - in_hbm),
+        out_specs=[pl.BlockSpec(memory_space=pltpu.HBM)] * hbm_outs
+        + [VMEM] * (len(outs) - hbm_outs),
         scratch_shapes=scratch,
+        input_output_aliases=aliases,
         compiler_params=pltpu.CompilerParams(vmem_limit_bytes=48 * 2**20),
         cost_estimate=pl.CostEstimate(flops=flops, bytes_accessed=2**20, transcendentals=0),
     )(*args)
@@ -544,7 +568,7 @@
         [shape(4, rows, width)] + payloads,
         [f32(rows, width), f32(rows // 2, width)] * 2 + [pltpu.SemaphoreType.DMA((4,))],
         arguments,
-        pltpu.HBM,
+        in_hbm=4,
     )
     received = swap_all(sends, "seq", distances)
 
@@ -582,28 +606,46 @@
     merged, sends, back, partial = main[0], main[1:seq_count], main[-2], main[-1]
     returned = swap_all(sends, "seq", distances)
 
-    attended, grad_query, local = call(
+    share = rows // head_count
+    attended, local, grad_query = call(
         local_kernel,
-        [shape(rows, width), shape(rows, width), shape(2, rows, width, dtype=F32)],
-        [],
+        [shape(rows, width), shape(2, rows, width, dtype=F32), shape(rows, width)],
+        [pltpu.SemaphoreType.DMA],
         (held, back, partial, merged),
+        hbm_outs=1,
         flops=50 * unit_flops,
     )
 
-    share = rows // head_count
-    parts = call(
+    order = head_order(head_count)
+    own, *parts = call(
         functools.partial(combine_kernel, seq_count, head_count),
-        [shape(3, share, width)] * head_count,
+        [
+            shape(*((2,) if d in paired(head_count) else ()), 3, share, width)
+            for d in [0] + order
+        ],
         [f32(2, rows, width), f32(2, rows // 2, width), f32(2, rows // 4, width)],
         (grad_query, local, *returned),
     )
-    parts = [parts[0]] + swap_all(parts[1:], "head", head_order(head_count))
+    parts = lax.optimization_barrier(swap_all(parts, "head", order))
+    far = [part[1] for d, part in zip(order, parts) if d in paired(head_count)]
+    late = swap_all([jnp.concatenate(far, axis=0)] if far else [], "head", [1])
     grads = call(
         functools.partial(place_kernel, head_count),
         [shape(share, head_count * width)] * 3,
         [],
-        parts,
+        (own, *parts),
+        flops=50 * unit_flops,
     )
+    if late:
+        grads = call(
+            functools.partial(place_late_kernel, head_count),
+            [shape(share, head_count * width)] * 3,
+            [pltpu.SemaphoreType.DMA((3 * len(far),))],
+            (*grads, *late),
+            in_hbm=3,
+            hbm_outs=3,
+            aliases={0: 0, 1: 1, 2: 2},
+        )
     return (attended, *grads)
 
 

time: 38.7 us -> 37.8 us (0.977)
  starting transfers between devices: 16.6 us -> 14.6 us
  waiting for transfers between devices: 13.3 us -> 14.2 us
    ppermute x13 -> x12, starting transfers between devices: 16.6 us -> 14.6 us  [swap_all(): lax.ppermute(x, axis, [(i, i ^ d) for i in range(size)])]
    ppermute x13 -> x12, waiting for transfers between devices: 13.3 us -> 14.2 us  [swap_all(): lax.ppermute(x, axis, [(i, i ^ d) for i in range(size)])]
    pallas_call x6 -> x7, Pallas kernels: 8.06 us -> 8.16 us  [call(): pl.pallas_call(kernel, out_shape=outs, in_specs=[pl.BlockSpec(memory_spac...]
  transfers between devices with their start and end apart: 13 -> 12, of which waited for: 9 -> 7; matrix products, arithmetic and copies ran while one was open for 0% -> 0% of each run, Pallas kernels for 7% -> 8%
where the time goes in v4:
time: 37.8 us; the launch traced here: 37.7 us
  starting transfers between devices  14.6 us (39%)
  waiting for transfers between devices  14.2 us (38%)
  Pallas kernels  8.16 us (22%)
  between operations  0.7 us (2%)
    ppermute x12, starting transfers between devices, swap_all(): lax.ppermute(x, axis, [(i, i ^ d) for i in range(size)])  14.6 us
    ppermute x12, waiting for transfers between devices, swap_all(): lax.ppermute(x, axis, [(i, i ^ d) for i in range(size)])  14.2 us
    pallas_call x7, Pallas kernels, call(): pl.pallas_call(kernel, out_shape=outs, in_specs=[pl.BlockSpec(memory_spac...  8.16 us
  transfers between devices with their start and end apart: 12, of which 7 were waited for; matrix products, arithmetic and copies ran while one was open for 0% of the time, Pallas kernels for 8%

profile of v4, /device:TPU:0, one launch (start us, length us, event | category | flops | bytes accessed | tf_op | source)
XLA Modules:
  0.0 37.7 jit_solution(15203536757037499077)
XLA Ops:
  0.6 1.1 %shard_map.75 = (bf16[4,512,128]{2,1,0:T(8,128)(2,1)S(1)}, bf16[2,320,128]{2,1,0:T(8,128)(2,1)S(1)}, bf16[2,320,128]{2,1,0:T(8,128)(2,1)S(1)}, bf16[2,128,128]{2,1,0:T(8,128)(2,1)S(1)}) custom-call(bf16[512,128]{1,0:T(8,128)(2,1)} %refs_0_.1, bf16[512,128]{1,0:T(8,128)(2,1)} %refs_1_.1, bf16[512,128]{1,0:T(8,128)(2,1)} %refs_2_.1, bf16[512,128]{1,0:T(8,128)(2,1)} %refs_3_.1), custom_call_target="tpu_custom_call" | custom-call | bytes 1048576 | tf_op jit(solution)/shard_map/pallas_call | solution.py:527
  1.8 4.0 %collective-permute-start = (bf16[2,320,128]{2,1,0:T(8,128)(2,1)S(1)}, bf16[2,320,128]{2,1,0:T(8,128)(2,1)S(1)}, u32[]{:S(2)}, u32[]{:S(2)}) collective-permute-start(bf16[2,320,128]{2,1,0:T(8,128)(2,1)S(1)} %get-tuple-element.41), channel_id=1, source_target_pairs={{0,24},{8,16},{16,8},{24,0},{1,25},{9,17},{17,9},{25,1},{2,26},{10... | collective-permute-start | bytes 491528 | tf_op jit(solution)/shard_map/ppermute | solution.py:543
  5.7 0.5 %collective-permute-start.1 = (bf16[2,320,128]{2,1,0:T(8,128)(2,1)S(1)}, bf16[2,320,128]{2,1,0:T(8,128)(2,1)S(1)}, u32[]{:S(2)}, u32[]{:S(2)}) collective-permute-start(bf16[2,320,128]{2,1,0:T(8,128)(2,1)S(1)} %get-tuple-element.42), channel_id=1, source_target_pairs={{0,8},{8,0},{16,24},{24,16},{1,9},{9,1},{17,25},{25,17},{2,10},{10... | collective-permute-start | bytes 491528 | tf_op jit(solution)/shard_map/ppermute | solution.py:543
  6.4 1.1 %shard_map.76 = (f32[3,512,128]{2,1,0:T(8,128)S(1)}, bf16[256,128]{1,0:T(8,128)(2,1)S(1)}, bf16[128,128]{1,0:T(8,128)(2,1)S(1)}) custom-call(bf16[4,512,128]{2,1,0:T(8,128)(2,1)S(1)} %get-tuple-element.37.held.refs_0_), custom_call_target="tpu_custom_call" | custom-call | flops 83886080 | bytes 1048576 | tf_op jit(solution)/shard_map/pallas_call | solution.py:527
  7.5 3.8 %collective-permute-done.2.refs_6_ = bf16[2,128,128]{2,1,0:T(8,128)(2,1)S(1)} collective-permute-done((bf16[2,128,128]{2,1,0:T(8,128)(2,1)S(1)}, bf16[2,128,128]{2,1,0:T(8,128)(2,1)S(1)}, u32[]{:S(2)}, u32[]{:S(2)}) %collective-permute-start.2) | collective-permute-done | bytes 65568 | tf_op jit(solution)/shard_map/ppermute | solution.py:543
  11.3 2.4 %collective-permute-done.1.refs_5_ = bf16[2,320,128]{2,1,0:T(8,128)(2,1)S(1)} collective-permute-done((bf16[2,320,128]{2,1,0:T(8,128)(2,1)S(1)}, bf16[2,320,128]{2,1,0:T(8,128)(2,1)S(1)}, u32[]{:S(2)}, u32[]{:S(2)}) %collective-permute-start.1) | collective-permute-done | bytes 163872 | tf_op jit(solution)/shard_map/ppermute | solution.py:543
  13.7 3.0 %shard_map.77 = (bf16[512,128]{1,0:T(8,128)(2,1)S(1)}, bf16[2,320,128]{2,1,0:T(8,128)(2,1)S(1)}, bf16[2,320,128]{2,1,0:T(8,128)(2,1)S(1)}, bf16[2,128,128]{2,1,0...) custom-call(bf16[4,512,128]{2,1,0:T(8,128)(2,1)S(1)} %get-tuple-element.37.held.refs_0_, ...), custom_call_target="tpu_custom_call" | custom-call | flops 293601280 | bytes 1048576 | tf_op jit(solution)/shard_map/pallas_call | solution.py:527
  16.7 1.5 %collective-permute-start.3 = (bf16[2,320,128]{2,1,0:T(8,128)(2,1)S(1)}, bf16[2,320,128]{2,1,0:T(8,128)(2,1)S(1)}, u32[]{:S(2)}, u32[]{:S(2)}) collective-permute-start(bf16[2,320,128]{2,1,0:T(8,128)(2,1)S(1)} %get-tuple-element.50), channel_id=1, source_target_pairs={{0,24},{8,16},{16,8},{24,0},{1,25},{9,17},{17,9},{25,1},{2,26},{10... | collective-permute-start | bytes 491528 | tf_op jit(solution)/shard_map/ppermute | solution.py:543
  18.2 0.3 collective-permute-start.4
  18.5 1.8 %collective-permute-start.5 = (bf16[2,128,128]{2,1,0:T(8,128)(2,1)S(1)}, bf16[2,128,128]{2,1,0:T(8,128)(2,1)S(1)}, u32[]{:S(2)}, u32[]{:S(2)}) collective-permute-start(bf16[2,128,128]{2,1,0:T(8,128)(2,1)S(1)} %get-tuple-element.52), channel_id=1, source_target_pairs={{0,16},{8,24},{16,0},{24,8},{1,17},{9,25},{17,1},{25,9},{2,18},{10... | collective-permute-start | bytes 196616 | tf_op jit(solution)/shard_map/ppermute | solution.py:543
  20.3 1.2 %shard_map.78 = (bf16[512,128]{1,0:T(8,128)(2,1)}, f32[2,512,128]{2,1,0:T(8,128)S(1)}, bf16[512,128]{1,0:T(8,128)(2,1)S(1)}) custom-call(bf16[4,512,128]{2,1,0:T(8,128)(2,1)S(1)} %get-tuple-element.37.held.refs_0_, f32[3,512,128]{2,1,0:T(8,128)S(1)} %get-tuple-element.44.back, f32[512,128]{1,0:T(8,128)S(1)} %get-tuple-element.45.partial_ref, ...), custom_call_target="tpu_custom_call" | custom-call | flops 209715200 | bytes 1048576 | tf_op jit(solution)/shard_map/pallas_call | solution.py:527
  21.5 2.0 %collective-permute-done.5.refs_2_ = bf16[2,128,128]{2,1,0:T(8,128)(2,1)S(1)} collective-permute-done((bf16[2,128,128]{2,1,0:T(8,128)(2,1)S(1)}, bf16[2,128,128]{2,1,0:T(8,128)(2,1)S(1)}, u32[]{:S(2)}, u32[]{:S(2)}) %collective-permute-start.5) | collective-permute-done | bytes 65568 | tf_op jit(solution)/shard_map/ppermute | solution.py:543
  23.5 1.0 %collective-permute-done.3.refs_0_ = bf16[2,320,128]{2,1,0:T(8,128)(2,1)S(1)} collective-permute-done((bf16[2,320,128]{2,1,0:T(8,128)(2,1)S(1)}, bf16[2,320,128]{2,1,0:T(8,128)(2,1)S(1)}, u32[]{:S(2)}, u32[]{:S(2)}) %collective-permute-start.3) | collective-permute-done | bytes 163872 | tf_op jit(solution)/shard_map/ppermute | solution.py:543
  24.5 0.9 %collective-permute-done.4.refs_1_ = bf16[2,320,128]{2,1,0:T(8,128)(2,1)S(1)} collective-permute-done((bf16[2,320,128]{2,1,0:T(8,128)(2,1)S(1)}, bf16[2,320,128]{2,1,0:T(8,128)(2,1)S(1)}, u32[]{:S(2)}, u32[]{:S(2)}) %collective-permute-start.4) | collective-permute-done | bytes 163872 | tf_op jit(solution)/shard_map/ppermute | solution.py:543
  25.4 0.2 shard_map.79
  25.6 2.5 %collective-permute-start.8 = (bf16[2,3,64,128]{3,2,1,0:T(8,128)(2,1)S(1)}, bf16[2,3,64,128]{3,2,1,0:T(8,128)(2,1)S(1)}, u32[]{:S(2)}, u32[]{:S(2)}) collective-permute-start(bf16[2,3,64,128]{3,2,1,0:T(8,128)(2,1)S(1)} %get-tuple-element.56), channel_id=1, source_target_pairs={{0,4},{1,5},{2,6},{3,7},{4,0},{5,1},{6,2},{7,3},{8,12},{9,13},{10,... | collective-permute-start | bytes 294920 | tf_op jit(solution)/shard_map/ppermute | solution.py:543
  28.2 1.3 %collective-permute-start.9 = (bf16[2,3,64,128]{3,2,1,0:T(8,128)(2,1)S(1)}, bf16[2,3,64,128]{3,2,1,0:T(8,128)(2,1)S(1)}, u32[]{:S(2)}, u32[]{:S(2)}) collective-permute-start(bf16[2,3,64,128]{3,2,1,0:T(8,128)(2,1)S(1)} %get-tuple-element.57), channel_id=1, source_target_pairs={{0,6},{1,7},{2,4},{3,5},{4,2},{5,3},{6,0},{7,1},{8,14},{9,15},{10,... | collective-permute-start | bytes 294920 | tf_op jit(solution)/shard_map/ppermute | solution.py:543
  29.5 0.2 collective-permute-start.6
  29.7 1.9 %collective-permute-start.10 = (bf16[3,64,128]{2,1,0:T(8,128)(2,1)S(1)}, bf16[3,64,128]{2,1,0:T(8,128)(2,1)S(1)}, u32[]{:S(2)}, u32[]{:S(2)}) collective-permute-start(bf16[3,64,128]{2,1,0:T(8,128)(2,1)S(1)} %get-tuple-element.58), channel_id=1, source_target_pairs={{0,1},{1,0},{2,3},{3,2},{4,5},{5,4},{6,7},{7,6},{8,9},{9,8},{10,11... | collective-permute-start | bytes 147464 | tf_op jit(solution)/shard_map/ppermute | solution.py:543
  31.6 3.9 %collective-permute-done.6.refs_1_ = bf16[3,64,128]{2,1,0:T(8,128)(2,1)S(1)} collective-permute-done((bf16[3,64,128]{2,1,0:T(8,128)(2,1)S(1)}, bf16[3,64,128]{2,1,0:T(8,128)(2,1)S(1)}, u32[]{:S(2)}, u32[]{:S(2)}) %collective-permute-start.6) | collective-permute-done | bytes 49184 | tf_op jit(solution)/shard_map/ppermute | solution.py:543
  35.6 0.4 %collective-permute-start.11 = (bf16[6,64,128]{2,1,0:T(8,128)(2,1)S(1)}, bf16[6,64,128]{2,1,0:T(8,128)(2,1)S(1)}, u32[]{:S(2)}, u32[]{:S(2)}) collective-permute-start(bf16[6,64,128]{2,1,0:T(8,128)(2,1)S(1)} %pad_maximum_fusion), channel_id=1, source_target_pairs={{0,1},{1,0},{2,3},{3,2},{4,5},{5,4},{6,7},{7,6},{8,9},{9,8},{10,11... | collective-permute-start | bytes 294920 | tf_op jit(solution)/shard_map/ppermute | solution.py:543
  36.0 0.8 %shard_map.80 = (bf16[64,1024]{1,0:T(8,128)(2,1)}, bf16[64,1024]{1,0:T(8,128)(2,1)}, bf16[64,1024]{1,0:T(8,128)(2,1)}) custom-call(bf16[3,64,128]{2,1,0:T(8,128)(2,1)S(1)} %get-tuple-element.53.refs_0_, bf16[3,64,128]{2,1,0:T(8,128)(2,1)S(1)} %collective-permute-done.6.refs_1_, bf16[3,64,128]{2,1,0:T(8,128)(2,1)S(1)} %collective-permute-done.7.refs_2_, ...), custom_call_target="tpu_custom_call" | custom-call | flops 209715200 | bytes 1048576 | tf_op jit(solution)/shard_map/pallas_call | solution.py:527
  36.9 0.1 collective-permute-done.11.refs_3_
  37.0 0.7 %shard_map.81 = (bf16[64,1024]{1,0:T(8,128)(2,1)}, bf16[64,1024]{1,0:T(8,128)(2,1)}, bf16[64,1024]{1,0:T(8,128)(2,1)}) custom-call(bf16[64,1024]{1,0:T(8,128)(2,1)} %get-tuple-element.64.refs_0_, bf16[64,1024]{1,0:T(8,128)(2,1)} %get-tuple-element.65.refs_1_, ...), custom_call_target="tpu_custom_call", output_to_operand_aliasing={{0}: (0, {}), {1}: (1, {}), {2}: (2, {})} | custom-call | bytes 1048576 | tf_op jit(solution)/shard_map/pallas_call | solution.py:527
  (9 shorter events, 0.1 us)
Async XLA Ops:
  1.8 9.6 %collective-permute-start = (bf16[2,320,128]{2,1,0:T(8,128)(2,1)S(1)}, bf16[2,320,128]{2,1,0:T(8,128)(2,1)S(1)}, u32[]{:S(2)}, u32[]{:S(2)}) collective-permute-start(bf16[2,320,128]{2,1,0:T(8,128)(2,1)S(1)} %get-tuple-element.41), channel_id=1, source_target_pairs={{0,24},{8,16},{16,8},{24,0},{1,25},{9,17},{17,9},{25,1},{2,26},{10... | collective-permute-start | bytes 491528 | tf_op jit(solution)/shard_map/ppermute | solution.py:543
  5.7 8.0 %collective-permute-start.1 = (bf16[2,320,128]{2,1,0:T(8,128)(2,1)S(1)}, bf16[2,320,128]{2,1,0:T(8,128)(2,1)S(1)}, u32[]{:S(2)}, u32[]{:S(2)}) collective-permute-start(bf16[2,320,128]{2,1,0:T(8,128)(2,1)S(1)} %get-tuple-element.42), channel_id=1, source_target_pairs={{0,8},{8,0},{16,24},{24,16},{1,9},{9,1},{17,25},{25,17},{2,10},{10... | collective-permute-start | bytes 491528 | tf_op jit(solution)/shard_map/ppermute | solution.py:543
  6.3 5.1 %collective-permute-start.2 = (bf16[2,128,128]{2,1,0:T(8,128)(2,1)S(1)}, bf16[2,128,128]{2,1,0:T(8,128)(2,1)S(1)}, u32[]{:S(2)}, u32[]{:S(2)}) collective-permute-start(bf16[2,128,128]{2,1,0:T(8,128)(2,1)S(1)} %get-tuple-element.43), channel_id=1, source_target_pairs={{0,16},{8,24},{16,0},{24,8},{1,17},{9,25},{17,1},{25,9},{2,18},{10... | collective-permute-start | bytes 196616 | tf_op jit(solution)/shard_map/ppermute | solution.py:543
  16.7 7.8 %collective-permute-start.3 = (bf16[2,320,128]{2,1,0:T(8,128)(2,1)S(1)}, bf16[2,320,128]{2,1,0:T(8,128)(2,1)S(1)}, u32[]{:S(2)}, u32[]{:S(2)}) collective-permute-start(bf16[2,320,128]{2,1,0:T(8,128)(2,1)S(1)} %get-tuple-element.50), channel_id=1, source_target_pairs={{0,24},{8,16},{16,8},{24,0},{1,25},{9,17},{17,9},{25,1},{2,26},{10... | collective-permute-start | bytes 491528 | tf_op jit(solution)/shard_map/ppermute | solution.py:543
  18.2 7.2 %collective-permute-start.4 = (bf16[2,320,128]{2,1,0:T(8,128)(2,1)S(1)}, bf16[2,320,128]{2,1,0:T(8,128)(2,1)S(1)}, u32[]{:S(2)}, u32[]{:S(2)}) collective-permute-start(bf16[2,320,128]{2,1,0:T(8,128)(2,1)S(1)} %get-tuple-element.51), channel_id=1, source_target_pairs={{0,8},{8,0},{16,24},{24,16},{1,9},{9,1},{17,25},{25,17},{2,10},{10... | collective-permute-start | bytes 491528 | tf_op jit(solution)/shard_map/ppermute | solution.py:543
  18.5 5.0 %collective-permute-start.5 = (bf16[2,128,128]{2,1,0:T(8,128)(2,1)S(1)}, bf16[2,128,128]{2,1,0:T(8,128)(2,1)S(1)}, u32[]{:S(2)}, u32[]{:S(2)}) collective-permute-start(bf16[2,128,128]{2,1,0:T(8,128)(2,1)S(1)} %get-tuple-element.52), channel_id=1, source_target_pairs={{0,16},{8,24},{16,0},{24,8},{1,17},{9,25},{17,1},{25,9},{2,18},{10... | collective-permute-start | bytes 196616 | tf_op jit(solution)/shard_map/ppermute | solution.py:543
  25.6 10.0 %collective-permute-start.8 = (bf16[2,3,64,128]{3,2,1,0:T(8,128)(2,1)S(1)}, bf16[2,3,64,128]{3,2,1,0:T(8,128)(2,1)S(1)}, u32[]{:S(2)}, u32[]{:S(2)}) collective-permute-start(bf16[2,3,64,128]{3,2,1,0:T(8,128)(2,1)S(1)} %get-tuple-element.56), channel_id=1, source_target_pairs={{0,4},{1,5},{2,6},{3,7},{4,0},{5,1},{6,2},{7,3},{8,12},{9,13},{10,... | collective-permute-start | bytes 294920 | tf_op jit(solution)/shard_map/ppermute | solution.py:543
  28.2 7.4 %collective-permute-start.9 = (bf16[2,3,64,128]{3,2,1,0:T(8,128)(2,1)S(1)}, bf16[2,3,64,128]{3,2,1,0:T(8,128)(2,1)S(1)}, u32[]{:S(2)}, u32[]{:S(2)}) collective-permute-start(bf16[2,3,64,128]{3,2,1,0:T(8,128)(2,1)S(1)} %get-tuple-element.57), channel_id=1, source_target_pairs={{0,6},{1,7},{2,4},{3,5},{4,2},{5,3},{6,0},{7,1},{8,14},{9,15},{10,... | collective-permute-start | bytes 294920 | tf_op jit(solution)/shard_map/ppermute | solution.py:543
  29.5 6.1 %collective-permute-start.6 = (bf16[3,64,128]{2,1,0:T(8,128)(2,1)S(1)}, bf16[3,64,128]{2,1,0:T(8,128)(2,1)S(1)}, u32[]{:S(2)}, u32[]{:S(2)}) collective-permute-start(bf16[3,64,128]{2,1,0:T(8,128)(2,1)S(1)} %get-tuple-element.54), channel_id=1, source_target_pairs={{0,2},{1,3},{2,0},{3,1},{4,6},{5,7},{6,4},{7,5},{8,10},{9,11},{10,... | collective-permute-start | bytes 147464 | tf_op jit(solution)/shard_map/ppermute | solution.py:543
  29.7 5.8 %collective-permute-start.7 = (bf16[3,64,128]{2,1,0:T(8,128)(2,1)S(1)}, bf16[3,64,128]{2,1,0:T(8,128)(2,1)S(1)}, u32[]{:S(2)}, u32[]{:S(2)}) collective-permute-start(bf16[3,64,128]{2,1,0:T(8,128)(2,1)S(1)} %get-tuple-element.55), channel_id=1, source_target_pairs={{0,3},{1,2},{2,1},{3,0},{4,7},{5,6},{6,5},{7,4},{8,11},{9,10},{10,... | collective-permute-start | bytes 147464 | tf_op jit(solution)/shard_map/ppermute | solution.py:543
  29.7 5.8 %collective-permute-start.10 = (bf16[3,64,128]{2,1,0:T(8,128)(2,1)S(1)}, bf16[3,64,128]{2,1,0:T(8,128)(2,1)S(1)}, u32[]{:S(2)}, u32[]{:S(2)}) collective-permute-start(bf16[3,64,128]{2,1,0:T(8,128)(2,1)S(1)} %get-tuple-element.58), channel_id=1, source_target_pairs={{0,1},{1,0},{2,3},{3,2},{4,5},{5,4},{6,7},{7,6},{8,9},{9,8},{10,11... | collective-permute-start | bytes 147464 | tf_op jit(solution)/shard_map/ppermute | solution.py:543
  35.6 1.4 %collective-permute-start.11 = (bf16[6,64,128]{2,1,0:T(8,128)(2,1)S(1)}, bf16[6,64,128]{2,1,0:T(8,128)(2,1)S(1)}, u32[]{:S(2)}, u32[]{:S(2)}) collective-permute-start(bf16[6,64,128]{2,1,0:T(8,128)(2,1)S(1)} %pad_maximum_fusion), channel_id=1, source_target_pairs={{0,1},{1,0},{2,3},{3,2},{4,5},{5,4},{6,7},{7,6},{8,9},{9,8},{10,11... | collective-permute-start | bytes 294920 | tf_op jit(solution)/shard_map/ppermute | solution.py:543

commit v5 on v4

--- a/solution.py
+++ b/solution.py
@@ -56,11 +56,16 @@
 
 
 def paired(head_count):
-    return list(range(4, head_count, 2))
+    return list(range(4, head_count - 2, 2))
 
 
 def head_order(head_count):
-    return [d for d in [2, 3] + paired(head_count) + [1] if d < head_count]
+    far = [d for d in (head_count - 2, head_count - 1) if d >= 4]
+    return [d for d in paired(head_count) + [2, 3] + far + [1] if d < head_count]
+
+
+def last_heads(head_count):
+    return [d for d in head_order(head_count) if d in (1, head_count - 2, head_count - 1)]
 
 
 def prep_kernel(seq_count, *refs):
@@ -501,23 +506,23 @@
     parts, outs = refs[:-3], refs[-3:]
     head_index = lax.axis_index("head")
     width = parts[0].shape[-1]
-    for d, part in zip([0] + head_order(head_count), parts):
+    first = [d for d in head_order(head_count) if d not in last_heads(head_count)]
+    for d, part in zip([0] + first, parts):
         at = pl.ds(pl.multiple_of((head_index ^ d) * width, width), width)
         for i in range(3):
             outs[i][:, at] = part[0, i] if d in paired(head_count) else part[i]
 
 
 def place_late_kernel(head_count, *refs):
-    late, outs, sems = refs[3], refs[4:7], refs[7]
+    parts, outs, sems = refs[3:-4], refs[-4:-1], refs[-1]
     head_index = lax.axis_index("head")
-    width = late.shape[-1]
-    far = [d for d in head_order(head_count) if d in paired(head_count)]
+    width = parts[0].shape[-1]
     copies = []
-    for row, d in enumerate(far):
-        at = pl.ds(pl.multiple_of((head_index ^ d ^ 1) * width, width), width)
+    far = [d + 1 for d in head_order(head_count) if d in paired(head_count)]
+    for k, (d, part) in enumerate(zip(last_heads(head_count) + far, parts)):
+        at = pl.ds(pl.multiple_of((head_index ^ d) * width, width), width)
         for i in range(3):
-            k = 3 * row + i
-            copies.append(pltpu.make_async_copy(late.at[k], outs[i].at[:, at], sems.at[k]))
+            copies.append(pltpu.make_async_copy(part.at[i], outs[i].at[:, at], sems.at[k, i]))
             copies[-1].start()
     for copy in copies:
         copy.wait()
@@ -626,22 +631,23 @@
         [f32(2, rows, width), f32(2, rows // 2, width), f32(2, rows // 4, width)],
         (grad_query, local, *returned),
     )
-    parts = lax.optimization_barrier(swap_all(parts, "head", order))
-    far = [part[1] for d, part in zip(order, parts) if d in paired(head_count)]
-    late = swap_all([jnp.concatenate(far, axis=0)] if far else [], "head", [1])
+    parts = dict(zip(order, swap_all(parts, "head", order)))
+    far = [parts[d][1] for d in order if d in paired(head_count)]
+    late = swap_all(far, "head", [1] * len(far))
+    last = [parts.pop(d) for d in last_heads(head_count)] + late
     grads = call(
         functools.partial(place_kernel, head_count),
         [shape(share, head_count * width)] * 3,
         [],
-        (own, *parts),
+        (own, *parts.values()),
         flops=50 * unit_flops,
     )
-    if late:
+    if last:
         grads = call(
             functools.partial(place_late_kernel, head_count),
             [shape(share, head_count * width)] * 3,
-            [pltpu.SemaphoreType.DMA((3 * len(far),))],
-            (*grads, *late),
+            [pltpu.SemaphoreType.DMA((len(last), 3))],
+            (*grads, *last),
             in_hbm=3,
             hbm_outs=3,
             aliases={0: 0, 1: 1, 2: 2},

time: 37.8 us -> 37.3 us (0.987)
  waiting for transfers between devices: 14.2 us -> 11.7 us
  starting transfers between devices: 14.6 us -> 16.5 us
    ppermute x12 -> x13, waiting for transfers between devices: 14.2 us -> 11.7 us  [swap_all(): lax.ppermute(x, axis, [(i, i ^ d) for i in range(size)])]
    ppermute x12 -> x13, starting transfers between devices: 14.6 us -> 16.5 us  [swap_all(): lax.ppermute(x, axis, [(i, i ^ d) for i in range(size)])]
  transfers between devices with their start and end apart: 12 -> 13, of which waited for: 7 -> 7; matrix products, arithmetic and copies ran while one was open for 0% -> 0% of each run, Pallas kernels for 8% -> 8%
where the time goes in v5:
time: 37.3 us; the launch traced here: 37.1 us
  starting transfers between devices  16.5 us (44%)
  waiting for transfers between devices  11.7 us (31%)
  Pallas kernels  8.22 us (22%)
  between operations  0.68 us (2%)
    ppermute x13, starting transfers between devices, swap_all(): lax.ppermute(x, axis, [(i, i ^ d) for i in range(size)])  16.5 us
    ppermute x13, waiting for transfers between devices, swap_all(): lax.ppermute(x, axis, [(i, i ^ d) for i in range(size)])  11.7 us
    pallas_call x7, Pallas kernels, call(): pl.pallas_call(kernel, out_shape=outs, in_specs=[pl.BlockSpec(memory_spac...  8.22 us
  transfers between devices with their start and end apart: 13, of which 7 were waited for; matrix products, arithmetic and copies ran while one was open for 0% of the time, Pallas kernels for 8%

profile of v5, /device:TPU:0, one launch (start us, length us, event | category | flops | bytes accessed | tf_op | source)
XLA Modules:
  0.0 37.1 jit_solution(10527823499462460304)
XLA Ops:
  0.6 1.1 %shard_map.75 = (bf16[4,512,128]{2,1,0:T(8,128)(2,1)S(1)}, bf16[2,320,128]{2,1,0:T(8,128)(2,1)S(1)}, bf16[2,320,128]{2,1,0:T(8,128)(2,1)S(1)}, bf16[2,128,128]{2,1,0:T(8,128)(2,1)S(1)}) custom-call(bf16[512,128]{1,0:T(8,128)(2,1)} %refs_0_.1, bf16[512,128]{1,0:T(8,128)(2,1)} %refs_1_.1, bf16[512,128]{1,0:T(8,128)(2,1)} %refs_2_.1, bf16[512,128]{1,0:T(8,128)(2,1)} %refs_3_.1), custom_call_target="tpu_custom_call" | custom-call | bytes 1048576 | tf_op jit(solution)/shard_map/pallas_call | solution.py:532
  1.8 4.0 %collective-permute-start = (bf16[2,320,128]{2,1,0:T(8,128)(2,1)S(1)}, bf16[2,320,128]{2,1,0:T(8,128)(2,1)S(1)}, u32[]{:S(2)}, u32[]{:S(2)}) collective-permute-start(bf16[2,320,128]{2,1,0:T(8,128)(2,1)S(1)} %get-tuple-element.37), channel_id=1, source_target_pairs={{0,24},{8,16},{16,8},{24,0},{1,25},{9,17},{17,9},{25,1},{2,26},{10... | collective-permute-start | bytes 491528 | tf_op jit(solution)/shard_map/ppermute | solution.py:548
  5.7 0.5 %collective-permute-start.1 = (bf16[2,320,128]{2,1,0:T(8,128)(2,1)S(1)}, bf16[2,320,128]{2,1,0:T(8,128)(2,1)S(1)}, u32[]{:S(2)}, u32[]{:S(2)}) collective-permute-start(bf16[2,320,128]{2,1,0:T(8,128)(2,1)S(1)} %get-tuple-element.38), channel_id=1, source_target_pairs={{0,8},{8,0},{16,24},{24,16},{1,9},{9,1},{17,25},{25,17},{2,10},{10... | collective-permute-start | bytes 491528 | tf_op jit(solution)/shard_map/ppermute | solution.py:548
  6.4 1.1 %shard_map.76 = (f32[3,512,128]{2,1,0:T(8,128)S(1)}, bf16[256,128]{1,0:T(8,128)(2,1)S(1)}, bf16[128,128]{1,0:T(8,128)(2,1)S(1)}) custom-call(bf16[4,512,128]{2,1,0:T(8,128)(2,1)S(1)} %get-tuple-element.33.held.refs_0_), custom_call_target="tpu_custom_call" | custom-call | flops 83886080 | bytes 1048576 | tf_op jit(solution)/shard_map/pallas_call | solution.py:532
  7.5 3.8 %collective-permute-done.2.refs_6_ = bf16[2,128,128]{2,1,0:T(8,128)(2,1)S(1)} collective-permute-done((bf16[2,128,128]{2,1,0:T(8,128)(2,1)S(1)}, bf16[2,128,128]{2,1,0:T(8,128)(2,1)S(1)}, u32[]{:S(2)}, u32[]{:S(2)}) %collective-permute-start.2) | collective-permute-done | bytes 65568 | tf_op jit(solution)/shard_map/ppermute | solution.py:548
  11.3 2.4 %collective-permute-done.1.refs_5_ = bf16[2,320,128]{2,1,0:T(8,128)(2,1)S(1)} collective-permute-done((bf16[2,320,128]{2,1,0:T(8,128)(2,1)S(1)}, bf16[2,320,128]{2,1,0:T(8,128)(2,1)S(1)}, u32[]{:S(2)}, u32[]{:S(2)}) %collective-permute-start.1) | collective-permute-done | bytes 163872 | tf_op jit(solution)/shard_map/ppermute | solution.py:548
  13.7 3.0 %shard_map.77 = (bf16[512,128]{1,0:T(8,128)(2,1)S(1)}, bf16[2,320,128]{2,1,0:T(8,128)(2,1)S(1)}, bf16[2,320,128]{2,1,0:T(8,128)(2,1)S(1)}, bf16[2,128,128]{2,1,0...) custom-call(bf16[4,512,128]{2,1,0:T(8,128)(2,1)S(1)} %get-tuple-element.33.held.refs_0_, ...), custom_call_target="tpu_custom_call" | custom-call | flops 293601280 | bytes 1048576 | tf_op jit(solution)/shard_map/pallas_call | solution.py:532
  16.7 1.5 %collective-permute-start.3 = (bf16[2,320,128]{2,1,0:T(8,128)(2,1)S(1)}, bf16[2,320,128]{2,1,0:T(8,128)(2,1)S(1)}, u32[]{:S(2)}, u32[]{:S(2)}) collective-permute-start(bf16[2,320,128]{2,1,0:T(8,128)(2,1)S(1)} %get-tuple-element.46), channel_id=1, source_target_pairs={{0,24},{8,16},{16,8},{24,0},{1,25},{9,17},{17,9},{25,1},{2,26},{10... | collective-permute-start | bytes 491528 | tf_op jit(solution)/shard_map/ppermute | solution.py:548
  18.2 0.3 collective-permute-start.4
  18.5 1.8 %collective-permute-start.5 = (bf16[2,128,128]{2,1,0:T(8,128)(2,1)S(1)}, bf16[2,128,128]{2,1,0:T(8,128)(2,1)S(1)}, u32[]{:S(2)}, u32[]{:S(2)}) collective-permute-start(bf16[2,128,128]{2,1,0:T(8,128)(2,1)S(1)} %get-tuple-element.48), channel_id=1, source_target_pairs={{0,16},{8,24},{16,0},{24,8},{1,17},{9,25},{17,1},{25,9},{2,18},{10... | collective-permute-start | bytes 196616 | tf_op jit(solution)/shard_map/ppermute | solution.py:548
  20.3 1.2 %shard_map.78 = (bf16[512,128]{1,0:T(8,128)(2,1)}, f32[2,512,128]{2,1,0:T(8,128)S(1)}, bf16[512,128]{1,0:T(8,128)(2,1)S(1)}) custom-call(bf16[4,512,128]{2,1,0:T(8,128)(2,1)S(1)} %get-tuple-element.33.held.refs_0_, f32[3,512,128]{2,1,0:T(8,128)S(1)} %get-tuple-element.40.back, f32[512,128]{1,0:T(8,128)S(1)} %get-tuple-element.41.partial_ref, ...), custom_call_target="tpu_custom_call" | custom-call | flops 209715200 | bytes 1048576 | tf_op jit(solution)/shard_map/pallas_call | solution.py:532
  21.5 2.0 %collective-permute-done.5.refs_2_ = bf16[2,128,128]{2,1,0:T(8,128)(2,1)S(1)} collective-permute-done((bf16[2,128,128]{2,1,0:T(8,128)(2,1)S(1)}, bf16[2,128,128]{2,1,0:T(8,128)(2,1)S(1)}, u32[]{:S(2)}, u32[]{:S(2)}) %collective-permute-start.5) | collective-permute-done | bytes 65568 | tf_op jit(solution)/shard_map/ppermute | solution.py:548
  23.5 1.0 %collective-permute-done.3.refs_0_ = bf16[2,320,128]{2,1,0:T(8,128)(2,1)S(1)} collective-permute-done((bf16[2,320,128]{2,1,0:T(8,128)(2,1)S(1)}, bf16[2,320,128]{2,1,0:T(8,128)(2,1)S(1)}, u32[]{:S(2)}, u32[]{:S(2)}) %collective-permute-start.3) | collective-permute-done | bytes 163872 | tf_op jit(solution)/shard_map/ppermute | solution.py:548
  24.5 0.9 %collective-permute-done.4.refs_1_ = bf16[2,320,128]{2,1,0:T(8,128)(2,1)S(1)} collective-permute-done((bf16[2,320,128]{2,1,0:T(8,128)(2,1)S(1)}, bf16[2,320,128]{2,1,0:T(8,128)(2,1)S(1)}, u32[]{:S(2)}, u32[]{:S(2)}) %collective-permute-start.4) | collective-permute-done | bytes 163872 | tf_op jit(solution)/shard_map/ppermute | solution.py:548
  25.4 0.2 shard_map.79
  25.6 2.5 %collective-permute-start.6 = (bf16[2,3,64,128]{3,2,1,0:T(8,128)(2,1)S(1)}, bf16[2,3,64,128]{3,2,1,0:T(8,128)(2,1)S(1)}, u32[]{:S(2)}, u32[]{:S(2)}) collective-permute-start(bf16[2,3,64,128]{3,2,1,0:T(8,128)(2,1)S(1)} %get-tuple-element.50), channel_id=1, source_target_pairs={{0,4},{1,5},{2,6},{3,7},{4,0},{5,1},{6,2},{7,3},{8,12},{9,13},{10,... | collective-permute-start | bytes 294920 | tf_op jit(solution)/shard_map/ppermute | solution.py:548
  28.2 1.6 %collective-permute-start.7 = (bf16[3,64,128]{2,1,0:T(8,128)(2,1)S(1)}, bf16[3,64,128]{2,1,0:T(8,128)(2,1)S(1)}, u32[]{:S(2)}, u32[]{:S(2)}) collective-permute-start(bf16[3,64,128]{2,1,0:T(8,128)(2,1)S(1)} %get-tuple-element.51), channel_id=1, source_target_pairs={{0,2},{1,3},{2,0},{3,1},{4,6},{5,7},{6,4},{7,5},{8,10},{9,11},{10,... | collective-permute-start | bytes 147464 | tf_op jit(solution)/shard_map/ppermute | solution.py:548
  29.7 0.3 collective-permute-start.9
  30.1 3.4 %collective-permute-start.10 = (bf16[3,64,128]{2,1,0:T(8,128)(2,1)S(1)}, bf16[3,64,128]{2,1,0:T(8,128)(2,1)S(1)}, u32[]{:S(2)}, u32[]{:S(2)}) collective-permute-start(bf16[3,64,128]{2,1,0:T(8,128)(2,1)S(1)} %get-tuple-element.57), channel_id=1, source_target_pairs={{0,7},{1,6},{2,5},{3,4},{4,3},{5,2},{6,1},{7,0},{8,15},{9,14},{10,... | collective-permute-start | bytes 147464 | tf_op jit(solution)/shard_map/ppermute | solution.py:548
  33.4 0.2 collective-permute-start.11
  33.7 0.3 collective-permute-start.12
  34.0 0.8 %shard_map.80 = (bf16[64,1024]{1,0:T(8,128)(2,1)}, bf16[64,1024]{1,0:T(8,128)(2,1)}, bf16[64,1024]{1,0:T(8,128)(2,1)}) custom-call(bf16[3,64,128]{2,1,0:T(8,128)(2,1)S(1)} %get-tuple-element.49.refs_0_, bf16[2,3,64,128]{3,2,1,0:T(8,128)(2,1)S(1)} %collective-permute-done.6.refs_1_, bf16[3,64,128]{2,1,0:T(8,128)(2,1)S(1)} %collective-permute-done.7.refs_2_, ...), custom_call_target="tpu_custom_call" | custom-call | flops 209715200 | bytes 1048576 | tf_op jit(solution)/shard_map/pallas_call | solution.py:532
  34.8 1.3 %collective-permute-done.9.refs_3_ = bf16[3,64,128]{2,1,0:T(8,128)(2,1)S(1)} collective-permute-done((bf16[3,64,128]{2,1,0:T(8,128)(2,1)S(1)}, bf16[3,64,128]{2,1,0:T(8,128)(2,1)S(1)}, u32[]{:S(2)}, u32[]{:S(2)}) %collective-permute-start.9) | collective-permute-done | bytes 49184 | tf_op jit(solution)/shard_map/ppermute | solution.py:548
  36.4 0.8 %shard_map.81 = (bf16[64,1024]{1,0:T(8,128)(2,1)}, bf16[64,1024]{1,0:T(8,128)(2,1)}, bf16[64,1024]{1,0:T(8,128)(2,1)}) custom-call(bf16[64,1024]{1,0:T(8,128)(2,1)} %get-tuple-element.53.refs_0_, bf16[64,1024]{1,0:T(8,128)(2,1)} %get-tuple-element.54.refs_1_, ...), custom_call_target="tpu_custom_call", output_to_operand_aliasing={{0}: (0, {}), {1}: (1, {}), {2}: (2, {})} | custom-call | bytes 1048576 | tf_op jit(solution)/shard_map/pallas_call | solution.py:532
  (10 shorter events, 0.3 us)
Async XLA Ops:
  1.8 9.6 %collective-permute-start = (bf16[2,320,128]{2,1,0:T(8,128)(2,1)S(1)}, bf16[2,320,128]{2,1,0:T(8,128)(2,1)S(1)}, u32[]{:S(2)}, u32[]{:S(2)}) collective-permute-start(bf16[2,320,128]{2,1,0:T(8,128)(2,1)S(1)} %get-tuple-element.37), channel_id=1, source_target_pairs={{0,24},{8,16},{16,8},{24,0},{1,25},{9,17},{17,9},{25,1},{2,26},{10... | collective-permute-start | bytes 491528 | tf_op jit(solution)/shard_map/ppermute | solution.py:548
  5.7 8.0 %collective-permute-start.1 = (bf16[2,320,128]{2,1,0:T(8,128)(2,1)S(1)}, bf16[2,320,128]{2,1,0:T(8,128)(2,1)S(1)}, u32[]{:S(2)}, u32[]{:S(2)}) collective-permute-start(bf16[2,320,128]{2,1,0:T(8,128)(2,1)S(1)} %get-tuple-element.38), channel_id=1, source_target_pairs={{0,8},{8,0},{16,24},{24,16},{1,9},{9,1},{17,25},{25,17},{2,10},{10... | collective-permute-start | bytes 491528 | tf_op jit(solution)/shard_map/ppermute | solution.py:548
  6.3 5.1 %collective-permute-start.2 = (bf16[2,128,128]{2,1,0:T(8,128)(2,1)S(1)}, bf16[2,128,128]{2,1,0:T(8,128)(2,1)S(1)}, u32[]{:S(2)}, u32[]{:S(2)}) collective-permute-start(bf16[2,128,128]{2,1,0:T(8,128)(2,1)S(1)} %get-tuple-element.39), channel_id=1, source_target_pairs={{0,16},{8,24},{16,0},{24,8},{1,17},{9,25},{17,1},{25,9},{2,18},{10... | collective-permute-start | bytes 196616 | tf_op jit(solution)/shard_map/ppermute | solution.py:548
  16.7 7.8 %collective-permute-start.3 = (bf16[2,320,128]{2,1,0:T(8,128)(2,1)S(1)}, bf16[2,320,128]{2,1,0:T(8,128)(2,1)S(1)}, u32[]{:S(2)}, u32[]{:S(2)}) collective-permute-start(bf16[2,320,128]{2,1,0:T(8,128)(2,1)S(1)} %get-tuple-element.46), channel_id=1, source_target_pairs={{0,24},{8,16},{16,8},{24,0},{1,25},{9,17},{17,9},{25,1},{2,26},{10... | collective-permute-start | bytes 491528 | tf_op jit(solution)/shard_map/ppermute | solution.py:548
  18.2 7.2 %collective-permute-start.4 = (bf16[2,320,128]{2,1,0:T(8,128)(2,1)S(1)}, bf16[2,320,128]{2,1,0:T(8,128)(2,1)S(1)}, u32[]{:S(2)}, u32[]{:S(2)}) collective-permute-start(bf16[2,320,128]{2,1,0:T(8,128)(2,1)S(1)} %get-tuple-element.47), channel_id=1, source_target_pairs={{0,8},{8,0},{16,24},{24,16},{1,9},{9,1},{17,25},{25,17},{2,10},{10... | collective-permute-start | bytes 491528 | tf_op jit(solution)/shard_map/ppermute | solution.py:548
  18.5 5.0 %collective-permute-start.5 = (bf16[2,128,128]{2,1,0:T(8,128)(2,1)S(1)}, bf16[2,128,128]{2,1,0:T(8,128)(2,1)S(1)}, u32[]{:S(2)}, u32[]{:S(2)}) collective-permute-start(bf16[2,128,128]{2,1,0:T(8,128)(2,1)S(1)} %get-tuple-element.48), channel_id=1, source_target_pairs={{0,16},{8,24},{16,0},{24,8},{1,17},{9,25},{17,1},{25,9},{2,18},{10... | collective-permute-start | bytes 196616 | tf_op jit(solution)/shard_map/ppermute | solution.py:548
  25.6 7.8 %collective-permute-start.6 = (bf16[2,3,64,128]{3,2,1,0:T(8,128)(2,1)S(1)}, bf16[2,3,64,128]{3,2,1,0:T(8,128)(2,1)S(1)}, u32[]{:S(2)}, u32[]{:S(2)}) collective-permute-start(bf16[2,3,64,128]{3,2,1,0:T(8,128)(2,1)S(1)} %get-tuple-element.50), channel_id=1, source_target_pairs={{0,4},{1,5},{2,6},{3,7},{4,0},{5,1},{6,2},{7,3},{8,12},{9,13},{10,... | collective-permute-start | bytes 294920 | tf_op jit(solution)/shard_map/ppermute | solution.py:548
  28.2 5.5 %collective-permute-start.7 = (bf16[3,64,128]{2,1,0:T(8,128)(2,1)S(1)}, bf16[3,64,128]{2,1,0:T(8,128)(2,1)S(1)}, u32[]{:S(2)}, u32[]{:S(2)}) collective-permute-start(bf16[3,64,128]{2,1,0:T(8,128)(2,1)S(1)} %get-tuple-element.51), channel_id=1, source_target_pairs={{0,2},{1,3},{2,0},{3,1},{4,6},{5,7},{6,4},{7,5},{8,10},{9,11},{10,... | collective-permute-start | bytes 147464 | tf_op jit(solution)/shard_map/ppermute | solution.py:548
  29.7 4.3 %collective-permute-start.8 = (bf16[3,64,128]{2,1,0:T(8,128)(2,1)S(1)}, bf16[3,64,128]{2,1,0:T(8,128)(2,1)S(1)}, u32[]{:S(2)}, u32[]{:S(2)}) collective-permute-start(bf16[3,64,128]{2,1,0:T(8,128)(2,1)S(1)} %get-tuple-element.52), channel_id=1, source_target_pairs={{0,3},{1,2},{2,1},{3,0},{4,7},{5,6},{6,5},{7,4},{8,11},{9,10},{10,... | collective-permute-start | bytes 147464 | tf_op jit(solution)/shard_map/ppermute | solution.py:548
  29.7 6.4 %collective-permute-start.9 = (bf16[3,64,128]{2,1,0:T(8,128)(2,1)S(1)}, bf16[3,64,128]{2,1,0:T(8,128)(2,1)S(1)}, u32[]{:S(2)}, u32[]{:S(2)}) collective-permute-start(bf16[3,64,128]{2,1,0:T(8,128)(2,1)S(1)} %get-tuple-element.56), channel_id=1, source_target_pairs={{0,6},{1,7},{2,4},{3,5},{4,2},{5,3},{6,0},{7,1},{8,14},{9,15},{10,... | collective-permute-start | bytes 147464 | tf_op jit(solution)/shard_map/ppermute | solution.py:548
  30.1 6.3 %collective-permute-start.10 = (bf16[3,64,128]{2,1,0:T(8,128)(2,1)S(1)}, bf16[3,64,128]{2,1,0:T(8,128)(2,1)S(1)}, u32[]{:S(2)}, u32[]{:S(2)}) collective-permute-start(bf16[3,64,128]{2,1,0:T(8,128)(2,1)S(1)} %get-tuple-element.57), channel_id=1, source_target_pairs={{0,7},{1,6},{2,5},{3,4},{4,3},{5,2},{6,1},{7,0},{8,15},{9,14},{10,... | collective-permute-start | bytes 147464 | tf_op jit(solution)/shard_map/ppermute | solution.py:548
  33.4 2.9 %collective-permute-start.11 = (bf16[3,64,128]{2,1,0:T(8,128)(2,1)S(1)}, bf16[3,64,128]{2,1,0:T(8,128)(2,1)S(1)}, u32[]{:S(2)}, u32[]{:S(2)}) collective-permute-start(bf16[3,64,128]{2,1,0:T(8,128)(2,1)S(1)} %get-tuple-element.58), channel_id=1, source_target_pairs={{0,1},{1,0},{2,3},{3,2},{4,5},{5,4},{6,7},{7,6},{8,9},{9,8},{10,11... | collective-permute-start | bytes 147464 | tf_op jit(solution)/shard_map/ppermute | solution.py:548
  33.7 2.7 %collective-permute-start.12 = (bf16[3,64,128]{2,1,0:T(8,128)(2,1)S(1)}, bf16[3,64,128]{2,1,0:T(8,128)(2,1)S(1)}, u32[]{:S(2)}, u32[]{:S(2)}) collective-permute-start(bf16[3,64,128]{2,1,0:T(8,128)(2,1)S(1)} %slice_bitcast_fusion), channel_id=1, source_target_pairs={{0,1},{1,0},{2,3},{3,2},{4,5},{5,4},{6,7},{7,6},{8,9},{9,8},{10,11... | collective-permute-start | bytes 147464 | tf_op jit(solution)/shard_map/ppermute | solution.py:548

commit v6 on v5

--- a/solution.py
+++ b/solution.py
@@ -61,16 +61,17 @@
 
 def head_order(head_count):
     far = [d for d in (head_count - 2, head_count - 1) if d >= 4]
-    return [d for d in paired(head_count) + [2, 3] + far + [1] if d < head_count]
+    return [d for d in paired(head_count) + far[:1] + [2] + far[1:] + [3, 1] if d < head_count]
 
 
 def last_heads(head_count):
-    return [d for d in head_order(head_count) if d in (1, head_count - 2, head_count - 1)]
-
-
-def prep_kernel(seq_count, *refs):
+    return [d for d in head_order(head_count) if d in (1, 3, head_count - 1)]
+
+
+def prep_kernel(seq_count, top_level, *refs):
     sources, refs = refs[:4], refs[4:]
-    held, refs = refs[0], refs[1:]
+    (held, stats), refs = refs[:2], refs[2:]
+    queries, refs = refs[:top_level], refs[top_level:]
     sends, scratches, sems = refs[: seq_count - 1], refs[seq_count - 1 : -1], refs[-1]
     sends = dict(zip(seq_order(seq_count), sends))
     seq_index = lax.axis_index("seq")
@@ -109,6 +110,11 @@
                 out[i, BLOCK:] = level_1[:REST]
 
     copies[0].wait()
+
+    @pl.when(goes_first())
+    def _():
+        fine_work(held, stats, queries, scratches[4:])
+
     copies[3].wait()
 
 
@@ -153,8 +159,7 @@
     return max(a - 1, 0), min(a + 2, blocks)
 
 
-def fine_kernel(held, stats, *refs):
-    levels = len(refs) // 2
+def fine_work(held, stats, queries, scratches):
     blocks, width = held.shape[1] // BLOCK, held.shape[2]
     factor = width ** (-0.5) * LOG2E
     for a in range(blocks):
@@ -167,9 +172,27 @@
         stats[1, rows_of(a)] = row_sum(exps)
         stats[2, rows_of(a)] = nn(exps.astype(BF16), held[2, window])
     query = held[0]
-    for level in range(levels):
-        query = coarse(query, refs[levels + level])
-        refs[level][...] = query
+    for ref, scratch in zip(queries, scratches):
+        query = coarse(query, scratch)
+        ref[...] = query
+
+
+def goes_first():
+    return lax.axis_index("head") % 2 == 0
+
+
+def fine_kernel(held, *refs):
+    count = len(refs) // 3
+    done, (stats, *queries), scratches = refs[: count + 1], refs[count + 1 : -count], refs[-count:]
+
+    @pl.when(goes_first())
+    def _():
+        for ref, source in zip((stats, *queries), done):
+            ref[...] = source[...]
+
+    @pl.when(~goes_first())
+    def _():
+        fine_work(held, stats, queries, scratches)
 
 
 def main_kernel(seq_count, top_level, *refs):
@@ -186,9 +209,8 @@
     (attended_ref,) = take(1)
     sends = dict(zip(seq_order(seq_count), take(seq_count - 1)))
     back, partial_ref = take(2)
-    halo, near = take(2)
-    panels = take(top_level - 1)
-    panel_grads = take(top_level - 1)
+    panels = take(top_level - 1 if top_level > 2 else 0)
+    panel_grads = take(len(panels))
     pools = refs
 
     def pool():
@@ -202,70 +224,70 @@
     factor = scale * LOG2E
     has_prev, has_next = seq_index > 0, seq_index < seq_count - 1
 
-    for panel in panels:
-        panel[...] = jnp.zeros(panel.shape, BF16)
-
-    @pl.when(seq_index == 0)
-    def _():
-        halo[:, :BLOCK] = jnp.zeros((2, BLOCK, width), BF16)
-        near[:, : 2 * BLOCK] = jnp.zeros((2, 2 * BLOCK, width), BF16)
-
-    @pl.when(seq_index == seq_count - 1)
-    def _():
-        halo[:, BLOCK:] = jnp.zeros((2, BLOCK, width), BF16)
-        near[:, 2 * BLOCK :] = jnp.zeros((2, 2 * BLOCK, width), BF16)
-
-    halo_scratch = pool()
-    for d in range(1, seq_count):
-        got = received[d]
-        partner = seq_index ^ d
-        at = pl.ds(pl.multiple_of(partner * BLOCK, BLOCK), BLOCK)
-        if d not in wides:
-            for i in range(2):
-                panels[0][i, at] = got[i]
-            continue
-
-        @pl.when(partner == seq_index - 1)
-        def _():
-            for i in range(2):
-                halo[i, :BLOCK] = got[i, :BLOCK]
-                near[i, :REST] = got[i, BLOCK:]
-                near[i, REST : 2 * BLOCK] = coarse(got[i, :BLOCK], halo_scratch)
-
-        @pl.when(partner == seq_index + 1)
-        def _():
-            for i in range(2):
-                halo[i, BLOCK:] = got[i, :BLOCK]
-                near[i, 2 * BLOCK : 2 * BLOCK + EDGE] = coarse(got[i, :BLOCK], halo_scratch)
-                near[i, 2 * BLOCK + EDGE :] = got[i, BLOCK:]
-
-        @pl.when((partner != seq_index + 1) & (partner != seq_index - 1))
-        def _():
-            for i in range(2):
-                panels[0][i, at] = got[i, :BLOCK]
-
-    panel_scratch = pool()
-    for level in range(3, top_level + 1):
-        for i in range(2):
-            panels[level - 2][i] = coarse(panels[level - 3][i], panel_scratch)
-
-    def window(ref, lo, hi, valid):
-        return ref[0, rows_of(lo, hi - lo)], ref[1, rows_of(lo, hi - lo)], valid, (lo, hi)
+    odd = seq_index % 2 == 1
+    further = wides[1:] or wides
+
+    def is_neighbour(d):
+        return jnp.abs((seq_index ^ d) - seq_index) == 1
+
+    def by_side(near, far):
+        return jnp.where(odd, near, far), jnp.where(odd, far, near)
+
+    edges, nears = [], []
+    for i in range(2):
+        far = received[further[0]][i]
+        for d in further[1:]:
+            far = jnp.where(is_neighbour(d), received[d][i], far)
+        before, after = by_side(received[1][i], far)
+        edges.append((before[:BLOCK], after[:BLOCK]))
+        nears.append(
+            jnp.concatenate(
+                [
+                    before[BLOCK:],
+                    coarse(before[:BLOCK], pool()),
+                    coarse(after[:BLOCK], pool()),
+                    after[BLOCK:],
+                ],
+                axis=0,
+            )
+        )
+
+    def window(lo, hi, valid):
+        return nears[0][rows_of(lo, hi - lo)], nears[1][rows_of(lo, hi - lo)], valid, (lo, hi)
 
     level_pieces = [
-        [[window(halo, 0, 1, has_prev)], [window(halo, 1, 2, has_next)]],
         [
-            [window(near, 0, 1, has_prev), window(near, 2, 4, has_next)],
-            [window(near, 0, 2, has_prev), window(near, 3, 4, has_next)],
+            [(edges[0][side], edges[1][side], valid, (side, side + 1))]
+            for side, valid in enumerate((has_prev, has_next))
+        ],
+        [
+            [window(0, 1, has_prev), window(2, 4, has_next)],
+            [window(0, 2, has_prev), window(3, 4, has_next)],
         ],
     ]
-    for level in range(2, top_level + 1):
+    if top_level == 2:
         pieces = []
-        for index, valid in slots_of(seq_index >> (level - 2), seq_count >> (level - 2)):
-            at = pl.ds(pl.multiple_of(index * BLOCK, BLOCK), BLOCK)
-            panel = panels[level - 2]
-            pieces.append((panel[0, at], panel[1, at], valid, at))
+        for d in range(2, seq_count):
+            valid = ~is_neighbour(d) if d in wides else None
+            pieces.append((received[d][0, :BLOCK], received[d][1, :BLOCK], valid, d))
         level_pieces.append([pieces])
+    else:
+        for panel in panels:
+            panel[...] = jnp.zeros(panel.shape, BF16)
+        for d in range(2, seq_count):
+            at = pl.ds(pl.multiple_of((seq_index ^ d) * BLOCK, BLOCK), BLOCK)
+            for i in range(2):
+                panels[0][i, at] = received[d][i, :BLOCK]
+        panel_scratch = pool()
+        for level in range(2, top_level + 1):
+            panel, pieces = panels[level - 2], []
+            for i in range(2):
+                if level > 2:
+                    panel[i] = coarse(panels[level - 3][i], panel_scratch)
+            for index, valid in slots_of(seq_index >> (level - 2), seq_count >> (level - 2)):
+                at = pl.ds(pl.multiple_of(index * BLOCK, BLOCK), BLOCK)
+                pieces.append((panel[0, at], panel[1, at], valid, at))
+            level_pieces.append([pieces])
     level_queries = [[held[0, rows_of(0)], held[0, rows_of(blocks - 1)]]]
     for level in range(1, top_level + 1):
         query = query_refs[level - 1][...]
@@ -345,6 +367,7 @@
     for panel_grad in panel_grads:
         panel_grad[...] = jnp.zeros(panel_grad.shape, F32)
 
+    device_grads = {d: [None, None] for d in range(2, seq_count)}
     grad_queries = []
     parts_of = [[[[] for _ in range(4)] for _ in range(2)] for _ in range(2)]
     for level in range(top_level, -1, -1):
@@ -366,6 +389,9 @@
                 query_parts.append(nn(score_grad, key))
                 outs = tn(score_grad, query), tn(r, grad_rounded)
                 for i in range(2):
+                    if level >= 2 and top_level == 2:
+                        device_grads[where][i] = outs[i]
+                        continue
                     if level >= 2:
                         panel_grads[level - 2][i, where] += outs[i]
                         continue
@@ -382,42 +408,37 @@
     for a, block in enumerate((0, blocks - 1)):
         partial_ref[rows_of(block)] += grad_queries[-1][a]
 
-    for level in range(top_level, 2, -1):
-        for i in range(2):
-            panel_grads[level - 3][i] += 0.5 * spread(panel_grads[level - 2][i], panel_scratch)
-
-    near_grads = [[total_of(p) for p in parts_of[1][i]] for i in range(2)]
-    halo_grads = [[total_of(p) for p in parts_of[0][i][:2]] for i in range(2)]
-    to_prev = [halo_grads[i][0] + 0.5 * spread(near_grads[i][1][EDGE:], pool()) for i in range(2)]
-    to_next = [halo_grads[i][1] + 0.5 * spread(near_grads[i][2][:EDGE], pool()) for i in range(2)]
-    for d in range(1, seq_count):
-        out = sends[d]
-        partner = seq_index ^ d
-        at = pl.ds(pl.multiple_of(partner * BLOCK, BLOCK), BLOCK)
-        if d not in wides:
+    if top_level > 2:
+        for level in range(top_level, 2, -1):
             for i in range(2):
-                out[i] = panel_grads[0][i, at].astype(BF16)
-            continue
-
-        @pl.when(partner == seq_index - 1)
-        def _():
-            for i in range(2):
-                out[i, :BLOCK] = to_prev[i].astype(BF16)
-                out[i, BLOCK : 2 * BLOCK] = near_grads[i][0].astype(BF16)
-                out[i, 2 * BLOCK :] = near_grads[i][1][:EDGE].astype(BF16)
-
-        @pl.when(partner == seq_index + 1)
-        def _():
-            for i in range(2):
-                out[i, :BLOCK] = to_next[i].astype(BF16)
-                out[i, BLOCK : BLOCK + EDGE] = near_grads[i][2][EDGE:].astype(BF16)
-                out[i, BLOCK + EDGE :] = near_grads[i][3].astype(BF16)
-
-        @pl.when((partner != seq_index + 1) & (partner != seq_index - 1))
-        def _():
-            for i in range(2):
-                out[i, :BLOCK] = panel_grads[0][i, at].astype(BF16)
-                out[i, BLOCK:] = jnp.zeros((REST, width), BF16)
+                panel_grads[level - 3][i] += 0.5 * spread(panel_grads[level - 2][i], panel_scratch)
+        for d in device_grads:
+            at = pl.ds(pl.multiple_of((seq_index ^ d) * BLOCK, BLOCK), BLOCK)
+            device_grads[d] = [panel_grads[0][i, at] for i in range(2)]
+
+    for i in range(2):
+        near_grads = [total_of(p) for p in parts_of[1][i]]
+        edge_grads = [total_of(p) for p in parts_of[0][i][:2]]
+        before = [
+            edge_grads[0] + 0.5 * spread(near_grads[1][EDGE:], pool()),
+            near_grads[0],
+            near_grads[1][:EDGE],
+        ]
+        after = [
+            edge_grads[1] + 0.5 * spread(near_grads[2][:EDGE], pool()),
+            near_grads[2][EDGE:],
+            near_grads[3],
+        ]
+        before, after = [jnp.concatenate(p, axis=0).astype(BF16) for p in (before, after)]
+        sends[1][i] = jnp.where(odd, before, after)
+        far = jnp.where(odd, after, before)
+        for d in range(2, seq_count):
+            device_grad = device_grads[d][i].astype(BF16)
+            if d in wides:
+                sends[d][i, :BLOCK] = jnp.where(is_neighbour(d), far[:BLOCK], device_grad)
+                sends[d][i, BLOCK:] = far[BLOCK:]
+            else:
+                sends[d][i] = device_grad
 
 
 def local_kernel(held, back, partial_ref, merged, attended_hbm, local_ref, grad_query_ref, sem):
@@ -568,27 +589,29 @@
     arguments = [
         pltpu.with_memory_space_constraint(x, pltpu.HBM) for x in (queries, keys, values, grad_out)
     ]
-    held, *sends = call(
-        functools.partial(prep_kernel, seq_count),
-        [shape(4, rows, width)] + payloads,
-        [f32(rows, width), f32(rows // 2, width)] * 2 + [pltpu.SemaphoreType.DMA((4,))],
+    fine_shapes = [shape(3, rows, width, dtype=F32)]
+    fine_shapes += [shape(rows >> level, width) for level in range(1, top_level + 1)]
+    fine_scratch = [f32(rows >> level, width) for level in range(top_level)]
+    held, *outs = call(
+        functools.partial(prep_kernel, seq_count, top_level),
+        [shape(4, rows, width)] + fine_shapes + payloads,
+        [f32(rows, width), f32(rows // 2, width)] * 2
+        + fine_scratch
+        + [pltpu.SemaphoreType.DMA((4,))],
         arguments,
         in_hbm=4,
     )
+    done, sends = outs[: 1 + top_level], outs[1 + top_level :]
     received = swap_all(sends, "seq", distances)
 
     unit_flops = 2 * BLOCK * BLOCK * width
     stats, *level_queries = call(
-        fine_kernel,
-        [shape(3, rows, width, dtype=F32)]
-        + [shape(rows >> level, width) for level in range(1, top_level + 1)],
-        [f32(rows >> level, width) for level in range(top_level)],
-        (held,),
-        flops=20 * unit_flops,
+        fine_kernel, fine_shapes, fine_scratch, (held, *done), flops=20 * unit_flops
     )
 
     panel_rows = [(seq_count >> (level - 2)) * BLOCK for level in range(2, top_level + 1)]
-    pools = [f32(BLOCK, width), f32(max(seq_count * BLOCK, rows), width)]
+    panel_rows = panel_rows if top_level > 2 else []
+    pools = [f32(BLOCK, width)] * 4 + [f32(r, width) for r in panel_rows[:1]]
     for level in range(top_level - 1, -1, -1):
         pools += [f32(rows >> level, width)] * 3
     for level in range(top_level):
@@ -601,8 +624,7 @@
         [shape(rows, width)]
         + payloads
         + [shape(3, rows, width, dtype=F32), shape(rows, width, dtype=F32)],
-        [pltpu.VMEM((2, 2 * BLOCK, width), BF16), pltpu.VMEM((2, 4 * BLOCK, width), BF16)]
-        + [pltpu.VMEM((2, r, width), BF16) for r in panel_rows]
+        [pltpu.VMEM((2, r, width), BF16) for r in panel_rows]
         + [f32(2, r, width) for r in panel_rows]
         + pools,
         (held, stats, *level_queries, *received),

time: 37.3 us -> 35.5 us (0.952)
  starting transfers between devices: 16.5 us -> 15.4 us
  waiting for transfers between devices: 11.7 us -> 11 us
    ppermute x13, starting transfers between devices: 16.5 us -> 15.4 us  [swap_all(): lax.ppermute(x, axis, [(i, i ^ d) for i in range(size)])]
    ppermute x13, waiting for transfers between devices: 11.7 us -> 11 us  [swap_all(): lax.ppermute(x, axis, [(i, i ^ d) for i in range(size)])]
  transfers between devices with their start and end apart: 13 -> 13, of which waited for: 7 -> 6; matrix products, arithmetic and copies ran while one was open for 0% -> 0% of each run, Pallas kernels for 8% -> 6%
where the time goes in v6:
time: 35.5 us; the launch traced here: 35.2 us
  starting transfers between devices  15.4 us (43%)
  waiting for transfers between devices  11 us (31%)
  Pallas kernels  8.13 us (23%)
  between operations  0.69 us (2%)
    ppermute x13, starting transfers between devices, swap_all(): lax.ppermute(x, axis, [(i, i ^ d) for i in range(size)])  15.4 us
    ppermute x13, waiting for transfers between devices, swap_all(): lax.ppermute(x, axis, [(i, i ^ d) for i in range(size)])  11 us
    pallas_call x7, Pallas kernels, call(): pl.pallas_call(kernel, out_shape=outs, in_specs=[pl.BlockSpec(memory_spac...  8.13 us
  transfers between devices with their start and end apart: 13, of which 6 were waited for; matrix products, arithmetic and copies ran while one was open for 0% of the time, Pallas kernels for 6%

profile of v6, /device:TPU:0, one launch (start us, length us, event | category | flops | bytes accessed | tf_op | source)
XLA Modules:
  0.0 35.2 jit_solution(18338107266209389671)
XLA Ops:
  0.6 2.2 %shard_map.75 = (bf16[4,512,128]{2,1,0:T(8,128)(2,1)S(1)}, f32[3,512,128]{2,1,0:T(8,128)S(1)}, bf16[256,128]{1,0:T(8,128)(2,1)S(1)}, bf16[128,128]{1,0:T(8,128)(...) custom-call(bf16[512,128]{1,0:T(8,128)(2,1)} %refs_0_.1, ...), custom_call_target="tpu_custom_call" | custom-call | bytes 1048576 | tf_op jit(solution)/shard_map/pallas_call | solution.py:553
  2.9 4.0 %collective-permute-start = (bf16[2,320,128]{2,1,0:T(8,128)(2,1)S(1)}, bf16[2,320,128]{2,1,0:T(8,128)(2,1)S(1)}, u32[]{:S(2)}, u32[]{:S(2)}) collective-permute-start(bf16[2,320,128]{2,1,0:T(8,128)(2,1)S(1)} %get-tuple-element.43), channel_id=1, source_target_pairs={{0,24},{8,16},{16,8},{24,0},{1,25},{9,17},{17,9},{25,1},{2,26},{10... | collective-permute-start | bytes 491528 | tf_op jit(solution)/shard_map/ppermute | solution.py:569
  6.8 0.5 %collective-permute-start.1 = (bf16[2,320,128]{2,1,0:T(8,128)(2,1)S(1)}, bf16[2,320,128]{2,1,0:T(8,128)(2,1)S(1)}, u32[]{:S(2)}, u32[]{:S(2)}) collective-permute-start(bf16[2,320,128]{2,1,0:T(8,128)(2,1)S(1)} %get-tuple-element.44), channel_id=1, source_target_pairs={{0,8},{8,0},{16,24},{24,16},{1,9},{9,1},{17,25},{25,17},{2,10},{10... | collective-permute-start | bytes 491528 | tf_op jit(solution)/shard_map/ppermute | solution.py:569
  7.4 0.1 collective-permute-start.2
  7.5 0.1 shard_map.76
  7.5 4.6 %collective-permute-done.2.refs_6_ = bf16[2,128,128]{2,1,0:T(8,128)(2,1)S(1)} collective-permute-done((bf16[2,128,128]{2,1,0:T(8,128)(2,1)S(1)}, bf16[2,128,128]{2,1,0:T(8,128)(2,1)S(1)}, u32[]{:S(2)}, u32[]{:S(2)}) %collective-permute-start.2) | collective-permute-done | bytes 65568 | tf_op jit(solution)/shard_map/ppermute | solution.py:569
  12.1 0.0 collective-permute-done.refs_4_
  12.2 1.5 %collective-permute-done.1.refs_5_ = bf16[2,320,128]{2,1,0:T(8,128)(2,1)S(1)} collective-permute-done((bf16[2,320,128]{2,1,0:T(8,128)(2,1)S(1)}, bf16[2,320,128]{2,1,0:T(8,128)(2,1)S(1)}, u32[]{:S(2)}, u32[]{:S(2)}) %collective-permute-start.1) | collective-permute-done | bytes 163872 | tf_op jit(solution)/shard_map/ppermute | solution.py:569
  13.7 2.8 %shard_map.77 = (bf16[512,128]{1,0:T(8,128)(2,1)S(1)}, bf16[2,320,128]{2,1,0:T(8,128)(2,1)S(1)}, bf16[2,320,128]{2,1,0:T(8,128)(2,1)S(1)}, bf16[2,128,128]{2,1,0...) custom-call(bf16[4,512,128]{2,1,0:T(8,128)(2,1)S(1)} %get-tuple-element.36.held.refs_0_, ...), custom_call_target="tpu_custom_call" | custom-call | flops 293601280 | bytes 1048576 | tf_op jit(solution)/shard_map/pallas_call | solution.py:553
  16.5 1.5 %collective-permute-start.3 = (bf16[2,320,128]{2,1,0:T(8,128)(2,1)S(1)}, bf16[2,320,128]{2,1,0:T(8,128)(2,1)S(1)}, u32[]{:S(2)}, u32[]{:S(2)}) collective-permute-start(bf16[2,320,128]{2,1,0:T(8,128)(2,1)S(1)} %get-tuple-element.52), channel_id=1, source_target_pairs={{0,24},{8,16},{16,8},{24,0},{1,25},{9,17},{17,9},{25,1},{2,26},{10... | collective-permute-start | bytes 491528 | tf_op jit(solution)/shard_map/ppermute | solution.py:569
  18.0 0.3 collective-permute-start.4
  18.4 1.7 %collective-permute-start.5 = (bf16[2,128,128]{2,1,0:T(8,128)(2,1)S(1)}, bf16[2,128,128]{2,1,0:T(8,128)(2,1)S(1)}, u32[]{:S(2)}, u32[]{:S(2)}) collective-permute-start(bf16[2,128,128]{2,1,0:T(8,128)(2,1)S(1)} %get-tuple-element.54), channel_id=1, source_target_pairs={{0,16},{8,24},{16,0},{24,8},{1,17},{9,25},{17,1},{25,9},{2,18},{10... | collective-permute-start | bytes 196616 | tf_op jit(solution)/shard_map/ppermute | solution.py:569
  20.1 1.2 %shard_map.78 = (bf16[512,128]{1,0:T(8,128)(2,1)}, f32[2,512,128]{2,1,0:T(8,128)S(1)}, bf16[512,128]{1,0:T(8,128)(2,1)S(1)}) custom-call(bf16[4,512,128]{2,1,0:T(8,128)(2,1)S(1)} %get-tuple-element.36.held.refs_0_, f32[3,512,128]{2,1,0:T(8,128)S(1)} %get-tuple-element.46.back, f32[512,128]{1,0:T(8,128)S(1)} %get-tuple-element.47.partial_ref, ...), custom_call_target="tpu_custom_call" | custom-call | flops 209715200 | bytes 1048576 | tf_op jit(solution)/shard_map/pallas_call | solution.py:553
  21.3 2.6 %collective-permute-done.5.refs_2_ = bf16[2,128,128]{2,1,0:T(8,128)(2,1)S(1)} collective-permute-done((bf16[2,128,128]{2,1,0:T(8,128)(2,1)S(1)}, bf16[2,128,128]{2,1,0:T(8,128)(2,1)S(1)}, u32[]{:S(2)}, u32[]{:S(2)}) %collective-permute-start.5) | collective-permute-done | bytes 65568 | tf_op jit(solution)/shard_map/ppermute | solution.py:569
  23.9 0.2 collective-permute-done.4.refs_1_
  24.0 0.2 shard_map.79
  24.3 2.6 %collective-permute-start.6 = (bf16[2,3,64,128]{3,2,1,0:T(8,128)(2,1)S(1)}, bf16[2,3,64,128]{3,2,1,0:T(8,128)(2,1)S(1)}, u32[]{:S(2)}, u32[]{:S(2)}) collective-permute-start(bf16[2,3,64,128]{3,2,1,0:T(8,128)(2,1)S(1)} %get-tuple-element.56), channel_id=1, source_target_pairs={{0,4},{1,5},{2,6},{3,7},{4,0},{5,1},{6,2},{7,3},{8,12},{9,13},{10,... | collective-permute-start | bytes 294920 | tf_op jit(solution)/shard_map/ppermute | solution.py:569
  26.9 1.3 %collective-permute-start.7 = (bf16[3,64,128]{2,1,0:T(8,128)(2,1)S(1)}, bf16[3,64,128]{2,1,0:T(8,128)(2,1)S(1)}, u32[]{:S(2)}, u32[]{:S(2)}) collective-permute-start(bf16[3,64,128]{2,1,0:T(8,128)(2,1)S(1)} %get-tuple-element.57), channel_id=1, source_target_pairs={{0,6},{1,7},{2,4},{3,5},{4,2},{5,3},{6,0},{7,1},{8,14},{9,15},{10,... | collective-permute-start | bytes 147464 | tf_op jit(solution)/shard_map/ppermute | solution.py:569
  28.2 0.2 collective-permute-start.8
  28.4 3.1 %collective-permute-start.10 = (bf16[3,64,128]{2,1,0:T(8,128)(2,1)S(1)}, bf16[3,64,128]{2,1,0:T(8,128)(2,1)S(1)}, u32[]{:S(2)}, u32[]{:S(2)}) collective-permute-start(bf16[3,64,128]{2,1,0:T(8,128)(2,1)S(1)} %get-tuple-element.63), channel_id=1, source_target_pairs={{0,3},{1,2},{2,1},{3,0},{4,7},{5,6},{6,5},{7,4},{8,11},{9,10},{10,... | collective-permute-start | bytes 147464 | tf_op jit(solution)/shard_map/ppermute | solution.py:569
  31.6 1.3 %collective-permute-done.7.refs_2_ = bf16[3,64,128]{2,1,0:T(8,128)(2,1)S(1)} collective-permute-done((bf16[3,64,128]{2,1,0:T(8,128)(2,1)S(1)}, bf16[3,64,128]{2,1,0:T(8,128)(2,1)S(1)}, u32[]{:S(2)}, u32[]{:S(2)}) %collective-permute-start.7) | collective-permute-done | bytes 49184 | tf_op jit(solution)/shard_map/ppermute | solution.py:569
  32.8 0.8 %shard_map.80 = (bf16[64,1024]{1,0:T(8,128)(2,1)}, bf16[64,1024]{1,0:T(8,128)(2,1)}, bf16[64,1024]{1,0:T(8,128)(2,1)}) custom-call(bf16[3,64,128]{2,1,0:T(8,128)(2,1)S(1)} %get-tuple-element.55.refs_0_, bf16[2,3,64,128]{3,2,1,0:T(8,128)(2,1)S(1)} %collective-permute-done.6.refs_1_, bf16[3,64,128]{2,1,0:T(8,128)(2,1)S(1)} %collective-permute-done.7.refs_2_, ...), custom_call_target="tpu_custom_call" | custom-call | flops 209715200 | bytes 1048576 | tf_op jit(solution)/shard_map/pallas_call | solution.py:553
  33.6 0.7 %collective-permute-done.9.refs_3_ = bf16[3,64,128]{2,1,0:T(8,128)(2,1)S(1)} collective-permute-done((bf16[3,64,128]{2,1,0:T(8,128)(2,1)S(1)}, bf16[3,64,128]{2,1,0:T(8,128)(2,1)S(1)}, u32[]{:S(2)}, u32[]{:S(2)}) %collective-permute-start.9) | collective-permute-done | bytes 49184 | tf_op jit(solution)/shard_map/ppermute | solution.py:569
  34.4 0.8 %shard_map.81 = (bf16[64,1024]{1,0:T(8,128)(2,1)}, bf16[64,1024]{1,0:T(8,128)(2,1)}, bf16[64,1024]{1,0:T(8,128)(2,1)}) custom-call(bf16[64,1024]{1,0:T(8,128)(2,1)} %get-tuple-element.59.refs_0_, bf16[64,1024]{1,0:T(8,128)(2,1)} %get-tuple-element.60.refs_1_, ...), custom_call_target="tpu_custom_call", output_to_operand_aliasing={{0}: (0, {}), {1}: (1, {}), {2}: (2, {})} | custom-call | bytes 1048576 | tf_op jit(solution)/shard_map/pallas_call | solution.py:553
  (10 shorter events, 0.0 us)
Async XLA Ops:
  2.9 9.3 %collective-permute-start = (bf16[2,320,128]{2,1,0:T(8,128)(2,1)S(1)}, bf16[2,320,128]{2,1,0:T(8,128)(2,1)S(1)}, u32[]{:S(2)}, u32[]{:S(2)}) collective-permute-start(bf16[2,320,128]{2,1,0:T(8,128)(2,1)S(1)} %get-tuple-element.43), channel_id=1, source_target_pairs={{0,24},{8,16},{16,8},{24,0},{1,25},{9,17},{17,9},{25,1},{2,26},{10... | collective-permute-start | bytes 491528 | tf_op jit(solution)/shard_map/ppermute | solution.py:569
  6.8 6.9 %collective-permute-start.1 = (bf16[2,320,128]{2,1,0:T(8,128)(2,1)S(1)}, bf16[2,320,128]{2,1,0:T(8,128)(2,1)S(1)}, u32[]{:S(2)}, u32[]{:S(2)}) collective-permute-start(bf16[2,320,128]{2,1,0:T(8,128)(2,1)S(1)} %get-tuple-element.44), channel_id=1, source_target_pairs={{0,8},{8,0},{16,24},{24,16},{1,9},{9,1},{17,25},{25,17},{2,10},{10... | collective-permute-start | bytes 491528 | tf_op jit(solution)/shard_map/ppermute | solution.py:569
  7.4 4.8 %collective-permute-start.2 = (bf16[2,128,128]{2,1,0:T(8,128)(2,1)S(1)}, bf16[2,128,128]{2,1,0:T(8,128)(2,1)S(1)}, u32[]{:S(2)}, u32[]{:S(2)}) collective-permute-start(bf16[2,128,128]{2,1,0:T(8,128)(2,1)S(1)} %get-tuple-element.45), channel_id=1, source_target_pairs={{0,16},{8,24},{16,0},{24,8},{1,17},{9,25},{17,1},{25,9},{2,18},{10... | collective-permute-start | bytes 196616 | tf_op jit(solution)/shard_map/ppermute | solution.py:569
  16.5 7.3 %collective-permute-start.3 = (bf16[2,320,128]{2,1,0:T(8,128)(2,1)S(1)}, bf16[2,320,128]{2,1,0:T(8,128)(2,1)S(1)}, u32[]{:S(2)}, u32[]{:S(2)}) collective-permute-start(bf16[2,320,128]{2,1,0:T(8,128)(2,1)S(1)} %get-tuple-element.52), channel_id=1, source_target_pairs={{0,24},{8,16},{16,8},{24,0},{1,25},{9,17},{17,9},{25,1},{2,26},{10... | collective-permute-start | bytes 491528 | tf_op jit(solution)/shard_map/ppermute | solution.py:569
  18.0 6.0 %collective-permute-start.4 = (bf16[2,320,128]{2,1,0:T(8,128)(2,1)S(1)}, bf16[2,320,128]{2,1,0:T(8,128)(2,1)S(1)}, u32[]{:S(2)}, u32[]{:S(2)}) collective-permute-start(bf16[2,320,128]{2,1,0:T(8,128)(2,1)S(1)} %get-tuple-element.53), channel_id=1, source_target_pairs={{0,8},{8,0},{16,24},{24,16},{1,9},{9,1},{17,25},{25,17},{2,10},{10... | collective-permute-start | bytes 491528 | tf_op jit(solution)/shard_map/ppermute | solution.py:569
  18.4 5.5 %collective-permute-start.5 = (bf16[2,128,128]{2,1,0:T(8,128)(2,1)S(1)}, bf16[2,128,128]{2,1,0:T(8,128)(2,1)S(1)}, u32[]{:S(2)}, u32[]{:S(2)}) collective-permute-start(bf16[2,128,128]{2,1,0:T(8,128)(2,1)S(1)} %get-tuple-element.54), channel_id=1, source_target_pairs={{0,16},{8,24},{16,0},{24,8},{1,17},{9,25},{17,1},{25,9},{2,18},{10... | collective-permute-start | bytes 196616 | tf_op jit(solution)/shard_map/ppermute | solution.py:569
  24.3 7.2 %collective-permute-start.6 = (bf16[2,3,64,128]{3,2,1,0:T(8,128)(2,1)S(1)}, bf16[2,3,64,128]{3,2,1,0:T(8,128)(2,1)S(1)}, u32[]{:S(2)}, u32[]{:S(2)}) collective-permute-start(bf16[2,3,64,128]{3,2,1,0:T(8,128)(2,1)S(1)} %get-tuple-element.56), channel_id=1, source_target_pairs={{0,4},{1,5},{2,6},{3,7},{4,0},{5,1},{6,2},{7,3},{8,12},{9,13},{10,... | collective-permute-start | bytes 294920 | tf_op jit(solution)/shard_map/ppermute | solution.py:569
  26.9 6.0 %collective-permute-start.7 = (bf16[3,64,128]{2,1,0:T(8,128)(2,1)S(1)}, bf16[3,64,128]{2,1,0:T(8,128)(2,1)S(1)}, u32[]{:S(2)}, u32[]{:S(2)}) collective-permute-start(bf16[3,64,128]{2,1,0:T(8,128)(2,1)S(1)} %get-tuple-element.57), channel_id=1, source_target_pairs={{0,6},{1,7},{2,4},{3,5},{4,2},{5,3},{6,0},{7,1},{8,14},{9,15},{10,... | collective-permute-start | bytes 147464 | tf_op jit(solution)/shard_map/ppermute | solution.py:569
  28.2 4.6 %collective-permute-start.8 = (bf16[3,64,128]{2,1,0:T(8,128)(2,1)S(1)}, bf16[3,64,128]{2,1,0:T(8,128)(2,1)S(1)}, u32[]{:S(2)}, u32[]{:S(2)}) collective-permute-start(bf16[3,64,128]{2,1,0:T(8,128)(2,1)S(1)} %get-tuple-element.58), channel_id=1, source_target_pairs={{0,2},{1,3},{2,0},{3,1},{4,6},{5,7},{6,4},{7,5},{8,10},{9,11},{10,... | collective-permute-start | bytes 147464 | tf_op jit(solution)/shard_map/ppermute | solution.py:569
  28.4 5.9 %collective-permute-start.9 = (bf16[3,64,128]{2,1,0:T(8,128)(2,1)S(1)}, bf16[3,64,128]{2,1,0:T(8,128)(2,1)S(1)}, u32[]{:S(2)}, u32[]{:S(2)}) collective-permute-start(bf16[3,64,128]{2,1,0:T(8,128)(2,1)S(1)} %get-tuple-element.62), channel_id=1, source_target_pairs={{0,7},{1,6},{2,5},{3,4},{4,3},{5,2},{6,1},{7,0},{8,15},{9,14},{10,... | collective-permute-start | bytes 147464 | tf_op jit(solution)/shard_map/ppermute | solution.py:569
  28.4 5.9 %collective-permute-start.10 = (bf16[3,64,128]{2,1,0:T(8,128)(2,1)S(1)}, bf16[3,64,128]{2,1,0:T(8,128)(2,1)S(1)}, u32[]{:S(2)}, u32[]{:S(2)}) collective-permute-start(bf16[3,64,128]{2,1,0:T(8,128)(2,1)S(1)} %get-tuple-element.63), channel_id=1, source_target_pairs={{0,3},{1,2},{2,1},{3,0},{4,7},{5,6},{6,5},{7,4},{8,11},{9,10},{10,... | collective-permute-start | bytes 147464 | tf_op jit(solution)/shard_map/ppermute | solution.py:569
  31.5 2.8 %collective-permute-start.11 = (bf16[3,64,128]{2,1,0:T(8,128)(2,1)S(1)}, bf16[3,64,128]{2,1,0:T(8,128)(2,1)S(1)}, u32[]{:S(2)}, u32[]{:S(2)}) collective-permute-start(bf16[3,64,128]{2,1,0:T(8,128)(2,1)S(1)} %get-tuple-element.64), channel_id=1, source_target_pairs={{0,1},{1,0},{2,3},{3,2},{4,5},{5,4},{6,7},{7,6},{8,9},{9,8},{10,11... | collective-permute-start | bytes 147464 | tf_op jit(solution)/shard_map/ppermute | solution.py:569
  32.8 1.6 %collective-permute-start.12 = (bf16[3,64,128]{2,1,0:T(8,128)(2,1)S(1)}, bf16[3,64,128]{2,1,0:T(8,128)(2,1)S(1)}, u32[]{:S(2)}, u32[]{:S(2)}) collective-permute-start(bf16[3,64,128]{2,1,0:T(8,128)(2,1)S(1)} %slice_bitcast_fusion), channel_id=1, source_target_pairs={{0,1},{1,0},{2,3},{3,2},{4,5},{5,4},{6,7},{7,6},{8,9},{9,8},{10,11... | collective-permute-start | bytes 147464 | tf_op jit(solution)/shard_map/ppermute | solution.py:569

commit v7 on v6

--- a/solution.py
+++ b/solution.py
@@ -162,15 +162,23 @@
 def fine_work(held, stats, queries, scratches):
     blocks, width = held.shape[1] // BLOCK, held.shape[2]
     factor = width ** (-0.5) * LOG2E
-    for a in range(blocks):
-        lo, hi = own_window(a, blocks)
-        window = rows_of(lo, hi - lo)
-        scores = nt(held[0, rows_of(a)], held[1, window]) * factor
+
+    @pl.loop(0, blocks)
+    def _(a):
+        lo = jnp.clip(a - 1, 0, blocks - 3)
+        own = pl.ds(pl.multiple_of(a * BLOCK, BLOCK), BLOCK)
+        window = pl.ds(pl.multiple_of(lo * BLOCK, BLOCK), 3 * BLOCK)
+        scores = nt(held[0, own], held[1, window]) * factor
+        parts = [
+            jnp.where(jnp.abs(lo + b - a) <= 1, scores[:, rows_of(b)], MASKED) for b in range(3)
+        ]
+        scores = jnp.concatenate(parts, axis=1)
         peak = row_max(scores)
         exps = jnp.exp2(scores - across(peak, scores.shape[1]))
-        stats[0, rows_of(a)] = peak
-        stats[1, rows_of(a)] = row_sum(exps)
-        stats[2, rows_of(a)] = nn(exps.astype(BF16), held[2, window])
+        stats[0, own] = peak
+        stats[1, own] = row_sum(exps)
+        stats[2, own] = nn(exps.astype(BF16), held[2, window])
+
     query = held[0]
     for ref, scratch in zip(queries, scratches):
         query = coarse(query, scratch)

time: 35.5 us -> 35.1 us (0.989)
  waiting for transfers between devices: 11 us -> 9.93 us
  Pallas kernels: 8.13 us -> 8.68 us
    ppermute x13, waiting for transfers between devices: 11 us -> 9.93 us  [swap_all(): lax.ppermute(x, axis, [(i, i ^ d) for i in range(size)])]
    pallas_call x7, Pallas kernels: 8.13 us -> 8.68 us  [call(): pl.pallas_call(kernel, out_shape=outs, in_specs=[pl.BlockSpec(memory_spac...]
  transfers between devices with their start and end apart: 13 -> 13, of which waited for: 6 -> 5; matrix products, arithmetic and copies ran while one was open for 0% -> 0% of each run, Pallas kernels for 6% -> 6%
where the time goes in v7:
time: 35.1 us; the launch traced here: 34.8 us
  starting transfers between devices  15.5 us (44%)
  waiting for transfers between devices  9.93 us (28%)
  Pallas kernels  8.68 us (25%)
  between operations  0.69 us (2%)
    ppermute x13, starting transfers between devices, swap_all(): lax.ppermute(x, axis, [(i, i ^ d) for i in range(size)])  15.5 us
    ppermute x13, waiting for transfers between devices, swap_all(): lax.ppermute(x, axis, [(i, i ^ d) for i in range(size)])  9.93 us
    pallas_call x7, Pallas kernels, call(): pl.pallas_call(kernel, out_shape=outs, in_specs=[pl.BlockSpec(memory_spac...  8.68 us
  transfers between devices with their start and end apart: 13, of which 5 were waited for; matrix products, arithmetic and copies ran while one was open for 0% of the time, Pallas kernels for 6%

profile of v7, /device:TPU:0, one launch (start us, length us, event | category | flops | bytes accessed | tf_op | source)
XLA Modules:
  0.0 34.8 jit_solution(4796662798342065210)
XLA Ops:
  0.6 2.8 %shard_map.75 = (bf16[4,512,128]{2,1,0:T(8,128)(2,1)S(1)}, f32[3,512,128]{2,1,0:T(8,128)S(1)}, bf16[256,128]{1,0:T(8,128)(2,1)S(1)}, bf16[128,128]{1,0:T(8,128)(...) custom-call(bf16[512,128]{1,0:T(8,128)(2,1)} %refs_0_.1, ...), custom_call_target="tpu_custom_call" | custom-call | bytes 1048576 | tf_op jit(solution)/shard_map/pallas_call | solution.py:561
  3.4 4.0 %collective-permute-start = (bf16[2,320,128]{2,1,0:T(8,128)(2,1)S(1)}, bf16[2,320,128]{2,1,0:T(8,128)(2,1)S(1)}, u32[]{:S(2)}, u32[]{:S(2)}) collective-permute-start(bf16[2,320,128]{2,1,0:T(8,128)(2,1)S(1)} %get-tuple-element.43), channel_id=1, source_target_pairs={{0,24},{8,16},{16,8},{24,0},{1,25},{9,17},{17,9},{25,1},{2,26},{10... | collective-permute-start | bytes 491528 | tf_op jit(solution)/shard_map/ppermute | solution.py:577
  7.4 0.5 %collective-permute-start.1 = (bf16[2,320,128]{2,1,0:T(8,128)(2,1)S(1)}, bf16[2,320,128]{2,1,0:T(8,128)(2,1)S(1)}, u32[]{:S(2)}, u32[]{:S(2)}) collective-permute-start(bf16[2,320,128]{2,1,0:T(8,128)(2,1)S(1)} %get-tuple-element.44), channel_id=1, source_target_pairs={{0,8},{8,0},{16,24},{24,16},{1,9},{9,1},{17,25},{25,17},{2,10},{10... | collective-permute-start | bytes 491528 | tf_op jit(solution)/shard_map/ppermute | solution.py:577
  7.9 0.1 collective-permute-start.2
  8.0 0.1 shard_map.76
  8.1 4.3 %collective-permute-done.2.refs_6_ = bf16[2,128,128]{2,1,0:T(8,128)(2,1)S(1)} collective-permute-done((bf16[2,128,128]{2,1,0:T(8,128)(2,1)S(1)}, bf16[2,128,128]{2,1,0:T(8,128)(2,1)S(1)}, u32[]{:S(2)}, u32[]{:S(2)}) %collective-permute-start.2) | collective-permute-done | bytes 65568 | tf_op jit(solution)/shard_map/ppermute | solution.py:577
  12.4 1.3 %collective-permute-done.1.refs_5_ = bf16[2,320,128]{2,1,0:T(8,128)(2,1)S(1)} collective-permute-done((bf16[2,320,128]{2,1,0:T(8,128)(2,1)S(1)}, bf16[2,320,128]{2,1,0:T(8,128)(2,1)S(1)}, u32[]{:S(2)}, u32[]{:S(2)}) %collective-permute-start.1) | collective-permute-done | bytes 163872 | tf_op jit(solution)/shard_map/ppermute | solution.py:577
  13.7 2.8 %shard_map.77 = (bf16[512,128]{1,0:T(8,128)(2,1)S(1)}, bf16[2,320,128]{2,1,0:T(8,128)(2,1)S(1)}, bf16[2,320,128]{2,1,0:T(8,128)(2,1)S(1)}, bf16[2,128,128]{2,1,0...) custom-call(bf16[4,512,128]{2,1,0:T(8,128)(2,1)S(1)} %get-tuple-element.36.held.refs_0_, ...), custom_call_target="tpu_custom_call" | custom-call | flops 293601280 | bytes 1048576 | tf_op jit(solution)/shard_map/pallas_call | solution.py:561
  16.6 1.5 %collective-permute-start.3 = (bf16[2,320,128]{2,1,0:T(8,128)(2,1)S(1)}, bf16[2,320,128]{2,1,0:T(8,128)(2,1)S(1)}, u32[]{:S(2)}, u32[]{:S(2)}) collective-permute-start(bf16[2,320,128]{2,1,0:T(8,128)(2,1)S(1)} %get-tuple-element.52), channel_id=1, source_target_pairs={{0,24},{8,16},{16,8},{24,0},{1,25},{9,17},{17,9},{25,1},{2,26},{10... | collective-permute-start | bytes 491528 | tf_op jit(solution)/shard_map/ppermute | solution.py:577
  18.0 0.3 collective-permute-start.4
  18.4 1.8 %collective-permute-start.5 = (bf16[2,128,128]{2,1,0:T(8,128)(2,1)S(1)}, bf16[2,128,128]{2,1,0:T(8,128)(2,1)S(1)}, u32[]{:S(2)}, u32[]{:S(2)}) collective-permute-start(bf16[2,128,128]{2,1,0:T(8,128)(2,1)S(1)} %get-tuple-element.54), channel_id=1, source_target_pairs={{0,16},{8,24},{16,0},{24,8},{1,17},{9,25},{17,1},{25,9},{2,18},{10... | collective-permute-start | bytes 196616 | tf_op jit(solution)/shard_map/ppermute | solution.py:577
  20.1 1.2 %shard_map.78 = (bf16[512,128]{1,0:T(8,128)(2,1)}, f32[2,512,128]{2,1,0:T(8,128)S(1)}, bf16[512,128]{1,0:T(8,128)(2,1)S(1)}) custom-call(bf16[4,512,128]{2,1,0:T(8,128)(2,1)S(1)} %get-tuple-element.36.held.refs_0_, f32[3,512,128]{2,1,0:T(8,128)S(1)} %get-tuple-element.46.back, f32[512,128]{1,0:T(8,128)S(1)} %get-tuple-element.47.partial_ref, ...), custom_call_target="tpu_custom_call" | custom-call | flops 209715200 | bytes 1048576 | tf_op jit(solution)/shard_map/pallas_call | solution.py:561
  21.3 2.2 %collective-permute-done.5.refs_2_ = bf16[2,128,128]{2,1,0:T(8,128)(2,1)S(1)} collective-permute-done((bf16[2,128,128]{2,1,0:T(8,128)(2,1)S(1)}, bf16[2,128,128]{2,1,0:T(8,128)(2,1)S(1)}, u32[]{:S(2)}, u32[]{:S(2)}) %collective-permute-start.5) | collective-permute-done | bytes 65568 | tf_op jit(solution)/shard_map/ppermute | solution.py:577
  23.6 0.2 shard_map.79
  23.8 2.7 %collective-permute-start.6 = (bf16[2,3,64,128]{3,2,1,0:T(8,128)(2,1)S(1)}, bf16[2,3,64,128]{3,2,1,0:T(8,128)(2,1)S(1)}, u32[]{:S(2)}, u32[]{:S(2)}) collective-permute-start(bf16[2,3,64,128]{3,2,1,0:T(8,128)(2,1)S(1)} %get-tuple-element.56), channel_id=1, source_target_pairs={{0,4},{1,5},{2,6},{3,7},{4,0},{5,1},{6,2},{7,3},{8,12},{9,13},{10,... | collective-permute-start | bytes 294920 | tf_op jit(solution)/shard_map/ppermute | solution.py:577
  26.5 1.3 %collective-permute-start.7 = (bf16[3,64,128]{2,1,0:T(8,128)(2,1)S(1)}, bf16[3,64,128]{2,1,0:T(8,128)(2,1)S(1)}, u32[]{:S(2)}, u32[]{:S(2)}) collective-permute-start(bf16[3,64,128]{2,1,0:T(8,128)(2,1)S(1)} %get-tuple-element.57), channel_id=1, source_target_pairs={{0,6},{1,7},{2,4},{3,5},{4,2},{5,3},{6,0},{7,1},{8,14},{9,15},{10,... | collective-permute-start | bytes 147464 | tf_op jit(solution)/shard_map/ppermute | solution.py:577
  27.9 0.2 collective-permute-start.8
  28.1 0.0 collective-permute-start.9
  28.1 3.1 %collective-permute-start.10 = (bf16[3,64,128]{2,1,0:T(8,128)(2,1)S(1)}, bf16[3,64,128]{2,1,0:T(8,128)(2,1)S(1)}, u32[]{:S(2)}, u32[]{:S(2)}) collective-permute-start(bf16[3,64,128]{2,1,0:T(8,128)(2,1)S(1)} %get-tuple-element.63), channel_id=1, source_target_pairs={{0,3},{1,2},{2,1},{3,0},{4,7},{5,6},{6,5},{7,4},{8,11},{9,10},{10,... | collective-permute-start | bytes 147464 | tf_op jit(solution)/shard_map/ppermute | solution.py:577
  31.2 1.3 %collective-permute-done.7.refs_2_ = bf16[3,64,128]{2,1,0:T(8,128)(2,1)S(1)} collective-permute-done((bf16[3,64,128]{2,1,0:T(8,128)(2,1)S(1)}, bf16[3,64,128]{2,1,0:T(8,128)(2,1)S(1)}, u32[]{:S(2)}, u32[]{:S(2)}) %collective-permute-start.7) | collective-permute-done | bytes 49184 | tf_op jit(solution)/shard_map/ppermute | solution.py:577
  32.5 0.0 collective-permute-start.12
  32.5 0.8 %shard_map.80 = (bf16[64,1024]{1,0:T(8,128)(2,1)}, bf16[64,1024]{1,0:T(8,128)(2,1)}, bf16[64,1024]{1,0:T(8,128)(2,1)}) custom-call(bf16[3,64,128]{2,1,0:T(8,128)(2,1)S(1)} %get-tuple-element.55.refs_0_, bf16[2,3,64,128]{3,2,1,0:T(8,128)(2,1)S(1)} %collective-permute-done.6.refs_1_, bf16[3,64,128]{2,1,0:T(8,128)(2,1)S(1)} %collective-permute-done.7.refs_2_, ...), custom_call_target="tpu_custom_call" | custom-call | flops 209715200 | bytes 1048576 | tf_op jit(solution)/shard_map/pallas_call | solution.py:561
  33.3 0.7 %collective-permute-done.9.refs_3_ = bf16[3,64,128]{2,1,0:T(8,128)(2,1)S(1)} collective-permute-done((bf16[3,64,128]{2,1,0:T(8,128)(2,1)S(1)}, bf16[3,64,128]{2,1,0:T(8,128)(2,1)S(1)}, u32[]{:S(2)}, u32[]{:S(2)}) %collective-permute-start.9) | collective-permute-done | bytes 49184 | tf_op jit(solution)/shard_map/ppermute | solution.py:577
  34.0 0.8 %shard_map.81 = (bf16[64,1024]{1,0:T(8,128)(2,1)}, bf16[64,1024]{1,0:T(8,128)(2,1)}, bf16[64,1024]{1,0:T(8,128)(2,1)}) custom-call(bf16[64,1024]{1,0:T(8,128)(2,1)} %get-tuple-element.59.refs_0_, bf16[64,1024]{1,0:T(8,128)(2,1)} %get-tuple-element.60.refs_1_, ...), custom_call_target="tpu_custom_call", output_to_operand_aliasing={{0}: (0, {}), {1}: (1, {}), {2}: (2, {})} | custom-call | bytes 1048576 | tf_op jit(solution)/shard_map/pallas_call | solution.py:561
  (10 shorter events, 0.0 us)
Async XLA Ops:
  3.4 9.0 %collective-permute-start = (bf16[2,320,128]{2,1,0:T(8,128)(2,1)S(1)}, bf16[2,320,128]{2,1,0:T(8,128)(2,1)S(1)}, u32[]{:S(2)}, u32[]{:S(2)}) collective-permute-start(bf16[2,320,128]{2,1,0:T(8,128)(2,1)S(1)} %get-tuple-element.43), channel_id=1, source_target_pairs={{0,24},{8,16},{16,8},{24,0},{1,25},{9,17},{17,9},{25,1},{2,26},{10... | collective-permute-start | bytes 491528 | tf_op jit(solution)/shard_map/ppermute | solution.py:577
  7.4 6.4 %collective-permute-start.1 = (bf16[2,320,128]{2,1,0:T(8,128)(2,1)S(1)}, bf16[2,320,128]{2,1,0:T(8,128)(2,1)S(1)}, u32[]{:S(2)}, u32[]{:S(2)}) collective-permute-start(bf16[2,320,128]{2,1,0:T(8,128)(2,1)S(1)} %get-tuple-element.44), channel_id=1, source_target_pairs={{0,8},{8,0},{16,24},{24,16},{1,9},{9,1},{17,25},{25,17},{2,10},{10... | collective-permute-start | bytes 491528 | tf_op jit(solution)/shard_map/ppermute | solution.py:577
  7.9 4.5 %collective-permute-start.2 = (bf16[2,128,128]{2,1,0:T(8,128)(2,1)S(1)}, bf16[2,128,128]{2,1,0:T(8,128)(2,1)S(1)}, u32[]{:S(2)}, u32[]{:S(2)}) collective-permute-start(bf16[2,128,128]{2,1,0:T(8,128)(2,1)S(1)} %get-tuple-element.45), channel_id=1, source_target_pairs={{0,16},{8,24},{16,0},{24,8},{1,17},{9,25},{17,1},{25,9},{2,18},{10... | collective-permute-start | bytes 196616 | tf_op jit(solution)/shard_map/ppermute | solution.py:577
  16.6 7.0 %collective-permute-start.3 = (bf16[2,320,128]{2,1,0:T(8,128)(2,1)S(1)}, bf16[2,320,128]{2,1,0:T(8,128)(2,1)S(1)}, u32[]{:S(2)}, u32[]{:S(2)}) collective-permute-start(bf16[2,320,128]{2,1,0:T(8,128)(2,1)S(1)} %get-tuple-element.52), channel_id=1, source_target_pairs={{0,24},{8,16},{16,8},{24,0},{1,25},{9,17},{17,9},{25,1},{2,26},{10... | collective-permute-start | bytes 491528 | tf_op jit(solution)/shard_map/ppermute | solution.py:577
  18.0 5.5 %collective-permute-start.4 = (bf16[2,320,128]{2,1,0:T(8,128)(2,1)S(1)}, bf16[2,320,128]{2,1,0:T(8,128)(2,1)S(1)}, u32[]{:S(2)}, u32[]{:S(2)}) collective-permute-start(bf16[2,320,128]{2,1,0:T(8,128)(2,1)S(1)} %get-tuple-element.53), channel_id=1, source_target_pairs={{0,8},{8,0},{16,24},{24,16},{1,9},{9,1},{17,25},{25,17},{2,10},{10... | collective-permute-start | bytes 491528 | tf_op jit(solution)/shard_map/ppermute | solution.py:577
  18.4 5.2 %collective-permute-start.5 = (bf16[2,128,128]{2,1,0:T(8,128)(2,1)S(1)}, bf16[2,128,128]{2,1,0:T(8,128)(2,1)S(1)}, u32[]{:S(2)}, u32[]{:S(2)}) collective-permute-start(bf16[2,128,128]{2,1,0:T(8,128)(2,1)S(1)} %get-tuple-element.54), channel_id=1, source_target_pairs={{0,16},{8,24},{16,0},{24,8},{1,17},{9,25},{17,1},{25,9},{2,18},{10... | collective-permute-start | bytes 196616 | tf_op jit(solution)/shard_map/ppermute | solution.py:577
  23.8 7.4 %collective-permute-start.6 = (bf16[2,3,64,128]{3,2,1,0:T(8,128)(2,1)S(1)}, bf16[2,3,64,128]{3,2,1,0:T(8,128)(2,1)S(1)}, u32[]{:S(2)}, u32[]{:S(2)}) collective-permute-start(bf16[2,3,64,128]{3,2,1,0:T(8,128)(2,1)S(1)} %get-tuple-element.56), channel_id=1, source_target_pairs={{0,4},{1,5},{2,6},{3,7},{4,0},{5,1},{6,2},{7,3},{8,12},{9,13},{10,... | collective-permute-start | bytes 294920 | tf_op jit(solution)/shard_map/ppermute | solution.py:577
  26.5 6.0 %collective-permute-start.7 = (bf16[3,64,128]{2,1,0:T(8,128)(2,1)S(1)}, bf16[3,64,128]{2,1,0:T(8,128)(2,1)S(1)}, u32[]{:S(2)}, u32[]{:S(2)}) collective-permute-start(bf16[3,64,128]{2,1,0:T(8,128)(2,1)S(1)} %get-tuple-element.57), channel_id=1, source_target_pairs={{0,6},{1,7},{2,4},{3,5},{4,2},{5,3},{6,0},{7,1},{8,14},{9,15},{10,... | collective-permute-start | bytes 147464 | tf_op jit(solution)/shard_map/ppermute | solution.py:577
  27.9 4.6 %collective-permute-start.8 = (bf16[3,64,128]{2,1,0:T(8,128)(2,1)S(1)}, bf16[3,64,128]{2,1,0:T(8,128)(2,1)S(1)}, u32[]{:S(2)}, u32[]{:S(2)}) collective-permute-start(bf16[3,64,128]{2,1,0:T(8,128)(2,1)S(1)} %get-tuple-element.58), channel_id=1, source_target_pairs={{0,2},{1,3},{2,0},{3,1},{4,6},{5,7},{6,4},{7,5},{8,10},{9,11},{10,... | collective-permute-start | bytes 147464 | tf_op jit(solution)/shard_map/ppermute | solution.py:577
  28.1 5.9 %collective-permute-start.9 = (bf16[3,64,128]{2,1,0:T(8,128)(2,1)S(1)}, bf16[3,64,128]{2,1,0:T(8,128)(2,1)S(1)}, u32[]{:S(2)}, u32[]{:S(2)}) collective-permute-start(bf16[3,64,128]{2,1,0:T(8,128)(2,1)S(1)} %get-tuple-element.62), channel_id=1, source_target_pairs={{0,7},{1,6},{2,5},{3,4},{4,3},{5,2},{6,1},{7,0},{8,15},{9,14},{10,... | collective-permute-start | bytes 147464 | tf_op jit(solution)/shard_map/ppermute | solution.py:577
  28.1 5.9 %collective-permute-start.10 = (bf16[3,64,128]{2,1,0:T(8,128)(2,1)S(1)}, bf16[3,64,128]{2,1,0:T(8,128)(2,1)S(1)}, u32[]{:S(2)}, u32[]{:S(2)}) collective-permute-start(bf16[3,64,128]{2,1,0:T(8,128)(2,1)S(1)} %get-tuple-element.63), channel_id=1, source_target_pairs={{0,3},{1,2},{2,1},{3,0},{4,7},{5,6},{6,5},{7,4},{8,11},{9,10},{10,... | collective-permute-start | bytes 147464 | tf_op jit(solution)/shard_map/ppermute | solution.py:577
  31.2 2.8 %collective-permute-start.11 = (bf16[3,64,128]{2,1,0:T(8,128)(2,1)S(1)}, bf16[3,64,128]{2,1,0:T(8,128)(2,1)S(1)}, u32[]{:S(2)}, u32[]{:S(2)}) collective-permute-start(bf16[3,64,128]{2,1,0:T(8,128)(2,1)S(1)} %get-tuple-element.64), channel_id=1, source_target_pairs={{0,1},{1,0},{2,3},{3,2},{4,5},{5,4},{6,7},{7,6},{8,9},{9,8},{10,11... | collective-permute-start | bytes 147464 | tf_op jit(solution)/shard_map/ppermute | solution.py:577
  32.5 1.6 %collective-permute-start.12 = (bf16[3,64,128]{2,1,0:T(8,128)(2,1)S(1)}, bf16[3,64,128]{2,1,0:T(8,128)(2,1)S(1)}, u32[]{:S(2)}, u32[]{:S(2)}) collective-permute-start(bf16[3,64,128]{2,1,0:T(8,128)(2,1)S(1)} %slice_bitcast_fusion), channel_id=1, source_target_pairs={{0,1},{1,0},{2,3},{3,2},{4,5},{5,4},{6,7},{7,6},{8,9},{9,8},{10,11... | collective-permute-start | bytes 147464 | tf_op jit(solution)/shard_map/ppermute | solution.py:577

commit v8 on v7

--- a/solution.py
+++ b/solution.py
@@ -9,6 +9,7 @@
 
 BLOCK = 128
 EDGE = BLOCK // 2
+SPARE = 8
 REST = 2 * BLOCK - EDGE
 MASKED = -1e30
 LOG2E = 1.4426950408889634
@@ -490,7 +491,7 @@
     level_1[...] = jnp.zeros(level_1.shape, F32)
     level_2[...] = jnp.zeros(level_2.shape, F32)
     for i in range(2):
-        total[i] = local_ref[i]
+        total[i, :rows] = local_ref[i]
     for d in range(1, seq_count):
         got = received[d]
         partner = seq_index ^ d
@@ -503,12 +504,12 @@
         def _():
             for i in range(2):
                 total[i, :BLOCK] += got[i, :BLOCK].astype(F32)
-                level_1[i, EDGE:] += got[i, BLOCK:].astype(F32)
+                level_1[i, EDGE : EDGE + REST] += got[i, BLOCK:].astype(F32)
 
         @pl.when(partner == seq_index + 1)
         def _():
             for i in range(2):
-                total[i, rows - BLOCK :] += got[i, :BLOCK].astype(F32)
+                total[i, rows - BLOCK : rows] += got[i, :BLOCK].astype(F32)
                 level_1[i, :REST] += got[i, BLOCK:].astype(F32)
 
         @pl.when((partner != seq_index + 1) & (partner != seq_index - 1))
@@ -520,7 +521,7 @@
         half = level_2[i] * 0.5
         for phase in range(2):
             level_1[i, pl.ds(phase, half.shape[0], stride=2), :] += half
-        half = level_1[i] * 0.5
+        half = level_1[i, : rows // 2] * 0.5
         for phase in range(2):
             total[i, pl.ds(phase, half.shape[0], stride=2), :] += half
     for d in range(head_count):
@@ -593,17 +594,20 @@
     def f32(*dims):
         return pltpu.VMEM(dims, F32)
 
+    def strided(rows):
+        return f32(rows + SPARE, width)
+
     payloads = [shape(2, BLOCK + REST if d in wides else BLOCK, width) for d in distances]
     arguments = [
         pltpu.with_memory_space_constraint(x, pltpu.HBM) for x in (queries, keys, values, grad_out)
     ]
     fine_shapes = [shape(3, rows, width, dtype=F32)]
     fine_shapes += [shape(rows >> level, width) for level in range(1, top_level + 1)]
-    fine_scratch = [f32(rows >> level, width) for level in range(top_level)]
+    fine_scratch = [strided(rows >> level) for level in range(top_level)]
     held, *outs = call(
         functools.partial(prep_kernel, seq_count, top_level),
         [shape(4, rows, width)] + fine_shapes + payloads,
-        [f32(rows, width), f32(rows // 2, width)] * 2
+        [strided(rows), strided(rows // 2)] * 2
         + fine_scratch
         + [pltpu.SemaphoreType.DMA((4,))],
         arguments,
@@ -619,14 +623,14 @@
 
     panel_rows = [(seq_count >> (level - 2)) * BLOCK for level in range(2, top_level + 1)]
     panel_rows = panel_rows if top_level > 2 else []
-    pools = [f32(BLOCK, width)] * 4 + [f32(r, width) for r in panel_rows[:1]]
+    pools = [strided(BLOCK)] * 4 + [strided(r) for r in panel_rows[:1]]
     for level in range(top_level - 1, -1, -1):
-        pools += [f32(rows >> level, width)] * 3
+        pools += [strided(rows >> level)] * 3
     for level in range(top_level):
-        pools += [f32(rows >> level, width)] * 2
+        pools += [strided(rows >> level)] * 2
     for level in range(top_level - 1, -1, -1):
-        pools += [f32(rows >> level, width)]
-    pools += [f32(BLOCK, width)] * 4
+        pools += [strided(rows >> level)]
+    pools += [strided(BLOCK)] * 4
     main = call(
         functools.partial(main_kernel, seq_count, top_level),
         [shape(rows, width)]
@@ -658,7 +662,11 @@
             shape(*((2,) if d in paired(head_count) else ()), 3, share, width)
             for d in [0] + order
         ],
-        [f32(2, rows, width), f32(2, rows // 2, width), f32(2, rows // 4, width)],
+        [
+            f32(2, rows + SPARE, width),
+            f32(2, rows // 2 + SPARE, width),
+            f32(2, rows // 4, width),
+        ],
         (grad_query, local, *returned),
     )
     parts = dict(zip(order, swap_all(parts, "head", order)))

time: 35.1 us -> 35.1 us (level)
  no operation moved by 1% of the time
where the time goes in v8:
time: 35.1 us; the launch traced here: 34.8 us
  starting transfers between devices  15.5 us (44%)
  waiting for transfers between devices  9.93 us (28%)
  Pallas kernels  8.66 us (25%)
  between operations  0.69 us (2%)
    ppermute x13, starting transfers between devices, swap_all(): lax.ppermute(x, axis, [(i, i ^ d) for i in range(size)])  15.5 us
    ppermute x13, waiting for transfers between devices, swap_all(): lax.ppermute(x, axis, [(i, i ^ d) for i in range(size)])  9.93 us
    pallas_call x7, Pallas kernels, call(): pl.pallas_call(kernel, out_shape=outs, in_specs=[pl.BlockSpec(memory_spac...  8.66 us
  transfers between devices with their start and end apart: 13, of which 5 were waited for; matrix products, arithmetic and copies ran while one was open for 0% of the time, Pallas kernels for 6%

profile of v8, /device:TPU:0, one launch (start us, length us, event | category | flops | bytes accessed | tf_op | source)
XLA Modules:
  0.0 34.8 jit_solution(14591028819394199403)
XLA Ops:
  0.6 2.8 %shard_map.75 = (bf16[4,512,128]{2,1,0:T(8,128)(2,1)S(1)}, f32[3,512,128]{2,1,0:T(8,128)S(1)}, bf16[256,128]{1,0:T(8,128)(2,1)S(1)}, bf16[128,128]{1,0:T(8,128)(...) custom-call(bf16[512,128]{1,0:T(8,128)(2,1)} %refs_0_.1, ...), custom_call_target="tpu_custom_call" | custom-call | bytes 1048576 | tf_op jit(solution)/shard_map/pallas_call | solution.py:562
  3.4 4.0 %collective-permute-start = (bf16[2,320,128]{2,1,0:T(8,128)(2,1)S(1)}, bf16[2,320,128]{2,1,0:T(8,128)(2,1)S(1)}, u32[]{:S(2)}, u32[]{:S(2)}) collective-permute-start(bf16[2,320,128]{2,1,0:T(8,128)(2,1)S(1)} %get-tuple-element.43), channel_id=1, source_target_pairs={{0,24},{8,16},{16,8},{24,0},{1,25},{9,17},{17,9},{25,1},{2,26},{10... | collective-permute-start | bytes 491528 | tf_op jit(solution)/shard_map/ppermute | solution.py:578
  7.4 0.5 %collective-permute-start.1 = (bf16[2,320,128]{2,1,0:T(8,128)(2,1)S(1)}, bf16[2,320,128]{2,1,0:T(8,128)(2,1)S(1)}, u32[]{:S(2)}, u32[]{:S(2)}) collective-permute-start(bf16[2,320,128]{2,1,0:T(8,128)(2,1)S(1)} %get-tuple-element.44), channel_id=1, source_target_pairs={{0,8},{8,0},{16,24},{24,16},{1,9},{9,1},{17,25},{25,17},{2,10},{10... | collective-permute-start | bytes 491528 | tf_op jit(solution)/shard_map/ppermute | solution.py:578
  7.9 0.1 collective-permute-start.2
  8.0 0.1 shard_map.76
  8.1 4.3 %collective-permute-done.2.refs_6_ = bf16[2,128,128]{2,1,0:T(8,128)(2,1)S(1)} collective-permute-done((bf16[2,128,128]{2,1,0:T(8,128)(2,1)S(1)}, bf16[2,128,128]{2,1,0:T(8,128)(2,1)S(1)}, u32[]{:S(2)}, u32[]{:S(2)}) %collective-permute-start.2) | collective-permute-done | bytes 65568 | tf_op jit(solution)/shard_map/ppermute | solution.py:578
  12.4 1.3 %collective-permute-done.1.refs_5_ = bf16[2,320,128]{2,1,0:T(8,128)(2,1)S(1)} collective-permute-done((bf16[2,320,128]{2,1,0:T(8,128)(2,1)S(1)}, bf16[2,320,128]{2,1,0:T(8,128)(2,1)S(1)}, u32[]{:S(2)}, u32[]{:S(2)}) %collective-permute-start.1) | collective-permute-done | bytes 163872 | tf_op jit(solution)/shard_map/ppermute | solution.py:578
  13.7 2.8 %shard_map.77 = (bf16[512,128]{1,0:T(8,128)(2,1)S(1)}, bf16[2,320,128]{2,1,0:T(8,128)(2,1)S(1)}, bf16[2,320,128]{2,1,0:T(8,128)(2,1)S(1)}, bf16[2,128,128]{2,1,0...) custom-call(bf16[4,512,128]{2,1,0:T(8,128)(2,1)S(1)} %get-tuple-element.36.held.refs_0_, ...), custom_call_target="tpu_custom_call" | custom-call | flops 293601280 | bytes 1048576 | tf_op jit(solution)/shard_map/pallas_call | solution.py:562
  16.6 1.5 %collective-permute-start.3 = (bf16[2,320,128]{2,1,0:T(8,128)(2,1)S(1)}, bf16[2,320,128]{2,1,0:T(8,128)(2,1)S(1)}, u32[]{:S(2)}, u32[]{:S(2)}) collective-permute-start(bf16[2,320,128]{2,1,0:T(8,128)(2,1)S(1)} %get-tuple-element.52), channel_id=1, source_target_pairs={{0,24},{8,16},{16,8},{24,0},{1,25},{9,17},{17,9},{25,1},{2,26},{10... | collective-permute-start | bytes 491528 | tf_op jit(solution)/shard_map/ppermute | solution.py:578
  18.0 0.3 collective-permute-start.4
  18.4 1.8 %collective-permute-start.5 = (bf16[2,128,128]{2,1,0:T(8,128)(2,1)S(1)}, bf16[2,128,128]{2,1,0:T(8,128)(2,1)S(1)}, u32[]{:S(2)}, u32[]{:S(2)}) collective-permute-start(bf16[2,128,128]{2,1,0:T(8,128)(2,1)S(1)} %get-tuple-element.54), channel_id=1, source_target_pairs={{0,16},{8,24},{16,0},{24,8},{1,17},{9,25},{17,1},{25,9},{2,18},{10... | collective-permute-start | bytes 196616 | tf_op jit(solution)/shard_map/ppermute | solution.py:578
  20.1 1.2 %shard_map.78 = (bf16[512,128]{1,0:T(8,128)(2,1)}, f32[2,512,128]{2,1,0:T(8,128)S(1)}, bf16[512,128]{1,0:T(8,128)(2,1)S(1)}) custom-call(bf16[4,512,128]{2,1,0:T(8,128)(2,1)S(1)} %get-tuple-element.36.held.refs_0_, f32[3,512,128]{2,1,0:T(8,128)S(1)} %get-tuple-element.46.back, f32[512,128]{1,0:T(8,128)S(1)} %get-tuple-element.47.partial_ref, ...), custom_call_target="tpu_custom_call" | custom-call | flops 209715200 | bytes 1048576 | tf_op jit(solution)/shard_map/pallas_call | solution.py:562
  21.3 2.2 %collective-permute-done.5.refs_2_ = bf16[2,128,128]{2,1,0:T(8,128)(2,1)S(1)} collective-permute-done((bf16[2,128,128]{2,1,0:T(8,128)(2,1)S(1)}, bf16[2,128,128]{2,1,0:T(8,128)(2,1)S(1)}, u32[]{:S(2)}, u32[]{:S(2)}) %collective-permute-start.5) | collective-permute-done | bytes 65568 | tf_op jit(solution)/shard_map/ppermute | solution.py:578
  23.6 0.2 shard_map.79
  23.8 2.7 %collective-permute-start.6 = (bf16[2,3,64,128]{3,2,1,0:T(8,128)(2,1)S(1)}, bf16[2,3,64,128]{3,2,1,0:T(8,128)(2,1)S(1)}, u32[]{:S(2)}, u32[]{:S(2)}) collective-permute-start(bf16[2,3,64,128]{3,2,1,0:T(8,128)(2,1)S(1)} %get-tuple-element.56), channel_id=1, source_target_pairs={{0,4},{1,5},{2,6},{3,7},{4,0},{5,1},{6,2},{7,3},{8,12},{9,13},{10,... | collective-permute-start | bytes 294920 | tf_op jit(solution)/shard_map/ppermute | solution.py:578
  26.5 1.3 %collective-permute-start.7 = (bf16[3,64,128]{2,1,0:T(8,128)(2,1)S(1)}, bf16[3,64,128]{2,1,0:T(8,128)(2,1)S(1)}, u32[]{:S(2)}, u32[]{:S(2)}) collective-permute-start(bf16[3,64,128]{2,1,0:T(8,128)(2,1)S(1)} %get-tuple-element.57), channel_id=1, source_target_pairs={{0,6},{1,7},{2,4},{3,5},{4,2},{5,3},{6,0},{7,1},{8,14},{9,15},{10,... | collective-permute-start | bytes 147464 | tf_op jit(solution)/shard_map/ppermute | solution.py:578
  27.9 0.2 collective-permute-start.8
  28.1 3.1 %collective-permute-start.10 = (bf16[3,64,128]{2,1,0:T(8,128)(2,1)S(1)}, bf16[3,64,128]{2,1,0:T(8,128)(2,1)S(1)}, u32[]{:S(2)}, u32[]{:S(2)}) collective-permute-start(bf16[3,64,128]{2,1,0:T(8,128)(2,1)S(1)} %get-tuple-element.63), channel_id=1, source_target_pairs={{0,3},{1,2},{2,1},{3,0},{4,7},{5,6},{6,5},{7,4},{8,11},{9,10},{10,... | collective-permute-start | bytes 147464 | tf_op jit(solution)/shard_map/ppermute | solution.py:578
  31.2 1.3 %collective-permute-done.7.refs_2_ = bf16[3,64,128]{2,1,0:T(8,128)(2,1)S(1)} collective-permute-done((bf16[3,64,128]{2,1,0:T(8,128)(2,1)S(1)}, bf16[3,64,128]{2,1,0:T(8,128)(2,1)S(1)}, u32[]{:S(2)}, u32[]{:S(2)}) %collective-permute-start.7) | collective-permute-done | bytes 49184 | tf_op jit(solution)/shard_map/ppermute | solution.py:578
  32.5 0.0 collective-permute-start.12
  32.5 0.0 collective-permute-done.8.refs_3_
  32.5 0.8 %shard_map.80 = (bf16[64,1024]{1,0:T(8,128)(2,1)}, bf16[64,1024]{1,0:T(8,128)(2,1)}, bf16[64,1024]{1,0:T(8,128)(2,1)}) custom-call(bf16[3,64,128]{2,1,0:T(8,128)(2,1)S(1)} %get-tuple-element.55.refs_0_, bf16[2,3,64,128]{3,2,1,0:T(8,128)(2,1)S(1)} %collective-permute-done.6.refs_1_, bf16[3,64,128]{2,1,0:T(8,128)(2,1)S(1)} %collective-permute-done.7.refs_2_, ...), custom_call_target="tpu_custom_call" | custom-call | flops 209715200 | bytes 1048576 | tf_op jit(solution)/shard_map/pallas_call | solution.py:562
  33.3 0.7 %collective-permute-done.9.refs_3_ = bf16[3,64,128]{2,1,0:T(8,128)(2,1)S(1)} collective-permute-done((bf16[3,64,128]{2,1,0:T(8,128)(2,1)S(1)}, bf16[3,64,128]{2,1,0:T(8,128)(2,1)S(1)}, u32[]{:S(2)}, u32[]{:S(2)}) %collective-permute-start.9) | collective-permute-done | bytes 49184 | tf_op jit(solution)/shard_map/ppermute | solution.py:578
  34.0 0.8 %shard_map.81 = (bf16[64,1024]{1,0:T(8,128)(2,1)}, bf16[64,1024]{1,0:T(8,128)(2,1)}, bf16[64,1024]{1,0:T(8,128)(2,1)}) custom-call(bf16[64,1024]{1,0:T(8,128)(2,1)} %get-tuple-element.59.refs_0_, bf16[64,1024]{1,0:T(8,128)(2,1)} %get-tuple-element.60.refs_1_, ...), custom_call_target="tpu_custom_call", output_to_operand_aliasing={{0}: (0, {}), {1}: (1, {}), {2}: (2, {})} | custom-call | bytes 1048576 | tf_op jit(solution)/shard_map/pallas_call | solution.py:562
  (10 shorter events, 0.0 us)
Async XLA Ops:
  3.4 9.0 %collective-permute-start = (bf16[2,320,128]{2,1,0:T(8,128)(2,1)S(1)}, bf16[2,320,128]{2,1,0:T(8,128)(2,1)S(1)}, u32[]{:S(2)}, u32[]{:S(2)}) collective-permute-start(bf16[2,320,128]{2,1,0:T(8,128)(2,1)S(1)} %get-tuple-element.43), channel_id=1, source_target_pairs={{0,24},{8,16},{16,8},{24,0},{1,25},{9,17},{17,9},{25,1},{2,26},{10... | collective-permute-start | bytes 491528 | tf_op jit(solution)/shard_map/ppermute | solution.py:578
  7.4 6.4 %collective-permute-start.1 = (bf16[2,320,128]{2,1,0:T(8,128)(2,1)S(1)}, bf16[2,320,128]{2,1,0:T(8,128)(2,1)S(1)}, u32[]{:S(2)}, u32[]{:S(2)}) collective-permute-start(bf16[2,320,128]{2,1,0:T(8,128)(2,1)S(1)} %get-tuple-element.44), channel_id=1, source_target_pairs={{0,8},{8,0},{16,24},{24,16},{1,9},{9,1},{17,25},{25,17},{2,10},{10... | collective-permute-start | bytes 491528 | tf_op jit(solution)/shard_map/ppermute | solution.py:578
  7.9 4.5 %collective-permute-start.2 = (bf16[2,128,128]{2,1,0:T(8,128)(2,1)S(1)}, bf16[2,128,128]{2,1,0:T(8,128)(2,1)S(1)}, u32[]{:S(2)}, u32[]{:S(2)}) collective-permute-start(bf16[2,128,128]{2,1,0:T(8,128)(2,1)S(1)} %get-tuple-element.45), channel_id=1, source_target_pairs={{0,16},{8,24},{16,0},{24,8},{1,17},{9,25},{17,1},{25,9},{2,18},{10... | collective-permute-start | bytes 196616 | tf_op jit(solution)/shard_map/ppermute | solution.py:578
  16.6 7.0 %collective-permute-start.3 = (bf16[2,320,128]{2,1,0:T(8,128)(2,1)S(1)}, bf16[2,320,128]{2,1,0:T(8,128)(2,1)S(1)}, u32[]{:S(2)}, u32[]{:S(2)}) collective-permute-start(bf16[2,320,128]{2,1,0:T(8,128)(2,1)S(1)} %get-tuple-element.52), channel_id=1, source_target_pairs={{0,24},{8,16},{16,8},{24,0},{1,25},{9,17},{17,9},{25,1},{2,26},{10... | collective-permute-start | bytes 491528 | tf_op jit(solution)/shard_map/ppermute | solution.py:578
  18.0 5.5 %collective-permute-start.4 = (bf16[2,320,128]{2,1,0:T(8,128)(2,1)S(1)}, bf16[2,320,128]{2,1,0:T(8,128)(2,1)S(1)}, u32[]{:S(2)}, u32[]{:S(2)}) collective-permute-start(bf16[2,320,128]{2,1,0:T(8,128)(2,1)S(1)} %get-tuple-element.53), channel_id=1, source_target_pairs={{0,8},{8,0},{16,24},{24,16},{1,9},{9,1},{17,25},{25,17},{2,10},{10... | collective-permute-start | bytes 491528 | tf_op jit(solution)/shard_map/ppermute | solution.py:578
  18.4 5.2 %collective-permute-start.5 = (bf16[2,128,128]{2,1,0:T(8,128)(2,1)S(1)}, bf16[2,128,128]{2,1,0:T(8,128)(2,1)S(1)}, u32[]{:S(2)}, u32[]{:S(2)}) collective-permute-start(bf16[2,128,128]{2,1,0:T(8,128)(2,1)S(1)} %get-tuple-element.54), channel_id=1, source_target_pairs={{0,16},{8,24},{16,0},{24,8},{1,17},{9,25},{17,1},{25,9},{2,18},{10... | collective-permute-start | bytes 196616 | tf_op jit(solution)/shard_map/ppermute | solution.py:578
  23.8 7.4 %collective-permute-start.6 = (bf16[2,3,64,128]{3,2,1,0:T(8,128)(2,1)S(1)}, bf16[2,3,64,128]{3,2,1,0:T(8,128)(2,1)S(1)}, u32[]{:S(2)}, u32[]{:S(2)}) collective-permute-start(bf16[2,3,64,128]{3,2,1,0:T(8,128)(2,1)S(1)} %get-tuple-element.56), channel_id=1, source_target_pairs={{0,4},{1,5},{2,6},{3,7},{4,0},{5,1},{6,2},{7,3},{8,12},{9,13},{10,... | collective-permute-start | bytes 294920 | tf_op jit(solution)/shard_map/ppermute | solution.py:578
  26.5 6.0 %collective-permute-start.7 = (bf16[3,64,128]{2,1,0:T(8,128)(2,1)S(1)}, bf16[3,64,128]{2,1,0:T(8,128)(2,1)S(1)}, u32[]{:S(2)}, u32[]{:S(2)}) collective-permute-start(bf16[3,64,128]{2,1,0:T(8,128)(2,1)S(1)} %get-tuple-element.57), channel_id=1, source_target_pairs={{0,6},{1,7},{2,4},{3,5},{4,2},{5,3},{6,0},{7,1},{8,14},{9,15},{10,... | collective-permute-start | bytes 147464 | tf_op jit(solution)/shard_map/ppermute | solution.py:578
  27.9 4.6 %collective-permute-start.8 = (bf16[3,64,128]{2,1,0:T(8,128)(2,1)S(1)}, bf16[3,64,128]{2,1,0:T(8,128)(2,1)S(1)}, u32[]{:S(2)}, u32[]{:S(2)}) collective-permute-start(bf16[3,64,128]{2,1,0:T(8,128)(2,1)S(1)} %get-tuple-element.58), channel_id=1, source_target_pairs={{0,2},{1,3},{2,0},{3,1},{4,6},{5,7},{6,4},{7,5},{8,10},{9,11},{10,... | collective-permute-start | bytes 147464 | tf_op jit(solution)/shard_map/ppermute | solution.py:578
  28.1 5.9 %collective-permute-start.9 = (bf16[3,64,128]{2,1,0:T(8,128)(2,1)S(1)}, bf16[3,64,128]{2,1,0:T(8,128)(2,1)S(1)}, u32[]{:S(2)}, u32[]{:S(2)}) collective-permute-start(bf16[3,64,128]{2,1,0:T(8,128)(2,1)S(1)} %get-tuple-element.62), channel_id=1, source_target_pairs={{0,7},{1,6},{2,5},{3,4},{4,3},{5,2},{6,1},{7,0},{8,15},{9,14},{10,... | collective-permute-start | bytes 147464 | tf_op jit(solution)/shard_map/ppermute | solution.py:578
  28.1 5.9 %collective-permute-start.10 = (bf16[3,64,128]{2,1,0:T(8,128)(2,1)S(1)}, bf16[3,64,128]{2,1,0:T(8,128)(2,1)S(1)}, u32[]{:S(2)}, u32[]{:S(2)}) collective-permute-start(bf16[3,64,128]{2,1,0:T(8,128)(2,1)S(1)} %get-tuple-element.63), channel_id=1, source_target_pairs={{0,3},{1,2},{2,1},{3,0},{4,7},{5,6},{6,5},{7,4},{8,11},{9,10},{10,... | collective-permute-start | bytes 147464 | tf_op jit(solution)/shard_map/ppermute | solution.py:578
  31.2 2.8 %collective-permute-start.11 = (bf16[3,64,128]{2,1,0:T(8,128)(2,1)S(1)}, bf16[3,64,128]{2,1,0:T(8,128)(2,1)S(1)}, u32[]{:S(2)}, u32[]{:S(2)}) collective-permute-start(bf16[3,64,128]{2,1,0:T(8,128)(2,1)S(1)} %get-tuple-element.64), channel_id=1, source_target_pairs={{0,1},{1,0},{2,3},{3,2},{4,5},{5,4},{6,7},{7,6},{8,9},{9,8},{10,11... | collective-permute-start | bytes 147464 | tf_op jit(solution)/shard_map/ppermute | solution.py:578
  32.5 1.6 %collective-permute-start.12 = (bf16[3,64,128]{2,1,0:T(8,128)(2,1)S(1)}, bf16[3,64,128]{2,1,0:T(8,128)(2,1)S(1)}, u32[]{:S(2)}, u32[]{:S(2)}) collective-permute-start(bf16[3,64,128]{2,1,0:T(8,128)(2,1)S(1)} %slice_bitcast_fusion), channel_id=1, source_target_pairs={{0,1},{1,0},{2,3},{3,2},{4,5},{5,4},{6,7},{7,6},{8,9},{9,8},{10,11... | collective-permute-start | bytes 147464 | tf_op jit(solution)/shard_map/ppermute | solution.py:578

commit v9 on v8

--- a/solution.py
+++ b/solution.py
@@ -204,6 +204,52 @@
         fine_work(held, stats, queries, scratches)
 
 
+def unit(query, pieces, before=None):
+    width = query.shape[1]
+    factor = width ** (-0.5) * LOG2E
+    scores = []
+    for key, _, valid, _ in pieces:
+        score = nt(query, key) * factor
+        scores.append(score if valid is None else jnp.where(valid, score, MASKED))
+    peak = functools.reduce(jnp.maximum, [row_max(score) for score in scores])
+    if before is not None:
+        peak = jnp.maximum(peak, before[0])
+    exps = [jnp.exp2(score - across(peak, score.shape[1])) for score in scores]
+    rounded = [e.astype(BF16) for e in exps]
+    ones = jnp.ones((BLOCK, width), BF16)
+    both = []
+    for r, piece in zip(rounded, pieces):
+        count = piece[1].shape[0] // BLOCK
+        both.append(nn(r, jnp.concatenate([piece[1], jnp.concatenate([ones] * count, axis=0)], axis=1)))
+    both = total_of(both)
+    sums, total = both[:, :width], both[:, width:]
+    if before is not None:
+        keep = jnp.exp2(before[0] - peak)
+        total, sums = total + keep * before[1], sums + keep * before[2]
+    return peak, total, sums, exps, rounded
+
+
+def far_pieces(seq_count, received):
+    seq_index, wides = lax.axis_index("seq"), wide_distances(seq_count)
+    pieces = []
+    for d in range(2, seq_count):
+        apart = jnp.abs((seq_index ^ d) - seq_index) > 1
+        valid = apart if d in wides else None
+        pieces.append((received[d][0, :BLOCK], received[d][1, :BLOCK], valid, d))
+    return pieces
+
+
+def far_kernel(seq_count, query_ref, *refs):
+    order = [d for d in seq_order(seq_count) if d > 1]
+    received, refs = dict(zip(order, refs)), refs[len(order) :]
+    up, exps_ref, scratches = refs[0], refs[1], refs[2:]
+    peak, total, sums, exps, _ = unit(query_ref[...], far_pieces(seq_count, received))
+    for w, value in enumerate((peak, total, sums)):
+        up[w] = spread(value, scratches[w])
+    for p, e in enumerate(exps):
+        exps_ref[p] = e
+
+
 def main_kernel(seq_count, top_level, *refs):
     refs = list(refs)
 
@@ -214,6 +260,7 @@
 
     held, stats = take(2)
     query_refs = take(top_level)
+    up_ref, exps_ref = take(2) if top_level == 2 else (None, None)
     received = dict(zip(seq_order(seq_count), take(seq_count - 1)))
     (attended_ref,) = take(1)
     sends = dict(zip(seq_order(seq_count), take(seq_count - 1)))
@@ -275,10 +322,7 @@
         ],
     ]
     if top_level == 2:
-        pieces = []
-        for d in range(2, seq_count):
-            valid = ~is_neighbour(d) if d in wides else None
-            pieces.append((received[d][0, :BLOCK], received[d][1, :BLOCK], valid, d))
+        pieces = far_pieces(seq_count, received)
         level_pieces.append([pieces])
     else:
         for panel in panels:
@@ -305,28 +349,6 @@
             [query[a * step : (a + 1) * step] for a in range(len(level_pieces[level]))]
         )
 
-    def unit(query, pieces, before=None):
-        scores = []
-        for key, _, valid, _ in pieces:
-            score = nt(query, key) * factor
-            scores.append(score if valid is None else jnp.where(valid, score, MASKED))
-        peak = functools.reduce(jnp.maximum, [row_max(score) for score in scores])
-        if before is not None:
-            peak = jnp.maximum(peak, before[0])
-        exps = [jnp.exp2(score - across(peak, score.shape[1])) for score in scores]
-        rounded = [e.astype(BF16) for e in exps]
-        ones = jnp.ones((BLOCK, width), BF16)
-        both = []
-        for r, piece in zip(rounded, pieces):
-            count = piece[1].shape[0] // BLOCK
-            both.append(nn(r, jnp.concatenate([piece[1], jnp.concatenate([ones] * count, axis=0)], axis=1)))
-        both = total_of(both)
-        sums, total = both[:, :width], both[:, width:]
-        if before is not None:
-            keep = jnp.exp2(before[0] - peak)
-            total, sums = total + keep * before[1], sums + keep * before[2]
-        return peak, total, sums, exps, rounded
-
     def before_of(block):
         return [stats[w, rows_of(block)] for w in range(3)]
 
@@ -337,6 +359,10 @@
         ]
     ]
     for level in range(1, top_level + 1):
+        if level == 2 and top_level == 2:
+            exps = [exps_ref[p] for p in range(exps_ref.shape[0])]
+            level_units.append([(None, None, None, exps, [e.astype(BF16) for e in exps])])
+            continue
         level_units.append(
             [unit(q, pieces) for q, pieces in zip(level_queries[level], level_pieces[level])]
         )
@@ -347,10 +373,13 @@
             units = [units[0], stats[which, rows_of(1, blocks - 2)], units[1]]
         return jnp.concatenate(units, axis=0)
 
-    run = [stacked(top_level, w) for w in range(3)]
+    run = None if top_level == 2 else [stacked(top_level, w) for w in range(3)]
     own_factors, run_factors = [None] * top_level, [None] * top_level
     for level in range(top_level - 1, -1, -1):
-        up_peak, up_total, up_sums = [spread(x, pool()) for x in run]
+        if run is None:
+            up_peak, up_total, up_sums = [up_ref[w] for w in range(3)]
+        else:
+            up_peak, up_total, up_sums = [spread(x, pool()) for x in run]
         peak, total, sums = [stacked(level, w) for w in range(3)]
         both = jnp.maximum(peak, up_peak)
         own = jnp.exp2(peak - both)
@@ -624,13 +653,23 @@
     panel_rows = [(seq_count >> (level - 2)) * BLOCK for level in range(2, top_level + 1)]
     panel_rows = panel_rows if top_level > 2 else []
     pools = [strided(BLOCK)] * 4 + [strided(r) for r in panel_rows[:1]]
-    for level in range(top_level - 1, -1, -1):
+    for level in range(top_level - 1 - (top_level == 2), -1, -1):
         pools += [strided(rows >> level)] * 3
     for level in range(top_level):
         pools += [strided(rows >> level)] * 2
     for level in range(top_level - 1, -1, -1):
         pools += [strided(rows >> level)]
     pools += [strided(BLOCK)] * 4
+    ahead = []
+    if top_level == 2:
+        count = seq_count - 2
+        ahead = call(
+            functools.partial(far_kernel, seq_count),
+            [shape(3, rows // 2, width, dtype=F32), shape(count, rows // 4, BLOCK, dtype=F32)],
+            [strided(rows // 2)] * 3,
+            (level_queries[-1], *[x for d, x in zip(distances, received) if d > 1]),
+            flops=10 * unit_flops,
+        )
     main = call(
         functools.partial(main_kernel, seq_count, top_level),
         [shape(rows, width)]
@@ -639,7 +678,7 @@
         [pltpu.VMEM((2, r, width), BF16) for r in panel_rows]
         + [f32(2, r, width) for r in panel_rows]
         + pools,
-        (held, stats, *level_queries, *received),
+        (held, stats, *level_queries, *ahead, *received),
         flops=70 * unit_flops,
     )
     merged, sends, back, partial = main[0], main[1:seq_count], main[-2], main[-1]

time: 35.1 us -> 35.1 us (level)
  waiting for transfers between devices: 9.93 us -> 9.55 us
    ppermute x13, waiting for transfers between devices: 9.93 us -> 9.55 us  [swap_all(): lax.ppermute(x, axis, [(i, i ^ d) for i in range(size)])]
    pallas_call x7 -> x8, Pallas kernels: 8.66 us -> 8.82 us  [call(): pl.pallas_call(kernel, out_shape=outs, in_specs=[pl.BlockSpec(memory_spac...]
  transfers between devices with their start and end apart: 13 -> 13, of which waited for: 5 -> 6; matrix products, arithmetic and copies ran while one was open for 0% -> 0% of each run, Pallas kernels for 6% -> 7%
where the time goes in v9:
time: 35.1 us; the launch traced here: 34.8 us
  starting transfers between devices  15.7 us (45%)
  waiting for transfers between devices  9.55 us (27%)
  Pallas kernels  8.82 us (25%)
  between operations  0.7 us (2%)
    ppermute x13, starting transfers between devices, swap_all(): lax.ppermute(x, axis, [(i, i ^ d) for i in range(size)])  15.7 us
    ppermute x13, waiting for transfers between devices, swap_all(): lax.ppermute(x, axis, [(i, i ^ d) for i in range(size)])  9.55 us
    pallas_call x8, Pallas kernels, call(): pl.pallas_call(kernel, out_shape=outs, in_specs=[pl.BlockSpec(memory_spac...  8.82 us
  transfers between devices with their start and end apart: 13, of which 6 were waited for; matrix products, arithmetic and copies ran while one was open for 0% of the time, Pallas kernels for 7%

profile of v9, /device:TPU:0, one launch (start us, length us, event | category | flops | bytes accessed | tf_op | source)
XLA Modules:
  0.0 34.8 jit_solution(11535825106853450150)
XLA Ops:
  0.6 2.8 %shard_map.75 = (bf16[4,512,128]{2,1,0:T(8,128)(2,1)S(1)}, f32[3,512,128]{2,1,0:T(8,128)S(1)}, bf16[256,128]{1,0:T(8,128)(2,1)S(1)}, bf16[128,128]{1,0:T(8,128)(...) custom-call(bf16[512,128]{1,0:T(8,128)(2,1)} %refs_0_.1, ...), custom_call_target="tpu_custom_call" | custom-call | bytes 1048576 | tf_op jit(solution)/shard_map/pallas_call | solution.py:591
  3.4 4.0 %collective-permute-start = (bf16[2,320,128]{2,1,0:T(8,128)(2,1)S(1)}, bf16[2,320,128]{2,1,0:T(8,128)(2,1)S(1)}, u32[]{:S(2)}, u32[]{:S(2)}) collective-permute-start(bf16[2,320,128]{2,1,0:T(8,128)(2,1)S(1)} %get-tuple-element.45), channel_id=1, source_target_pairs={{0,24},{8,16},{16,8},{24,0},{1,25},{9,17},{17,9},{25,1},{2,26},{10... | collective-permute-start | bytes 491528 | tf_op jit(solution)/shard_map/ppermute | solution.py:607
  7.4 0.5 %collective-permute-start.2 = (bf16[2,320,128]{2,1,0:T(8,128)(2,1)S(1)}, bf16[2,320,128]{2,1,0:T(8,128)(2,1)S(1)}, u32[]{:S(2)}, u32[]{:S(2)}) collective-permute-start(bf16[2,320,128]{2,1,0:T(8,128)(2,1)S(1)} %get-tuple-element.49), channel_id=1, source_target_pairs={{0,8},{8,0},{16,24},{24,16},{1,9},{9,1},{17,25},{25,17},{2,10},{10... | collective-permute-start | bytes 491528 | tf_op jit(solution)/shard_map/ppermute | solution.py:607
  7.9 0.1 collective-permute-start.1
  8.0 0.1 shard_map.76
  8.1 4.3 %collective-permute-done.1.refs_1_.refs_8_ = bf16[2,128,128]{2,1,0:T(8,128)(2,1)S(1)} collective-permute-done((bf16[2,128,128]{2,1,0:T(8,128)(2,1)S(1)}, bf16[2,128,128]{2,1,0:T(8,128)(2,1)S(1)}, u32[]{:S(2)}, u32[]{:S(2)}) %collective-permute-start.1) | collective-permute-done | bytes 65568 | tf_op jit(solution)/shard_map/ppermute | solution.py:607
  12.4 0.5 %shard_map.77 = (f32[3,256,128]{2,1,0:T(8,128)S(1)}, f32[2,128,128]{2,1,0:T(8,128)S(1)}) custom-call(bf16[128,128]{1,0:T(8,128)(2,1)S(1)} %get-tuple-element.44.query_ref.refs_3_, bf16[2,320,128]{2,1,0:T(8,128)(2,1)S(1)} %collective-permute-done.refs_0_.refs_6_, bf16[2,128,128]{2,1,0:T(8,128)(2,1)S(1)} %collective-permute-done.1.refs_1_.refs_8_), custom_call_target="tpu_custom_call" | custom-call | flops 41943040 | bytes 1048576 | tf_op jit(solution)/shard_map/pallas_call | solution.py:591
  12.9 0.9 %collective-permute-done.2.refs_7_ = bf16[2,320,128]{2,1,0:T(8,128)(2,1)S(1)} collective-permute-done((bf16[2,320,128]{2,1,0:T(8,128)(2,1)S(1)}, bf16[2,320,128]{2,1,0:T(8,128)(2,1)S(1)}, u32[]{:S(2)}, u32[]{:S(2)}) %collective-permute-start.2) | collective-permute-done | bytes 163872 | tf_op jit(solution)/shard_map/ppermute | solution.py:607
  13.7 2.5 %shard_map.78 = (bf16[512,128]{1,0:T(8,128)(2,1)S(1)}, bf16[2,320,128]{2,1,0:T(8,128)(2,1)S(1)}, bf16[2,320,128]{2,1,0:T(8,128)(2,1)S(1)}, bf16[2,128,128]{2,1,0...) custom-call(bf16[4,512,128]{2,1,0:T(8,128)(2,1)S(1)} %get-tuple-element.38.held.refs_0_, ...), custom_call_target="tpu_custom_call" | custom-call | flops 293601280 | bytes 1048576 | tf_op jit(solution)/shard_map/pallas_call | solution.py:591
  16.2 1.7 %collective-permute-start.3 = (bf16[2,320,128]{2,1,0:T(8,128)(2,1)S(1)}, bf16[2,320,128]{2,1,0:T(8,128)(2,1)S(1)}, u32[]{:S(2)}, u32[]{:S(2)}) collective-permute-start(bf16[2,320,128]{2,1,0:T(8,128)(2,1)S(1)} %get-tuple-element.56), channel_id=1, source_target_pairs={{0,24},{8,16},{16,8},{24,0},{1,25},{9,17},{17,9},{25,1},{2,26},{10... | collective-permute-start | bytes 491528 | tf_op jit(solution)/shard_map/ppermute | solution.py:607
  18.0 0.3 collective-permute-start.4
  18.3 1.5 %collective-permute-start.5 = (bf16[2,128,128]{2,1,0:T(8,128)(2,1)S(1)}, bf16[2,128,128]{2,1,0:T(8,128)(2,1)S(1)}, u32[]{:S(2)}, u32[]{:S(2)}) collective-permute-start(bf16[2,128,128]{2,1,0:T(8,128)(2,1)S(1)} %get-tuple-element.58), channel_id=1, source_target_pairs={{0,16},{8,24},{16,0},{24,8},{1,17},{9,25},{17,1},{25,9},{2,18},{10... | collective-permute-start | bytes 196616 | tf_op jit(solution)/shard_map/ppermute | solution.py:607
  19.8 1.2 %shard_map.79 = (bf16[512,128]{1,0:T(8,128)(2,1)}, f32[2,512,128]{2,1,0:T(8,128)S(1)}, bf16[512,128]{1,0:T(8,128)(2,1)S(1)}) custom-call(bf16[4,512,128]{2,1,0:T(8,128)(2,1)S(1)} %get-tuple-element.38.held.refs_0_, f32[3,512,128]{2,1,0:T(8,128)S(1)} %get-tuple-element.50.back, f32[512,128]{1,0:T(8,128)S(1)} %get-tuple-element.51.partial_ref, ...), custom_call_target="tpu_custom_call" | custom-call | flops 209715200 | bytes 1048576 | tf_op jit(solution)/shard_map/pallas_call | solution.py:591
  21.0 2.2 %collective-permute-done.5.refs_2_ = bf16[2,128,128]{2,1,0:T(8,128)(2,1)S(1)} collective-permute-done((bf16[2,128,128]{2,1,0:T(8,128)(2,1)S(1)}, bf16[2,128,128]{2,1,0:T(8,128)(2,1)S(1)}, u32[]{:S(2)}, u32[]{:S(2)}) %collective-permute-start.5) | collective-permute-done | bytes 65568 | tf_op jit(solution)/shard_map/ppermute | solution.py:607
  23.2 0.1 collective-permute-done.4.refs_1_
  23.3 0.2 shard_map.80
  23.6 2.9 %collective-permute-start.6 = (bf16[2,3,64,128]{3,2,1,0:T(8,128)(2,1)S(1)}, bf16[2,3,64,128]{3,2,1,0:T(8,128)(2,1)S(1)}, u32[]{:S(2)}, u32[]{:S(2)}) collective-permute-start(bf16[2,3,64,128]{3,2,1,0:T(8,128)(2,1)S(1)} %get-tuple-element.60), channel_id=1, source_target_pairs={{0,4},{1,5},{2,6},{3,7},{4,0},{5,1},{6,2},{7,3},{8,12},{9,13},{10,... | collective-permute-start | bytes 294920 | tf_op jit(solution)/shard_map/ppermute | solution.py:607
  26.4 1.3 %collective-permute-start.7 = (bf16[3,64,128]{2,1,0:T(8,128)(2,1)S(1)}, bf16[3,64,128]{2,1,0:T(8,128)(2,1)S(1)}, u32[]{:S(2)}, u32[]{:S(2)}) collective-permute-start(bf16[3,64,128]{2,1,0:T(8,128)(2,1)S(1)} %get-tuple-element.61), channel_id=1, source_target_pairs={{0,6},{1,7},{2,4},{3,5},{4,2},{5,3},{6,0},{7,1},{8,14},{9,15},{10,... | collective-permute-start | bytes 147464 | tf_op jit(solution)/shard_map/ppermute | solution.py:607
  27.8 0.2 collective-permute-start.8
  28.0 3.1 %collective-permute-start.10 = (bf16[3,64,128]{2,1,0:T(8,128)(2,1)S(1)}, bf16[3,64,128]{2,1,0:T(8,128)(2,1)S(1)}, u32[]{:S(2)}, u32[]{:S(2)}) collective-permute-start(bf16[3,64,128]{2,1,0:T(8,128)(2,1)S(1)} %get-tuple-element.67), channel_id=1, source_target_pairs={{0,3},{1,2},{2,1},{3,0},{4,7},{5,6},{6,5},{7,4},{8,11},{9,10},{10,... | collective-permute-start | bytes 147464 | tf_op jit(solution)/shard_map/ppermute | solution.py:607
  31.1 1.3 %collective-permute-done.7.refs_2_ = bf16[3,64,128]{2,1,0:T(8,128)(2,1)S(1)} collective-permute-done((bf16[3,64,128]{2,1,0:T(8,128)(2,1)S(1)}, bf16[3,64,128]{2,1,0:T(8,128)(2,1)S(1)}, u32[]{:S(2)}, u32[]{:S(2)}) %collective-permute-start.7) | collective-permute-done | bytes 49184 | tf_op jit(solution)/shard_map/ppermute | solution.py:607
  32.4 0.8 %shard_map.81 = (bf16[64,1024]{1,0:T(8,128)(2,1)}, bf16[64,1024]{1,0:T(8,128)(2,1)}, bf16[64,1024]{1,0:T(8,128)(2,1)}) custom-call(bf16[3,64,128]{2,1,0:T(8,128)(2,1)S(1)} %get-tuple-element.59.refs_0_, bf16[2,3,64,128]{3,2,1,0:T(8,128)(2,1)S(1)} %collective-permute-done.6.refs_1_, bf16[3,64,128]{2,1,0:T(8,128)(2,1)S(1)} %collective-permute-done.7.refs_2_, ...), custom_call_target="tpu_custom_call" | custom-call | flops 209715200 | bytes 1048576 | tf_op jit(solution)/shard_map/pallas_call | solution.py:591
  33.2 0.7 %collective-permute-done.9.refs_3_ = bf16[3,64,128]{2,1,0:T(8,128)(2,1)S(1)} collective-permute-done((bf16[3,64,128]{2,1,0:T(8,128)(2,1)S(1)}, bf16[3,64,128]{2,1,0:T(8,128)(2,1)S(1)}, u32[]{:S(2)}, u32[]{:S(2)}) %collective-permute-start.9) | collective-permute-done | bytes 49184 | tf_op jit(solution)/shard_map/ppermute | solution.py:607
  34.0 0.8 %shard_map.82 = (bf16[64,1024]{1,0:T(8,128)(2,1)}, bf16[64,1024]{1,0:T(8,128)(2,1)}, bf16[64,1024]{1,0:T(8,128)(2,1)}) custom-call(bf16[64,1024]{1,0:T(8,128)(2,1)} %get-tuple-element.63.refs_0_, bf16[64,1024]{1,0:T(8,128)(2,1)} %get-tuple-element.64.refs_1_, ...), custom_call_target="tpu_custom_call", output_to_operand_aliasing={{0}: (0, {}), {1}: (1, {}), {2}: (2, {})} | custom-call | bytes 1048576 | tf_op jit(solution)/shard_map/pallas_call | solution.py:591
  (11 shorter events, 0.0 us)
Async XLA Ops:
  3.4 9.0 %collective-permute-start = (bf16[2,320,128]{2,1,0:T(8,128)(2,1)S(1)}, bf16[2,320,128]{2,1,0:T(8,128)(2,1)S(1)}, u32[]{:S(2)}, u32[]{:S(2)}) collective-permute-start(bf16[2,320,128]{2,1,0:T(8,128)(2,1)S(1)} %get-tuple-element.45), channel_id=1, source_target_pairs={{0,24},{8,16},{16,8},{24,0},{1,25},{9,17},{17,9},{25,1},{2,26},{10... | collective-permute-start | bytes 491528 | tf_op jit(solution)/shard_map/ppermute | solution.py:607
  7.4 6.4 %collective-permute-start.2 = (bf16[2,320,128]{2,1,0:T(8,128)(2,1)S(1)}, bf16[2,320,128]{2,1,0:T(8,128)(2,1)S(1)}, u32[]{:S(2)}, u32[]{:S(2)}) collective-permute-start(bf16[2,320,128]{2,1,0:T(8,128)(2,1)S(1)} %get-tuple-element.49), channel_id=1, source_target_pairs={{0,8},{8,0},{16,24},{24,16},{1,9},{9,1},{17,25},{25,17},{2,10},{10... | collective-permute-start | bytes 491528 | tf_op jit(solution)/shard_map/ppermute | solution.py:607
  7.9 4.5 %collective-permute-start.1 = (bf16[2,128,128]{2,1,0:T(8,128)(2,1)S(1)}, bf16[2,128,128]{2,1,0:T(8,128)(2,1)S(1)}, u32[]{:S(2)}, u32[]{:S(2)}) collective-permute-start(bf16[2,128,128]{2,1,0:T(8,128)(2,1)S(1)} %get-tuple-element.46), channel_id=1, source_target_pairs={{0,16},{8,24},{16,0},{24,8},{1,17},{9,25},{17,1},{25,9},{2,18},{10... | collective-permute-start | bytes 196616 | tf_op jit(solution)/shard_map/ppermute | solution.py:607
  16.2 7.0 %collective-permute-start.3 = (bf16[2,320,128]{2,1,0:T(8,128)(2,1)S(1)}, bf16[2,320,128]{2,1,0:T(8,128)(2,1)S(1)}, u32[]{:S(2)}, u32[]{:S(2)}) collective-permute-start(bf16[2,320,128]{2,1,0:T(8,128)(2,1)S(1)} %get-tuple-element.56), channel_id=1, source_target_pairs={{0,24},{8,16},{16,8},{24,0},{1,25},{9,17},{17,9},{25,1},{2,26},{10... | collective-permute-start | bytes 491528 | tf_op jit(solution)/shard_map/ppermute | solution.py:607
  18.0 5.4 %collective-permute-start.4 = (bf16[2,320,128]{2,1,0:T(8,128)(2,1)S(1)}, bf16[2,320,128]{2,1,0:T(8,128)(2,1)S(1)}, u32[]{:S(2)}, u32[]{:S(2)}) collective-permute-start(bf16[2,320,128]{2,1,0:T(8,128)(2,1)S(1)} %get-tuple-element.57), channel_id=1, source_target_pairs={{0,8},{8,0},{16,24},{24,16},{1,9},{9,1},{17,25},{25,17},{2,10},{10... | collective-permute-start | bytes 491528 | tf_op jit(solution)/shard_map/ppermute | solution.py:607
  18.3 4.9 %collective-permute-start.5 = (bf16[2,128,128]{2,1,0:T(8,128)(2,1)S(1)}, bf16[2,128,128]{2,1,0:T(8,128)(2,1)S(1)}, u32[]{:S(2)}, u32[]{:S(2)}) collective-permute-start(bf16[2,128,128]{2,1,0:T(8,128)(2,1)S(1)} %get-tuple-element.58), channel_id=1, source_target_pairs={{0,16},{8,24},{16,0},{24,8},{1,17},{9,25},{17,1},{25,9},{2,18},{10... | collective-permute-start | bytes 196616 | tf_op jit(solution)/shard_map/ppermute | solution.py:607
  23.6 7.5 %collective-permute-start.6 = (bf16[2,3,64,128]{3,2,1,0:T(8,128)(2,1)S(1)}, bf16[2,3,64,128]{3,2,1,0:T(8,128)(2,1)S(1)}, u32[]{:S(2)}, u32[]{:S(2)}) collective-permute-start(bf16[2,3,64,128]{3,2,1,0:T(8,128)(2,1)S(1)} %get-tuple-element.60), channel_id=1, source_target_pairs={{0,4},{1,5},{2,6},{3,7},{4,0},{5,1},{6,2},{7,3},{8,12},{9,13},{10,... | collective-permute-start | bytes 294920 | tf_op jit(solution)/shard_map/ppermute | solution.py:607
  26.4 6.0 %collective-permute-start.7 = (bf16[3,64,128]{2,1,0:T(8,128)(2,1)S(1)}, bf16[3,64,128]{2,1,0:T(8,128)(2,1)S(1)}, u32[]{:S(2)}, u32[]{:S(2)}) collective-permute-start(bf16[3,64,128]{2,1,0:T(8,128)(2,1)S(1)} %get-tuple-element.61), channel_id=1, source_target_pairs={{0,6},{1,7},{2,4},{3,5},{4,2},{5,3},{6,0},{7,1},{8,14},{9,15},{10,... | collective-permute-start | bytes 147464 | tf_op jit(solution)/shard_map/ppermute | solution.py:607
  27.8 4.6 %collective-permute-start.8 = (bf16[3,64,128]{2,1,0:T(8,128)(2,1)S(1)}, bf16[3,64,128]{2,1,0:T(8,128)(2,1)S(1)}, u32[]{:S(2)}, u32[]{:S(2)}) collective-permute-start(bf16[3,64,128]{2,1,0:T(8,128)(2,1)S(1)} %get-tuple-element.62), channel_id=1, source_target_pairs={{0,2},{1,3},{2,0},{3,1},{4,6},{5,7},{6,4},{7,5},{8,10},{9,11},{10,... | collective-permute-start | bytes 147464 | tf_op jit(solution)/shard_map/ppermute | solution.py:607
  28.0 5.9 %collective-permute-start.9 = (bf16[3,64,128]{2,1,0:T(8,128)(2,1)S(1)}, bf16[3,64,128]{2,1,0:T(8,128)(2,1)S(1)}, u32[]{:S(2)}, u32[]{:S(2)}) collective-permute-start(bf16[3,64,128]{2,1,0:T(8,128)(2,1)S(1)} %get-tuple-element.66), channel_id=1, source_target_pairs={{0,7},{1,6},{2,5},{3,4},{4,3},{5,2},{6,1},{7,0},{8,15},{9,14},{10,... | collective-permute-start | bytes 147464 | tf_op jit(solution)/shard_map/ppermute | solution.py:607
  28.0 5.9 %collective-permute-start.10 = (bf16[3,64,128]{2,1,0:T(8,128)(2,1)S(1)}, bf16[3,64,128]{2,1,0:T(8,128)(2,1)S(1)}, u32[]{:S(2)}, u32[]{:S(2)}) collective-permute-start(bf16[3,64,128]{2,1,0:T(8,128)(2,1)S(1)} %get-tuple-element.67), channel_id=1, source_target_pairs={{0,3},{1,2},{2,1},{3,0},{4,7},{5,6},{6,5},{7,4},{8,11},{9,10},{10,... | collective-permute-start | bytes 147464 | tf_op jit(solution)/shard_map/ppermute | solution.py:607
  31.1 2.8 %collective-permute-start.11 = (bf16[3,64,128]{2,1,0:T(8,128)(2,1)S(1)}, bf16[3,64,128]{2,1,0:T(8,128)(2,1)S(1)}, u32[]{:S(2)}, u32[]{:S(2)}) collective-permute-start(bf16[3,64,128]{2,1,0:T(8,128)(2,1)S(1)} %get-tuple-element.68), channel_id=1, source_target_pairs={{0,1},{1,0},{2,3},{3,2},{4,5},{5,4},{6,7},{7,6},{8,9},{9,8},{10,11... | collective-permute-start | bytes 147464 | tf_op jit(solution)/shard_map/ppermute | solution.py:607
  32.4 1.6 %collective-permute-start.12 = (bf16[3,64,128]{2,1,0:T(8,128)(2,1)S(1)}, bf16[3,64,128]{2,1,0:T(8,128)(2,1)S(1)}, u32[]{:S(2)}, u32[]{:S(2)}) collective-permute-start(bf16[3,64,128]{2,1,0:T(8,128)(2,1)S(1)} %slice_bitcast_fusion), channel_id=1, source_target_pairs={{0,1},{1,0},{2,3},{3,2},{4,5},{5,4},{6,7},{7,6},{8,9},{9,8},{10,11... | collective-permute-start | bytes 147464 | tf_op jit(solution)/shard_map/ppermute | solution.py:607

commit v10 on v9

--- a/solution.py
+++ b/solution.py
@@ -164,7 +164,7 @@
     blocks, width = held.shape[1] // BLOCK, held.shape[2]
     factor = width ** (-0.5) * LOG2E
 
-    @pl.loop(0, blocks)
+    @pl.loop(0, blocks, unroll=2)
     def _(a):
         lo = jnp.clip(a - 1, 0, blocks - 3)
         own = pl.ds(pl.multiple_of(a * BLOCK, BLOCK), BLOCK)

time: 35.1 us -> 34.9 us (level)
  waiting for transfers between devices: 9.55 us -> 9.98 us
    ppermute x13, waiting for transfers between devices: 9.55 us -> 9.98 us  [swap_all(): lax.ppermute(x, axis, [(i, i ^ d) for i in range(size)])]
where the time goes in v10:
time: 34.9 us; the launch traced here: 34.6 us
  starting transfers between devices  15.4 us (44%)
  waiting for transfers between devices  9.98 us (29%)
  Pallas kernels  8.54 us (24%)
  between operations  0.69 us (2%)
    ppermute x13, starting transfers between devices, swap_all(): lax.ppermute(x, axis, [(i, i ^ d) for i in range(size)])  15.4 us
    ppermute x13, waiting for transfers between devices, swap_all(): lax.ppermute(x, axis, [(i, i ^ d) for i in range(size)])  9.98 us
    pallas_call x8, Pallas kernels, call(): pl.pallas_call(kernel, out_shape=outs, in_specs=[pl.BlockSpec(memory_spac...  8.54 us
  transfers between devices with their start and end apart: 13, of which 6 were waited for; matrix products, arithmetic and copies ran while one was open for 0% of the time, Pallas kernels for 7%

profile of v10, /device:TPU:0, one launch (start us, length us, event | category | flops | bytes accessed | tf_op | source)
XLA Modules:
  0.0 34.6 jit_solution(18179397071434992564)
XLA Ops:
  0.6 2.5 %shard_map.75 = (bf16[4,512,128]{2,1,0:T(8,128)(2,1)S(1)}, f32[3,512,128]{2,1,0:T(8,128)S(1)}, bf16[256,128]{1,0:T(8,128)(2,1)S(1)}, bf16[128,128]{1,0:T(8,128)(...) custom-call(bf16[512,128]{1,0:T(8,128)(2,1)} %refs_0_.1, ...), custom_call_target="tpu_custom_call" | custom-call | bytes 1048576 | tf_op jit(solution)/shard_map/pallas_call | solution.py:591
  3.1 4.0 %collective-permute-start = (bf16[2,320,128]{2,1,0:T(8,128)(2,1)S(1)}, bf16[2,320,128]{2,1,0:T(8,128)(2,1)S(1)}, u32[]{:S(2)}, u32[]{:S(2)}) collective-permute-start(bf16[2,320,128]{2,1,0:T(8,128)(2,1)S(1)} %get-tuple-element.45), channel_id=1, source_target_pairs={{0,24},{8,16},{16,8},{24,0},{1,25},{9,17},{17,9},{25,1},{2,26},{10... | collective-permute-start | bytes 491528 | tf_op jit(solution)/shard_map/ppermute | solution.py:607
  7.1 0.5 %collective-permute-start.2 = (bf16[2,320,128]{2,1,0:T(8,128)(2,1)S(1)}, bf16[2,320,128]{2,1,0:T(8,128)(2,1)S(1)}, u32[]{:S(2)}, u32[]{:S(2)}) collective-permute-start(bf16[2,320,128]{2,1,0:T(8,128)(2,1)S(1)} %get-tuple-element.49), channel_id=1, source_target_pairs={{0,8},{8,0},{16,24},{24,16},{1,9},{9,1},{17,25},{25,17},{2,10},{10... | collective-permute-start | bytes 491528 | tf_op jit(solution)/shard_map/ppermute | solution.py:607
  7.6 0.1 collective-permute-start.1
  7.7 0.1 shard_map.76
  7.8 4.6 %collective-permute-done.1.refs_1_.refs_8_ = bf16[2,128,128]{2,1,0:T(8,128)(2,1)S(1)} collective-permute-done((bf16[2,128,128]{2,1,0:T(8,128)(2,1)S(1)}, bf16[2,128,128]{2,1,0:T(8,128)(2,1)S(1)}, u32[]{:S(2)}, u32[]{:S(2)}) %collective-permute-start.1) | collective-permute-done | bytes 65568 | tf_op jit(solution)/shard_map/ppermute | solution.py:607
  12.4 0.5 %shard_map.77 = (f32[3,256,128]{2,1,0:T(8,128)S(1)}, f32[2,128,128]{2,1,0:T(8,128)S(1)}) custom-call(bf16[128,128]{1,0:T(8,128)(2,1)S(1)} %get-tuple-element.44.query_ref.refs_3_, bf16[2,320,128]{2,1,0:T(8,128)(2,1)S(1)} %collective-permute-done.refs_0_.refs_6_, bf16[2,128,128]{2,1,0:T(8,128)(2,1)S(1)} %collective-permute-done.1.refs_1_.refs_8_), custom_call_target="tpu_custom_call" | custom-call | flops 41943040 | bytes 1048576 | tf_op jit(solution)/shard_map/pallas_call | solution.py:591
  12.9 0.8 %collective-permute-done.2.refs_7_ = bf16[2,320,128]{2,1,0:T(8,128)(2,1)S(1)} collective-permute-done((bf16[2,320,128]{2,1,0:T(8,128)(2,1)S(1)}, bf16[2,320,128]{2,1,0:T(8,128)(2,1)S(1)}, u32[]{:S(2)}, u32[]{:S(2)}) %collective-permute-start.2) | collective-permute-done | bytes 163872 | tf_op jit(solution)/shard_map/ppermute | solution.py:607
  13.7 2.5 %shard_map.78 = (bf16[512,128]{1,0:T(8,128)(2,1)S(1)}, bf16[2,320,128]{2,1,0:T(8,128)(2,1)S(1)}, bf16[2,320,128]{2,1,0:T(8,128)(2,1)S(1)}, bf16[2,128,128]{2,1,0...) custom-call(bf16[4,512,128]{2,1,0:T(8,128)(2,1)S(1)} %get-tuple-element.38.held.refs_0_, ...), custom_call_target="tpu_custom_call" | custom-call | flops 293601280 | bytes 1048576 | tf_op jit(solution)/shard_map/pallas_call | solution.py:591
  16.2 1.5 %collective-permute-start.3 = (bf16[2,320,128]{2,1,0:T(8,128)(2,1)S(1)}, bf16[2,320,128]{2,1,0:T(8,128)(2,1)S(1)}, u32[]{:S(2)}, u32[]{:S(2)}) collective-permute-start(bf16[2,320,128]{2,1,0:T(8,128)(2,1)S(1)} %get-tuple-element.56), channel_id=1, source_target_pairs={{0,24},{8,16},{16,8},{24,0},{1,25},{9,17},{17,9},{25,1},{2,26},{10... | collective-permute-start | bytes 491528 | tf_op jit(solution)/shard_map/ppermute | solution.py:607
  17.7 0.3 collective-permute-start.4
  18.0 1.7 %collective-permute-start.5 = (bf16[2,128,128]{2,1,0:T(8,128)(2,1)S(1)}, bf16[2,128,128]{2,1,0:T(8,128)(2,1)S(1)}, u32[]{:S(2)}, u32[]{:S(2)}) collective-permute-start(bf16[2,128,128]{2,1,0:T(8,128)(2,1)S(1)} %get-tuple-element.58), channel_id=1, source_target_pairs={{0,16},{8,24},{16,0},{24,8},{1,17},{9,25},{17,1},{25,9},{2,18},{10... | collective-permute-start | bytes 196616 | tf_op jit(solution)/shard_map/ppermute | solution.py:607
  19.8 1.2 %shard_map.79 = (bf16[512,128]{1,0:T(8,128)(2,1)}, f32[2,512,128]{2,1,0:T(8,128)S(1)}, bf16[512,128]{1,0:T(8,128)(2,1)S(1)}) custom-call(bf16[4,512,128]{2,1,0:T(8,128)(2,1)S(1)} %get-tuple-element.38.held.refs_0_, f32[3,512,128]{2,1,0:T(8,128)S(1)} %get-tuple-element.50.back, f32[512,128]{1,0:T(8,128)S(1)} %get-tuple-element.51.partial_ref, ...), custom_call_target="tpu_custom_call" | custom-call | flops 209715200 | bytes 1048576 | tf_op jit(solution)/shard_map/pallas_call | solution.py:591
  21.0 2.3 %collective-permute-done.5.refs_2_ = bf16[2,128,128]{2,1,0:T(8,128)(2,1)S(1)} collective-permute-done((bf16[2,128,128]{2,1,0:T(8,128)(2,1)S(1)}, bf16[2,128,128]{2,1,0:T(8,128)(2,1)S(1)}, u32[]{:S(2)}, u32[]{:S(2)}) %collective-permute-start.5) | collective-permute-done | bytes 65568 | tf_op jit(solution)/shard_map/ppermute | solution.py:607
  23.3 0.2 collective-permute-done.4.refs_1_
  23.5 0.2 shard_map.80
  23.7 2.6 %collective-permute-start.6 = (bf16[2,3,64,128]{3,2,1,0:T(8,128)(2,1)S(1)}, bf16[2,3,64,128]{3,2,1,0:T(8,128)(2,1)S(1)}, u32[]{:S(2)}, u32[]{:S(2)}) collective-permute-start(bf16[2,3,64,128]{3,2,1,0:T(8,128)(2,1)S(1)} %get-tuple-element.60), channel_id=1, source_target_pairs={{0,4},{1,5},{2,6},{3,7},{4,0},{5,1},{6,2},{7,3},{8,12},{9,13},{10,... | collective-permute-start | bytes 294920 | tf_op jit(solution)/shard_map/ppermute | solution.py:607
  26.3 1.4 %collective-permute-start.7 = (bf16[3,64,128]{2,1,0:T(8,128)(2,1)S(1)}, bf16[3,64,128]{2,1,0:T(8,128)(2,1)S(1)}, u32[]{:S(2)}, u32[]{:S(2)}) collective-permute-start(bf16[3,64,128]{2,1,0:T(8,128)(2,1)S(1)} %get-tuple-element.61), channel_id=1, source_target_pairs={{0,6},{1,7},{2,4},{3,5},{4,2},{5,3},{6,0},{7,1},{8,14},{9,15},{10,... | collective-permute-start | bytes 147464 | tf_op jit(solution)/shard_map/ppermute | solution.py:607
  27.7 0.2 collective-permute-start.8
  27.9 3.1 %collective-permute-start.10 = (bf16[3,64,128]{2,1,0:T(8,128)(2,1)S(1)}, bf16[3,64,128]{2,1,0:T(8,128)(2,1)S(1)}, u32[]{:S(2)}, u32[]{:S(2)}) collective-permute-start(bf16[3,64,128]{2,1,0:T(8,128)(2,1)S(1)} %get-tuple-element.67), channel_id=1, source_target_pairs={{0,3},{1,2},{2,1},{3,0},{4,7},{5,6},{6,5},{7,4},{8,11},{9,10},{10,... | collective-permute-start | bytes 147464 | tf_op jit(solution)/shard_map/ppermute | solution.py:607
  31.0 1.3 %collective-permute-done.7.refs_2_ = bf16[3,64,128]{2,1,0:T(8,128)(2,1)S(1)} collective-permute-done((bf16[3,64,128]{2,1,0:T(8,128)(2,1)S(1)}, bf16[3,64,128]{2,1,0:T(8,128)(2,1)S(1)}, u32[]{:S(2)}, u32[]{:S(2)}) %collective-permute-start.7) | collective-permute-done | bytes 49184 | tf_op jit(solution)/shard_map/ppermute | solution.py:607
  32.3 0.8 %shard_map.81 = (bf16[64,1024]{1,0:T(8,128)(2,1)}, bf16[64,1024]{1,0:T(8,128)(2,1)}, bf16[64,1024]{1,0:T(8,128)(2,1)}) custom-call(bf16[3,64,128]{2,1,0:T(8,128)(2,1)S(1)} %get-tuple-element.59.refs_0_, bf16[2,3,64,128]{3,2,1,0:T(8,128)(2,1)S(1)} %collective-permute-done.6.refs_1_, bf16[3,64,128]{2,1,0:T(8,128)(2,1)S(1)} %collective-permute-done.7.refs_2_, ...), custom_call_target="tpu_custom_call" | custom-call | flops 209715200 | bytes 1048576 | tf_op jit(solution)/shard_map/pallas_call | solution.py:591
  33.1 0.7 %collective-permute-done.9.refs_3_ = bf16[3,64,128]{2,1,0:T(8,128)(2,1)S(1)} collective-permute-done((bf16[3,64,128]{2,1,0:T(8,128)(2,1)S(1)}, bf16[3,64,128]{2,1,0:T(8,128)(2,1)S(1)}, u32[]{:S(2)}, u32[]{:S(2)}) %collective-permute-start.9) | collective-permute-done | bytes 49184 | tf_op jit(solution)/shard_map/ppermute | solution.py:607
  33.8 0.8 %shard_map.82 = (bf16[64,1024]{1,0:T(8,128)(2,1)}, bf16[64,1024]{1,0:T(8,128)(2,1)}, bf16[64,1024]{1,0:T(8,128)(2,1)}) custom-call(bf16[64,1024]{1,0:T(8,128)(2,1)} %get-tuple-element.63.refs_0_, bf16[64,1024]{1,0:T(8,128)(2,1)} %get-tuple-element.64.refs_1_, ...), custom_call_target="tpu_custom_call", output_to_operand_aliasing={{0}: (0, {}), {1}: (1, {}), {2}: (2, {})} | custom-call | bytes 1048576 | tf_op jit(solution)/shard_map/pallas_call | solution.py:591
  (11 shorter events, 0.0 us)
Async XLA Ops:
  3.1 9.3 %collective-permute-start = (bf16[2,320,128]{2,1,0:T(8,128)(2,1)S(1)}, bf16[2,320,128]{2,1,0:T(8,128)(2,1)S(1)}, u32[]{:S(2)}, u32[]{:S(2)}) collective-permute-start(bf16[2,320,128]{2,1,0:T(8,128)(2,1)S(1)} %get-tuple-element.45), channel_id=1, source_target_pairs={{0,24},{8,16},{16,8},{24,0},{1,25},{9,17},{17,9},{25,1},{2,26},{10... | collective-permute-start | bytes 491528 | tf_op jit(solution)/shard_map/ppermute | solution.py:607
  7.1 6.6 %collective-permute-start.2 = (bf16[2,320,128]{2,1,0:T(8,128)(2,1)S(1)}, bf16[2,320,128]{2,1,0:T(8,128)(2,1)S(1)}, u32[]{:S(2)}, u32[]{:S(2)}) collective-permute-start(bf16[2,320,128]{2,1,0:T(8,128)(2,1)S(1)} %get-tuple-element.49), channel_id=1, source_target_pairs={{0,8},{8,0},{16,24},{24,16},{1,9},{9,1},{17,25},{25,17},{2,10},{10... | collective-permute-start | bytes 491528 | tf_op jit(solution)/shard_map/ppermute | solution.py:607
  7.6 4.8 %collective-permute-start.1 = (bf16[2,128,128]{2,1,0:T(8,128)(2,1)S(1)}, bf16[2,128,128]{2,1,0:T(8,128)(2,1)S(1)}, u32[]{:S(2)}, u32[]{:S(2)}) collective-permute-start(bf16[2,128,128]{2,1,0:T(8,128)(2,1)S(1)} %get-tuple-element.46), channel_id=1, source_target_pairs={{0,16},{8,24},{16,0},{24,8},{1,17},{9,25},{17,1},{25,9},{2,18},{10... | collective-permute-start | bytes 196616 | tf_op jit(solution)/shard_map/ppermute | solution.py:607
  16.2 7.1 %collective-permute-start.3 = (bf16[2,320,128]{2,1,0:T(8,128)(2,1)S(1)}, bf16[2,320,128]{2,1,0:T(8,128)(2,1)S(1)}, u32[]{:S(2)}, u32[]{:S(2)}) collective-permute-start(bf16[2,320,128]{2,1,0:T(8,128)(2,1)S(1)} %get-tuple-element.56), channel_id=1, source_target_pairs={{0,24},{8,16},{16,8},{24,0},{1,25},{9,17},{17,9},{25,1},{2,26},{10... | collective-permute-start | bytes 491528 | tf_op jit(solution)/shard_map/ppermute | solution.py:607
  17.7 5.8 %collective-permute-start.4 = (bf16[2,320,128]{2,1,0:T(8,128)(2,1)S(1)}, bf16[2,320,128]{2,1,0:T(8,128)(2,1)S(1)}, u32[]{:S(2)}, u32[]{:S(2)}) collective-permute-start(bf16[2,320,128]{2,1,0:T(8,128)(2,1)S(1)} %get-tuple-element.57), channel_id=1, source_target_pairs={{0,8},{8,0},{16,24},{24,16},{1,9},{9,1},{17,25},{25,17},{2,10},{10... | collective-permute-start | bytes 491528 | tf_op jit(solution)/shard_map/ppermute | solution.py:607
  18.0 5.2 %collective-permute-start.5 = (bf16[2,128,128]{2,1,0:T(8,128)(2,1)S(1)}, bf16[2,128,128]{2,1,0:T(8,128)(2,1)S(1)}, u32[]{:S(2)}, u32[]{:S(2)}) collective-permute-start(bf16[2,128,128]{2,1,0:T(8,128)(2,1)S(1)} %get-tuple-element.58), channel_id=1, source_target_pairs={{0,16},{8,24},{16,0},{24,8},{1,17},{9,25},{17,1},{25,9},{2,18},{10... | collective-permute-start | bytes 196616 | tf_op jit(solution)/shard_map/ppermute | solution.py:607
  23.7 7.2 %collective-permute-start.6 = (bf16[2,3,64,128]{3,2,1,0:T(8,128)(2,1)S(1)}, bf16[2,3,64,128]{3,2,1,0:T(8,128)(2,1)S(1)}, u32[]{:S(2)}, u32[]{:S(2)}) collective-permute-start(bf16[2,3,64,128]{3,2,1,0:T(8,128)(2,1)S(1)} %get-tuple-element.60), channel_id=1, source_target_pairs={{0,4},{1,5},{2,6},{3,7},{4,0},{5,1},{6,2},{7,3},{8,12},{9,13},{10,... | collective-permute-start | bytes 294920 | tf_op jit(solution)/shard_map/ppermute | solution.py:607
  26.3 6.0 %collective-permute-start.7 = (bf16[3,64,128]{2,1,0:T(8,128)(2,1)S(1)}, bf16[3,64,128]{2,1,0:T(8,128)(2,1)S(1)}, u32[]{:S(2)}, u32[]{:S(2)}) collective-permute-start(bf16[3,64,128]{2,1,0:T(8,128)(2,1)S(1)} %get-tuple-element.61), channel_id=1, source_target_pairs={{0,6},{1,7},{2,4},{3,5},{4,2},{5,3},{6,0},{7,1},{8,14},{9,15},{10,... | collective-permute-start | bytes 147464 | tf_op jit(solution)/shard_map/ppermute | solution.py:607
  27.7 4.6 %collective-permute-start.8 = (bf16[3,64,128]{2,1,0:T(8,128)(2,1)S(1)}, bf16[3,64,128]{2,1,0:T(8,128)(2,1)S(1)}, u32[]{:S(2)}, u32[]{:S(2)}) collective-permute-start(bf16[3,64,128]{2,1,0:T(8,128)(2,1)S(1)} %get-tuple-element.62), channel_id=1, source_target_pairs={{0,2},{1,3},{2,0},{3,1},{4,6},{5,7},{6,4},{7,5},{8,10},{9,11},{10,... | collective-permute-start | bytes 147464 | tf_op jit(solution)/shard_map/ppermute | solution.py:607
  27.9 5.9 %collective-permute-start.9 = (bf16[3,64,128]{2,1,0:T(8,128)(2,1)S(1)}, bf16[3,64,128]{2,1,0:T(8,128)(2,1)S(1)}, u32[]{:S(2)}, u32[]{:S(2)}) collective-permute-start(bf16[3,64,128]{2,1,0:T(8,128)(2,1)S(1)} %get-tuple-element.66), channel_id=1, source_target_pairs={{0,7},{1,6},{2,5},{3,4},{4,3},{5,2},{6,1},{7,0},{8,15},{9,14},{10,... | collective-permute-start | bytes 147464 | tf_op jit(solution)/shard_map/ppermute | solution.py:607
  27.9 5.9 %collective-permute-start.10 = (bf16[3,64,128]{2,1,0:T(8,128)(2,1)S(1)}, bf16[3,64,128]{2,1,0:T(8,128)(2,1)S(1)}, u32[]{:S(2)}, u32[]{:S(2)}) collective-permute-start(bf16[3,64,128]{2,1,0:T(8,128)(2,1)S(1)} %get-tuple-element.67), channel_id=1, source_target_pairs={{0,3},{1,2},{2,1},{3,0},{4,7},{5,6},{6,5},{7,4},{8,11},{9,10},{10,... | collective-permute-start | bytes 147464 | tf_op jit(solution)/shard_map/ppermute | solution.py:607
  31.0 2.8 %collective-permute-start.11 = (bf16[3,64,128]{2,1,0:T(8,128)(2,1)S(1)}, bf16[3,64,128]{2,1,0:T(8,128)(2,1)S(1)}, u32[]{:S(2)}, u32[]{:S(2)}) collective-permute-start(bf16[3,64,128]{2,1,0:T(8,128)(2,1)S(1)} %get-tuple-element.68), channel_id=1, source_target_pairs={{0,1},{1,0},{2,3},{3,2},{4,5},{5,4},{6,7},{7,6},{8,9},{9,8},{10,11... | collective-permute-start | bytes 147464 | tf_op jit(solution)/shard_map/ppermute | solution.py:607
  32.3 1.5 %collective-permute-start.12 = (bf16[3,64,128]{2,1,0:T(8,128)(2,1)S(1)}, bf16[3,64,128]{2,1,0:T(8,128)(2,1)S(1)}, u32[]{:S(2)}, u32[]{:S(2)}) collective-permute-start(bf16[3,64,128]{2,1,0:T(8,128)(2,1)S(1)} %slice_bitcast_fusion), channel_id=1, source_target_pairs={{0,1},{1,0},{2,3},{3,2},{4,5},{5,4},{6,7},{7,6},{8,9},{9,8},{10,11... | collective-permute-start | bytes 147464 | tf_op jit(solution)/shard_map/ppermute | solution.py:607
